TPU v7x, 32 devices: a whole 2x2x4 slice. The times are simulated.
32 devices in a mesh: dp: 4 (over x, core), expert: 8 (over z, y).
Axes of the slice: x: 2, y: 2, z: 4, core: 2. Of those that a mesh axis runs over, the one named last changes fastest.
Arguments:
- inputs: bfloat16 [32, 1024, 768], P(('dp', 'expert')), may hold values from -9 to 9
- cotangent: bfloat16 [32, 1024, 768], P(('dp', 'expert')), may hold values from -6 to 6
- attn_gain: bfloat16 [768], P(('dp', 'expert')), may hold values from 0.25 to 1.75
- qkv_weight: bfloat16 [768, 2304], P(('dp', 'expert')), may hold values from -0.21875 to 0.21875
- out_weight: bfloat16 [768, 768], P(('dp', 'expert')), may hold values from -0.875 to 0.875
- ffn_gain: bfloat16 [768], P(('dp', 'expert')), may hold values from 0.25 to 1.75
- router_weight: bfloat16 [768, 8], P(('dp', 'expert')), may hold values from -0.15625 to 0.15625
- rel_bias: float32 [32, 12], replicated, may hold values from -4 to 4
- expert_in: bfloat16 [8, 768, 3072], P('expert'), may hold values from -0.21875 to 0.21875
- expert_out: bfloat16 [8, 3072, 768], P('expert'), may hold values from -1.25 to 1.25
- routes: int32 [32, 1024], P(('dp', 'expert')), may hold values from 0 to 7
- positions: int32 [32, 1024], P(('dp', 'expert')), may hold values from 0 to 160, as said below
- dropped: int32 [32, 1024], P(('dp', 'expert')), may hold values from 0 to 1, as said below
- segment_ids: int32 [32, 1024], P(('dp', 'expert')), may hold values from 0 to 7, never falling along the last dimension, each value on 1 to 512 neighbouring positions
- valid_mask: int32 [32, 1024], P(('dp', 'expert')), may hold values from 0 to 1, as said below
- buckets: int32 [2047], replicated, may hold values from 0 to 31
Outputs:
- output: bfloat16 [32, 1024, 768], P(('dp', 'expert'))
- input_grad: float32 [32, 1024, 768], P(('dp', 'expert'))
- grad_attn_gain: float32 [768], P(('dp', 'expert'))
- grad_qkv_weight: float32 [768, 2304], P(('dp', 'expert'))
- grad_out_weight: float32 [768, 768], P(('dp', 'expert'))
- grad_ffn_gain: float32 [768], P(('dp', 'expert'))
- grad_router_weight: float32 [768, 8], P(('dp', 'expert'))
- grad_rel_bias: float32 [32, 12], replicated
- grad_expert_in: float32 [8, 768, 3072], P('expert', None, 'dp')
- grad_expert_out: float32 [8, 3072, 768], P('expert', 'dp')
- stats: float32 [3], replicated
Inputs may be any that keep to these rules, and one draw needn't show every extreme that they name: `positions`: A kept token's position is its rank among the tokens of its aligned group of 1024 tokens that name the same expert, so no two kept tokens of a group share expert and position; a token beyond the capacity has position 160. dropped is 1 exactly where positions is 160. `valid_mask`: the first token of every sequence is real.
All inputs are finite; a program needn't handle non-finite values.
Results may differ from a plain program's by a relative error of at most 0.015.
Values may be sent and summed in bfloat16 or wider, within the bound.
No kernel may reach another device: no remote copies, remote signals or barrier semaphores. Data moves between devices by JAX's collectives and lax.ppermute only.
A program may use at most 320 MiB of HBM per device.

v0:
```python
import jax
import jax.numpy as jnp
from jax import lax
from jax.sharding import PartitionSpec as P

EPSILON = 1e-06
MASKED = -1e30
HIGHEST = lax.Precision.HIGHEST


def smooth_unit(values):
    return jax.nn.gelu(values, approximate=True)


def smooth_slope(values):
    unused_value, pullback = jax.vjp(smooth_unit, values)
    return pullback(jnp.ones_like(values))[0]


def norm_factor(values):
    return lax.rsqrt(jnp.mean(values * values, axis=-1, keepdims=True) + EPSILON)


def norm_backward(grad_rows, values, factor, norm_gain):
    normed = values * factor
    weighted = grad_rows * norm_gain
    gain_grad = jnp.sum(grad_rows * normed, axis=0)
    values_grad = factor * (weighted - normed * jnp.mean(weighted * normed, axis=-1, keepdims=True))
    return (values_grad, gain_grad)


def bucket_table(buckets, rel_bias):
    indices = jnp.arange(rel_bias.shape[0], dtype=jnp.int32)
    return (buckets[:, None] == indices[None, :]).astype(jnp.float32)


def scatter_rows(rows, slot_index, experts, capacity):
    empty = jnp.zeros((experts * capacity, rows.shape[1]), rows.dtype)
    return empty.at[slot_index].set(rows, mode="drop").reshape(experts, 1, capacity, rows.shape[1])


def band_start(first_row, block_rows, seq_length):
    return seq_length - first_row - block_rows


def toeplitz_block(head_bias, first_row, block_rows, seq_length):
    width = block_rows + seq_length - 1
    head_count = head_bias.shape[0]
    band = lax.dynamic_slice_in_dim(
        head_bias, band_start(first_row, block_rows, seq_length), width, 1
    )
    band = jnp.pad(band, ((0, 0), (0, 1)))
    tiled = jnp.tile(band, (1, block_rows))[:, : block_rows * width].reshape(
        head_count, block_rows, width
    )
    return tiled[:, :, block_rows - 1 : block_rows - 1 + seq_length]


def diagonal_sums(grad_scores):
    head_count, block_rows, seq_length = grad_scores.shape
    width = block_rows + seq_length - 1
    placed = jnp.pad(grad_scores, ((0, 0), (0, 0), (block_rows - 1, 0))).reshape(
        head_count, block_rows * width
    )
    placed = jnp.pad(placed, ((0, 0), (0, block_rows))).reshape(head_count, block_rows, width + 1)
    return jnp.sum(placed, axis=1)[:, :width]


def block_scores(query_block, keys_all, first_row, segments, validity, head_bias, score_scale):
    block_rows = query_block.shape[0]
    seq_length = keys_all.shape[0]
    rows_at = first_row + jnp.arange(block_rows, dtype=jnp.int32)
    cols_at = jnp.arange(seq_length, dtype=jnp.int32)
    bias_block = toeplitz_block(head_bias, first_row, block_rows, seq_length)
    raw_scores = (
        jnp.einsum("qhd,khd->hqk", query_block, keys_all, preferred_element_type=jnp.float32)
        * score_scale
        + bias_block
    )
    row_segments = lax.dynamic_slice_in_dim(segments, first_row, block_rows)
    allowed = (row_segments[:, None] == segments[None, :]) & (validity[None, :] == 1) | (
        rows_at[:, None] == cols_at[None, :]
    )
    return jnp.where(allowed[None], raw_scores, MASKED)


def split_heads(packed, model_width, head_count):
    seq_length = packed.shape[0]
    head_dim = model_width // head_count
    queries = packed[:, :model_width].reshape(seq_length, head_count, head_dim)
    keys_all = packed[:, model_width : 2 * model_width].reshape(seq_length, head_count, head_dim)
    values_all = packed[:, 2 * model_width :].reshape(seq_length, head_count, head_dim)
    return (queries, keys_all, values_all)


def attend_forward(layer_seq, segments, validity, norm_gain, w_qkv, w_out, head_bias, block_rows):
    seq_length, model_width = layer_seq.shape
    head_count = head_bias.shape[0]
    score_scale = (model_width // head_count) ** (-0.5)
    factor = norm_factor(layer_seq)
    normed = (layer_seq * factor * norm_gain).astype(jnp.bfloat16)
    packed = jnp.dot(normed, w_qkv, preferred_element_type=jnp.float32).astype(jnp.bfloat16)
    queries, keys_all, values_all = split_heads(packed, model_width, head_count)
    starts = jnp.arange(seq_length // block_rows, dtype=jnp.int32) * block_rows

    def one_block(first_row):
        query_block = lax.dynamic_slice_in_dim(queries, first_row, block_rows)
        scores = block_scores(
            query_block, keys_all, first_row, segments, validity, head_bias, score_scale
        )
        row_peak = jnp.max(scores, axis=-1, keepdims=True)
        log_total = row_peak + jnp.log(jnp.sum(jnp.exp(scores - row_peak), axis=-1, keepdims=True))
        weights = jnp.exp(scores - log_total).astype(jnp.bfloat16)
        mixed = jnp.einsum("hqk,khd->qhd", weights, values_all, preferred_element_type=jnp.float32)
        return (mixed.astype(jnp.bfloat16), log_total[..., 0])

    mixed, log_totals = lax.map(one_block, starts)
    mixed = mixed.reshape(seq_length, model_width)
    attn_out = jnp.dot(mixed, w_out, preferred_element_type=jnp.float32)
    return (attn_out, (normed, packed, mixed, log_totals, factor))


def attend_backward(
    grad_attn,
    layer_seq,
    segments,
    validity,
    norm_gain,
    w_qkv,
    w_out,
    head_bias,
    offset_table,
    saved_state,
    block_rows,
):
    normed, packed, mixed, log_totals, factor = saved_state
    seq_length, model_width = layer_seq.shape
    head_count = head_bias.shape[0]
    head_dim = model_width // head_count
    score_scale = head_dim ** (-0.5)
    band_width = block_rows + seq_length - 1
    grad_attn_low = grad_attn.astype(jnp.bfloat16)
    grad_out_w = jnp.einsum("td,te->de", mixed, grad_attn_low, preferred_element_type=jnp.float32)
    grad_mixed = jnp.einsum("te,de->td", grad_attn_low, w_out, preferred_element_type=jnp.float32)
    grad_mixed = grad_mixed.astype(jnp.bfloat16).reshape(seq_length, head_count, head_dim)
    queries, keys_all, values_all = split_heads(packed, model_width, head_count)
    starts = jnp.arange(seq_length // block_rows, dtype=jnp.int32) * block_rows

    def one_block(running, element):
        grad_keys, grad_values, grad_offsets = running
        first_row, log_total = element
        query_block = lax.dynamic_slice_in_dim(queries, first_row, block_rows)
        grad_block = lax.dynamic_slice_in_dim(grad_mixed, first_row, block_rows)
        scores = block_scores(
            query_block, keys_all, first_row, segments, validity, head_bias, score_scale
        )
        weights = jnp.exp(scores - log_total[..., None])
        grad_weights = jnp.einsum(
            "qhd,khd->hqk", grad_block, values_all, preferred_element_type=jnp.float32
        )
        row_delta = jnp.sum(weights * grad_weights, axis=-1, keepdims=True)
        grad_scores = (weights * (grad_weights - row_delta)).astype(jnp.bfloat16)
        grad_query = (
            jnp.einsum("hqk,khd->qhd", grad_scores, keys_all, preferred_element_type=jnp.float32)
            * score_scale
        )
        grad_keys = (
            grad_keys
            + jnp.einsum(
                "hqk,qhd->khd", grad_scores, query_block, preferred_element_type=jnp.float32
            )
            * score_scale
        )
        grad_values = grad_values + jnp.einsum(
            "hqk,qhd->khd",
            weights.astype(jnp.bfloat16),
            grad_block,
            preferred_element_type=jnp.float32,
        )
        along = diagonal_sums(grad_scores.astype(jnp.float32))
        offset_at = band_start(first_row, block_rows, seq_length)
        current = lax.dynamic_slice_in_dim(grad_offsets, offset_at, band_width, 1)
        grad_offsets = lax.dynamic_update_slice_in_dim(grad_offsets, current + along, offset_at, 1)
        return ((grad_keys, grad_values, grad_offsets), grad_query)

    start_state = (
        jnp.zeros((seq_length, head_count, head_dim), jnp.float32),
        jnp.zeros((seq_length, head_count, head_dim), jnp.float32),
        jnp.zeros((head_count, 2 * seq_length - 1), jnp.float32),
    )
    (grad_keys, grad_values, grad_offsets), grad_queries = lax.scan(
        one_block, start_state, (starts, log_totals)
    )
    grad_buckets = jnp.dot(
        grad_offsets, offset_table, precision=HIGHEST, preferred_element_type=jnp.float32
    ).T
    grad_packed = jnp.concatenate(
        [
            grad_queries.reshape(seq_length, model_width),
            grad_keys.reshape(seq_length, model_width),
            grad_values.reshape(seq_length, model_width),
        ],
        axis=1,
    ).astype(jnp.bfloat16)
    grad_qkv_w = jnp.einsum("td,te->de", normed, grad_packed, preferred_element_type=jnp.float32)
    grad_normed = jnp.einsum("te,de->td", grad_packed, w_qkv, preferred_element_type=jnp.float32)
    grad_layer, grad_gain = norm_backward(grad_normed, layer_seq, factor, norm_gain)
    return (grad_layer, (grad_qkv_w, grad_out_w, grad_gain, grad_buckets))


def body(
    inputs,
    cotangent,
    attn_gain,
    qkv_weight,
    out_weight,
    ffn_gain,
    router_weight,
    rel_bias,
    expert_in,
    expert_out,
    routes,
    positions,
    dropped,
    segment_ids,
    valid_mask,
    buckets,
):
    seq_count, seq_length, model_width = inputs.shape
    block_rows = min(512, seq_length)
    tokens = seq_count * seq_length
    bucket_count = rel_bias.shape[0]
    dense_full = (
        lax.all_gather(attn_gain, ("dp", "expert"), axis=0, tiled=True),
        lax.all_gather(qkv_weight, ("dp", "expert"), axis=0, tiled=True),
        lax.all_gather(out_weight, ("dp", "expert"), axis=0, tiled=True),
        lax.all_gather(ffn_gain, ("dp", "expert"), axis=0, tiled=True),
        lax.all_gather(router_weight, ("dp", "expert"), axis=0, tiled=True),
    )
    gain_one = dense_full[0].astype(jnp.float32)
    gain_two = dense_full[3].astype(jnp.float32)
    one_hot_buckets = bucket_table(buckets, rel_bias)
    head_bias = jnp.dot(
        one_hot_buckets, rel_bias, precision=HIGHEST, preferred_element_type=jnp.float32
    ).T
    layer_in = inputs.astype(jnp.float32)

    def forward_one(element):
        return attend_forward(
            element[0],
            element[1],
            element[2],
            gain_one,
            dense_full[1],
            dense_full[2],
            head_bias,
            block_rows,
        )

    attn_out, saved_state = lax.map(forward_one, (layer_in, segment_ids, valid_mask))
    mid_rows = (layer_in + attn_out).reshape(tokens, model_width)
    experts = dense_full[4].shape[1]
    capacity = 5 * tokens // (4 * experts)
    route_ids = routes.reshape(tokens)
    slot_index = jnp.where(
        dropped.reshape(tokens) == 1,
        experts * capacity,
        route_ids * capacity + positions.reshape(tokens),
    )
    mid_factor = norm_factor(mid_rows)
    ffn_normed = (mid_rows * mid_factor * gain_two).astype(jnp.bfloat16)
    logits = jnp.dot(ffn_normed, dense_full[4], preferred_element_type=jnp.float32)
    router_probs = jax.nn.softmax(logits, axis=-1)
    chosen = (route_ids[:, None] == jnp.arange(experts, dtype=jnp.int32)[None, :]).astype(
        jnp.float32
    )
    gate_value = jnp.sum(router_probs * chosen, axis=-1)
    send_rows = scatter_rows(ffn_normed, slot_index, experts, capacity)
    received = lax.all_to_all(send_rows, "expert", split_axis=0, concat_axis=1, tiled=True)
    pre_act = jnp.einsum("escd,edf->escf", received, expert_in, preferred_element_type=jnp.float32)
    hidden = smooth_unit(pre_act).astype(jnp.bfloat16)
    rows_out = jnp.einsum(
        "escf,efd->escd", hidden, expert_out, preferred_element_type=jnp.float32
    ).astype(jnp.bfloat16)
    returned = lax.all_to_all(rows_out, "expert", split_axis=1, concat_axis=0, tiled=True)
    picked = jnp.take(
        returned.reshape(experts * capacity, model_width),
        slot_index,
        axis=0,
        mode="fill",
        fill_value=0,
    ).astype(jnp.float32)
    final_rows = mid_rows + gate_value[:, None] * picked
    output = final_rows.astype(jnp.bfloat16).reshape(inputs.shape)
    live_rows = valid_mask.reshape(tokens).astype(jnp.float32)
    flat_in = layer_in.reshape(tokens, model_width)
    square_sums = jnp.stack(
        [
            jnp.sum(live_rows[:, None] * flat_in * flat_in),
            jnp.sum(live_rows[:, None] * mid_rows * mid_rows),
            jnp.sum(live_rows[:, None] * final_rows * final_rows),
        ]
    )
    live_count = jnp.sum(live_rows)
    dense_back = (
        lax.all_gather(attn_gain, ("dp", "expert"), axis=0, tiled=True),
        lax.all_gather(qkv_weight, ("dp", "expert"), axis=0, tiled=True),
        lax.all_gather(out_weight, ("dp", "expert"), axis=0, tiled=True),
        lax.all_gather(ffn_gain, ("dp", "expert"), axis=0, tiled=True),
        lax.all_gather(router_weight, ("dp", "expert"), axis=0, tiled=True),
    )
    back_gain_one = dense_back[0].astype(jnp.float32)
    back_gain_two = dense_back[3].astype(jnp.float32)
    grad_final = cotangent.astype(jnp.float32).reshape(tokens, model_width)
    grad_gate = jnp.sum(grad_final * picked, axis=-1)
    grad_rows = (gate_value[:, None] * grad_final).astype(jnp.bfloat16)
    grad_send = scatter_rows(grad_rows, slot_index, experts, capacity)
    grad_rows_out = lax.all_to_all(grad_send, "expert", split_axis=0, concat_axis=1, tiled=True)
    grad_hidden = jnp.einsum(
        "escd,efd->escf", grad_rows_out, expert_out, preferred_element_type=jnp.float32
    )
    grad_pre = (grad_hidden * smooth_slope(pre_act)).astype(jnp.bfloat16)
    grad_rows_in = jnp.einsum(
        "escf,edf->escd", grad_pre, expert_in, preferred_element_type=jnp.float32
    ).astype(jnp.bfloat16)
    grad_back = lax.all_to_all(grad_rows_in, "expert", split_axis=1, concat_axis=0, tiled=True)
    grad_expert_rows = jnp.take(
        grad_back.reshape(experts * capacity, model_width),
        slot_index,
        axis=0,
        mode="fill",
        fill_value=0,
    ).astype(jnp.float32)
    part_in = jnp.einsum("escd,escf->edf", received, grad_pre, preferred_element_type=jnp.float32)
    part_out = jnp.einsum(
        "escf,escd->efd", hidden, grad_rows_out, preferred_element_type=jnp.float32
    )
    grad_expert_in, grad_expert_out = (
        lax.psum_scatter(
            part_in.astype(jnp.bfloat16), "dp", scatter_dimension=2, tiled=True
        ).astype(jnp.float32),
        lax.psum_scatter(
            part_out.astype(jnp.bfloat16), "dp", scatter_dimension=1, tiled=True
        ).astype(jnp.float32),
    )
    grad_logits = (router_probs * (chosen - gate_value[:, None]) * grad_gate[:, None]).astype(
        jnp.bfloat16
    )
    grad_router = jnp.einsum(
        "td,te->de", ffn_normed, grad_logits, preferred_element_type=jnp.float32
    )
    grad_ffn_normed = (
        jnp.einsum("te,de->td", grad_logits, dense_back[4], preferred_element_type=jnp.float32)
        + grad_expert_rows
    )
    grad_mid_norm, grad_gain_two = norm_backward(
        grad_ffn_normed, mid_rows, mid_factor, back_gain_two
    )
    grad_mid = grad_final + grad_mid_norm
    grad_mid_seq = grad_mid.reshape(seq_count, seq_length, model_width)

    def backward_one(running, element):
        grad_layer, grads_local = attend_backward(
            element[0],
            element[1],
            element[2],
            element[3],
            back_gain_one,
            dense_back[1],
            dense_back[2],
            head_bias,
            one_hot_buckets,
            element[4],
            block_rows,
        )
        return (jax.tree.map(jnp.add, running, grads_local), grad_layer)

    zero_grads = (
        jnp.zeros(dense_back[1].shape, jnp.float32),
        jnp.zeros(dense_back[2].shape, jnp.float32),
        jnp.zeros((model_width,), jnp.float32),
        jnp.zeros((bucket_count, head_bias.shape[0]), jnp.float32),
    )
    attn_totals, grad_attn_in = lax.scan(
        backward_one, zero_grads, (grad_mid_seq, layer_in, segment_ids, valid_mask, saved_state)
    )
    input_grad = grad_mid_seq + grad_attn_in
    grad_rel_local = attn_totals[3]
    grad_shards = (
        lax.psum_scatter(attn_totals[2], ("dp", "expert"), scatter_dimension=0, tiled=True),
        lax.psum_scatter(attn_totals[0], ("dp", "expert"), scatter_dimension=0, tiled=True),
        lax.psum_scatter(attn_totals[1], ("dp", "expert"), scatter_dimension=0, tiled=True),
        lax.psum_scatter(grad_gain_two, ("dp", "expert"), scatter_dimension=0, tiled=True),
        lax.psum_scatter(grad_router, ("dp", "expert"), scatter_dimension=0, tiled=True),
    )
    totals, count_all, grad_rel = lax.psum(
        (square_sums, live_count, grad_rel_local), ("dp", "expert")
    )
    stats = jnp.sqrt(totals / (count_all * model_width))
    return (
        output,
        input_grad,
        grad_shards[0],
        grad_shards[1],
        grad_shards[2],
        grad_shards[3],
        grad_shards[4],
        grad_rel,
        grad_expert_in,
        grad_expert_out,
        stats,
    )


def solution(mesh):
    in_specs = (
        P(("dp", "expert"), None, None),
        P(("dp", "expert"), None, None),
        P(("dp", "expert")),
        P(("dp", "expert"), None),
        P(("dp", "expert"), None),
        P(("dp", "expert")),
        P(("dp", "expert"), None),
        P(),
        P("expert", None, None),
        P("expert", None, None),
        P(("dp", "expert"), None),
        P(("dp", "expert"), None),
        P(("dp", "expert"), None),
        P(("dp", "expert"), None),
        P(("dp", "expert"), None),
        P(),
    )
    out_specs = (
        P(("dp", "expert"), None, None),
        P(("dp", "expert"), None, None),
        P(("dp", "expert")),
        P(("dp", "expert"), None),
        P(("dp", "expert"), None),
        P(("dp", "expert")),
        P(("dp", "expert"), None),
        P(),
        P("expert", None, "dp"),
        P("expert", "dp", None),
        P(),
    )
    return jax.shard_map(body, mesh=mesh, in_specs=in_specs, out_specs=out_specs, check_vma=False)
```

profile of v0, /device:TPU:0, one launch (start us, length us, event | category | flops | bytes accessed | tf_op | source)
XLA Modules:
  0.0 2090.9 jit_solution(4029320301244251418)
XLA Ops:
  10.9 42.0 %all-reduce.10 = (bf16[768]{0:T(1024)(128)(2,1)S(1)}, bf16[768]{0:T(1024)(128)(2,1)S(1)}) all-reduce(bf16[768]{0:T(1024)(128)(2,1)S(1)} %dynamic-update-slice, bf16[768]{0:T(1024)(128)(2,1)S(1)} %dynamic-update-slice.1), channel_id=1, replica_groups=mesh['dp'=4,'expert'=8] {'dp','expert'}, use_global_device_ids=true, to_apply=%add.4 | all-reduce | flops 1536 | bytes 6144
  87.4 500.8 %while.64 = (s32[]{:T(128)}, bf16[2,512,12,64]{1,3,2,0:T(8,128)(2,1)}, f32[2,12,512]{2,1,0:T(8,128)}, s32[2]{0:T(128)}, s32[1024]{0:T(1024)S(1)}, /*index=5*/s32...) while((s32[]{:T(128)}, ...), condition=%wide.region_4.5_spmd, body=%wide.region_1.4_spmd.sunk | while | flops 1663430144 | bytes 497004672 | solution.py:117
  138.2 46.1 %copy.92 = f32[2,8,512,1536]{3,1,2,0:T(8,128)} copy(f32[2,8,512,1536]{3,2,1,0:T(8,128)} %bitcast.232) | data formatting | bytes 100663296 | tf_op jit(solution)/shard_map/while/body/eval_jaxpr/while
  184.4 33.4 %slice.101 = f32[12,785920]{1,0:T(8,128)} slice(f32[12,786432]{1,0:T(8,128)} %bitcast.235), slice={[0:12], [0:785920]} | slice | bytes 75448320 | tf_op jit(solution)/shard_map/while/body/eval_jaxpr/while/body/eval_jaxpr/slice | solution.py:53
  217.8 77.2 %reshape.602 = f32[12,512,1535]{2,1,0:T(8,128)} reshape(f32[12,785920]{1,0:T(8,128)} %slice.101) | data formatting | bytes 75448320 | tf_op jit(solution)/shard_map/while/body/eval_jaxpr/while/body/eval_jaxpr/reshape | solution.py:53
  393.2 46.1 %copy.92 = f32[2,8,512,1536]{3,1,2,0:T(8,128)} copy(f32[2,8,512,1536]{3,2,1,0:T(8,128)} %bitcast.232) | data formatting | bytes 100663296 | tf_op jit(solution)/shard_map/while/body/eval_jaxpr/while
  439.3 33.4 %slice.101 = f32[12,785920]{1,0:T(8,128)} slice(f32[12,786432]{1,0:T(8,128)} %bitcast.235), slice={[0:12], [0:785920]} | slice | bytes 75448320 | tf_op jit(solution)/shard_map/while/body/eval_jaxpr/while/body/eval_jaxpr/slice | solution.py:53
  472.8 59.0 %reshape.602 = f32[12,512,1535]{2,1,0:T(8,128)} reshape(f32[12,785920]{1,0:T(8,128)} %slice.101) | data formatting | bytes 75448320 | tf_op jit(solution)/shard_map/while/body/eval_jaxpr/while/body/eval_jaxpr/reshape | solution.py:53
  609.7 50.8 %all_to_all.16 = bf16[8,1,160,768]{3,2,1,0:T(8,128)(2,1)S(1)} all-to-all(bf16[8,1,160,768]{3,2,1,0:T(8,128)(2,1)} %bitcast.243), channel_id=1, replica_groups=mesh['dp'=4,'expert'=8] {'expert'}, dimensions={0} | all-to-all | bytes 3932160 | tf_op jit(solution)/shard_map/all_to_all | solution.py:279
  690.8 99.9 %all-gather = bf16[32,24,8]{1,2,0:T(8,128)(2,1)S(1)} all-gather(bf16[1,24,8]{1,2,0:T(8,128)(2,1)S(1)} %bitcast.265), channel_id=1, replica_groups=mesh['dp'=4,'expert'=8] {'dp','expert'}, dimensions={0}, use_global_device_ids=true | all-gather | bytes 12672 | tf_op jit(solution)/shard_map/all_gather | solution.py:238
  819.0 46.8 %all_to_all.17 = bf16[8,1,160,768]{3,2,1,0:T(8,128)(2,1)S(1)} all-to-all(bf16[8,1,160,768]{3,2,1,0:T(8,128)(2,1)} %bitcast.242), channel_id=1, replica_groups=mesh['dp'=4,'expert'=8] {'expert'}, dimensions={0} | all-to-all | bytes 3932160 | tf_op jit(solution)/shard_map/all_to_all | solution.py:318
  929.2 42.9 %all-to-all-done.3 = bf16[1,8,160,768]{3,2,0,1:T(8,128)(2,1)} async-done(((bf16[1,8,160,768]{3,2,0,1:T(8,128)(2,1)}), bf16[1,8,160,768]{3,2,0,1:T(8,128)(2,1)}, u32[]{:S(2)}, u32[]{:S(2)}) %all-to-all-start.3) | async-done | bytes 1966112 | tf_op jit(solution)/shard_map/all_to_all | solution.py:326
  999.6 948.9 %while.65 = (s32[]{:T(128)}, f32[1024,12,64]{0,2,1:T(8,128)}, f32[1024,12,64]{0,2,1:T(8,128)}, f32[12,2047]{1,0:T(8,128)}, bf16[2,512,12,64]{1,3,2,0:T(8,128)(2,...) while((s32[]{:T(128)}, f32[1024,12,64]{0,2,1:T(8,128)}, ...), condition=%wide.region_16.18_spmd.clone, body=%wide.region_13.17_spmd.clone.sunk | while | flops 4114738688 | bytes 905539328 | solution.py:191
  1065.1 46.2 %copy.93 = f32[2,8,512,1536]{3,1,2,0:T(8,128)} copy(f32[2,8,512,1536]{3,2,1,0:T(8,128)} %bitcast.233) | data formatting | bytes 100663296 | tf_op jit(solution)/shard_map/while/body/eval_jaxpr/while
  1111.3 33.4 %slice.104 = f32[12,785920]{1,0:T(8,128)} slice(f32[12,786432]{1,0:T(8,128)} %bitcast.236), slice={[0:12], [0:785920]} | slice | bytes 75448320 | tf_op jit(solution)/shard_map/while/body/eval_jaxpr/while/body/eval_jaxpr/slice | solution.py:53
  1144.7 67.4 %reshape.604 = f32[12,512,1535]{2,1,0:T(8,128)} reshape(f32[12,785920]{1,0:T(8,128)} %slice.104) | data formatting | bytes 75448320 | tf_op jit(solution)/shard_map/while/body/eval_jaxpr/while/body/eval_jaxpr/reshape | solution.py:53
  1311.6 69.3 %reshape.605 = bf16[12,785920]{1,0:T(8,128)(2,1)} reshape(bf16[12,512,1535]{2,1,0:T(8,128)(2,1)} %pad.84) | data formatting | bytes 37724160 | tf_op jit(solution)/shard_map/while/body/eval_jaxpr/while/body/eval_jaxpr/reshape | solution.py:62
  1408.0 45.9 %copy.94 = f32[2,8,512,1536]{3,2,1,0:T(8,128)} copy(f32[2,8,512,1536]{3,1,2,0:T(8,128)} %bitcast.234) | data formatting | bytes 100663296 | tf_op jit(solution)/shard_map/while/body/eval_jaxpr/while
  1534.2 46.1 %copy.93 = f32[2,8,512,1536]{3,1,2,0:T(8,128)} copy(f32[2,8,512,1536]{3,2,1,0:T(8,128)} %bitcast.233) | data formatting | bytes 100663296 | tf_op jit(solution)/shard_map/while/body/eval_jaxpr/while
  1613.8 67.4 %reshape.604 = f32[12,512,1535]{2,1,0:T(8,128)} reshape(f32[12,785920]{1,0:T(8,128)} %slice.104) | data formatting | bytes 75448320 | tf_op jit(solution)/shard_map/while/body/eval_jaxpr/while/body/eval_jaxpr/reshape | solution.py:53
  1782.3 69.3 %reshape.605 = bf16[12,785920]{1,0:T(8,128)(2,1)} reshape(bf16[12,512,1535]{2,1,0:T(8,128)(2,1)} %pad.84) | data formatting | bytes 37724160 | tf_op jit(solution)/shard_map/while/body/eval_jaxpr/while/body/eval_jaxpr/reshape | solution.py:62
  1878.6 45.9 %copy.94 = f32[2,8,512,1536]{3,2,1,0:T(8,128)} copy(f32[2,8,512,1536]{3,1,2,0:T(8,128)} %bitcast.234) | data formatting | bytes 100663296 | tf_op jit(solution)/shard_map/while/body/eval_jaxpr/while
  1979.7 38.7 %all-reduce.9 = (f32[768]{0:T(1024)S(1)}, f32[768]{0:T(1024)S(1)}, f32[768,8]{0,1:T(8,128)S(1)}, f32[32,12]{0,1:T(8,128)}, f32[3]{0:T(128)S(1)}, /*index=5*/f32[]{:T(128)}) all-reduce(f32[768]{0:T(1024)S(1)} %get-tuple-element.702, f32[768]{0:T(1024)S(1)} %copy-done.56, ...), channel_id=2, replica_groups=mesh['dp'=4,'expert'=8] {'dp','expert'}, use_global_device_ids=true, to_apply=%region_19.21.clone | all-reduce | flops 8068 | bytes 64544
  2037.8 46.0 %reduce-scatter.6.cloned.1.call-done = f32[24,2304]{1,0:T(8,128)} async-done(((f32[768,2304]{1,0:T(8,128)}), f32[24,2304]{1,0:T(8,128)}) %reduce-scatter.6.cloned.1.call-update) | async-done | bytes 221200 | tf_op jit(solution)/shard_map/reduce_scatter | solution.py:391
  (323 shorter events, 889.4 us)
Async XLA Ops:
  7.2 49.8 %copy-start.57 = (s32[1,1024]{1,0:T(1,128)S(1)}, s32[1,1024]{1,0:T(1,128)}, u32[]{:S(2)}) copy-start(s32[1,1024]{1,0:T(1,128)} %param.34) | copy-start | bytes 12292
  7.2 49.8 %copy-start.46 = (s32[1,1024]{1,0:T(1,128)S(1)}, s32[1,1024]{1,0:T(1,128)}, u32[]{:S(2)}) copy-start(s32[1,1024]{1,0:T(1,128)} %param.33) | copy-start | bytes 12292
  7.2 49.8 %copy-start.36 = (s32[1,1024]{1,0:T(1,128)S(1)}, s32[1,1024]{1,0:T(1,128)}, u32[]{:S(2)}) copy-start(s32[1,1024]{1,0:T(1,128)} %param.32) | copy-start | bytes 12292
  7.2 66.7 %all-gather.4.cloned.1.call-start = ((), (), s32[]{:S(2)}) async-start(), calls=%async_computation.8 | async-start | bytes 3649536 | tf_op jit(solution)/shard_map/all_gather | solution.py:235
  8.0 584.9 %all-gather.6.cloned.1.call-start = ((), (), s32[]{:S(2)}) async-start(), calls=%async_computation.9 | async-start | bytes 1216512 | tf_op jit(solution)/shard_map/all_gather | solution.py:236
  609.7 65.8 %slice-start = ((s8[4718592]{0:T(1024)(128)(4,1)}), s8[4194304]{0:T(1024)(128)(4,1)S(1)}, s32[]{:S(2)}) async-start(s8[4718592]{0:T(1024)(128)(4,1)} %bitcast.266), calls=%async_computation.14 | async-start | bytes 8388608
  686.0 107.4 %copy-start.58 = (s32[1,1024]{1,0:T(1,128)S(1)}, s32[1,1024]{1,0:T(1,128)}, u32[]{:S(2)}) copy-start(s32[1,1024]{1,0:T(1,128)} %param.34) | copy-start | bytes 12292
  686.0 107.4 %copy-start.37 = (s32[1,1024]{1,0:T(1,128)S(1)}, s32[1,1024]{1,0:T(1,128)}, u32[]{:S(2)}) copy-start(s32[1,1024]{1,0:T(1,128)} %param.32) | copy-start | bytes 12292
  686.0 107.4 %copy-start.47 = (s32[1,1024]{1,0:T(1,128)S(1)}, s32[1,1024]{1,0:T(1,128)}, u32[]{:S(2)}) copy-start(s32[1,1024]{1,0:T(1,128)} %param.33) | copy-start | bytes 12292
  686.0 109.3 %all-to-all-start.1 = ((bf16[1,8,160,768]{3,2,0,1:T(8,128)(2,1)}), bf16[1,8,160,768]{3,2,0,1:T(8,128)(2,1)}, u32[]{:S(2)}, u32[]{:S(2)}) async-start(bf16[1,8,160,768]{3,2,0,1:T(8,128)(2,1)} %convert_bitcast_fusion.2), calls=%async_computation.1 | async-start | bytes 3932160 | tf_op jit(solution)/shard_map/all_to_all | solution.py:285
  690.7 1341.4 %reduce-scatter.12.cloned.1.call-start = ((), (), s32[]{:S(2)}) async-start(), calls=%async_computation.13 | async-start | bytes 5898240 | tf_op jit(solution)/shard_map/reduce_scatter | solution.py:342
  795.2 186.8 %copy-start.31 = (f32[1024,8]{0,1:T(8,128)}, f32[1024,8]{0,1:T(8,128)S(1)}, u32[]{:S(2)}) copy-start(f32[1024,8]{0,1:T(8,128)S(1)} %get-tuple-element.780) | copy-start | bytes 98308
  795.2 186.8 %copy-start.39 = (f32[1024]{0:T(1024)}, f32[1024]{0:T(1024)S(1)}, u32[]{:S(2)}) copy-start(f32[1024]{0:T(1024)S(1)} %get-tuple-element.779) | copy-start | bytes 12292
  795.3 186.8 %copy-start.44 = (f32[1024]{0:T(1024)}, f32[1024]{0:T(1024)S(1)}, u32[]{:S(2)}) copy-start(f32[1024]{0:T(1024)S(1)} %fusion.89) | copy-start | bytes 12292
  795.3 188.9 %copy-start.41 = (f32[1024]{0:T(1024)}, f32[1024]{0:T(1024)S(1)}, u32[]{:S(2)}) copy-start(f32[1024]{0:T(1024)S(1)} %select_reduce_fusion) | copy-start | bytes 12292
  809.2 172.9 %copy-start.48 = (f32[1024]{0:T(1024)}, f32[1024]{0:T(1024)S(1)}, u32[]{:S(2)}) copy-start(f32[1024]{0:T(1024)S(1)} %get-tuple-element.776) | copy-start | bytes 12292
  880.4 1154.6 %reduce-scatter.10.cloned.1.call-start = ((), (), s32[]{:S(2)}) async-start(), calls=%async_computation.12 | async-start | bytes 5898240 | tf_op jit(solution)/shard_map/reduce_scatter | solution.py:339
  924.5 47.5 %all-to-all-start.3 = ((bf16[1,8,160,768]{3,2,0,1:T(8,128)(2,1)}), bf16[1,8,160,768]{3,2,0,1:T(8,128)(2,1)}, u32[]{:S(2)}, u32[]{:S(2)}) async-start(bf16[1,8,160,768]{3,2,0,1:T(8,128)(2,1)} %convert_bitcast_fusion.1), calls=%async_computation.3 | async-start | bytes 3932160 | tf_op jit(solution)/shard_map/all_to_all | solution.py:326
  928.9 1108.9 %reduce-scatter.8.cloned.1.call-start = ((), (), s32[]{:S(2)}) async-start(), calls=%async_computation.11 | async-start | bytes 2433024 | tf_op jit(solution)/shard_map/reduce_scatter | solution.py:392
  929.1 55.1 %copy-start.54 = (f32[1024]{0:T(1024)}, f32[1024]{0:T(1024)S(1)}, u32[]{:S(2)}) copy-start(f32[1024]{0:T(1024)S(1)} %convert_element_type.181) | copy-start | bytes 12292
  994.1 1089.7 %reduce-scatter.6.cloned.1.call-start = ((), (), s32[]{:S(2)}) async-start(), calls=%async_computation.10 | async-start | bytes 7299072 | tf_op jit(solution)/shard_map/reduce_scatter | solution.py:391
  1144.7 67.4 %copy-start.5 = (bf16[1024,12,64]{0,2,1:T(8,128)(2,1)S(1)}, bf16[1024,12,64]{0,2,1:T(8,128)(2,1)}, u32[]{:S(2)}) copy-start(bf16[1024,12,64]{0,2,1:T(8,128)(2,1)} %get-tuple-element.1036) | copy-start | bytes 4718596 | tf_op jit(solution)/shard_map/while/body/eval_jaxpr/while
  1613.8 67.4 %copy-start.5 = (bf16[1024,12,64]{0,2,1:T(8,128)(2,1)S(1)}, bf16[1024,12,64]{0,2,1:T(8,128)(2,1)}, u32[]{:S(2)}) copy-start(bf16[1024,12,64]{0,2,1:T(8,128)(2,1)} %get-tuple-element.1036) | copy-start | bytes 4718596 | tf_op jit(solution)/shard_map/while/body/eval_jaxpr/while
  2031.5 52.3 %copy-start.1 = (f32[32,12]{0,1:T(8,128)S(1)}, f32[32,12]{0,1:T(8,128)}, u32[]{:S(2)}) copy-start(f32[32,12]{0,1:T(8,128)} %param.29) | copy-start | bytes 4612
  (61 other events, 633.6 us)
Sparse Core Ops, SparseCore 0:
  11.0 62.9 all-gather.3
  76.9 53.0 all-gather.5
  880.5 45.9 reduce-scatter.11
  929.1 47.8 reduce-scatter.9
  994.2 97.5 reduce-scatter.7
  1965.9 117.8 reduce-scatter.5
where the time goes:
time: 2100 us; the launch traced here: 2090 us
  local copies, waits for them, and re-layouts  1130 us (54%)
  matrix products  336 us (16%)
  blocking collectives  278 us (13%)
  other arithmetic  186 us (9%)
  waiting for transfers between devices  107 us (5%)
  loops' own time  32.5 us (2%)
    while x58, local copies, waits for them, and re-layouts  400 us
    reshape x4, local copies, waits for them, and re-layouts, toeplitz_block(): jnp.tile(band, (1, block_rows))[:, :block_rows * width]  271 us
    reshape x2, local copies, waits for them, and re-layouts, diagonal_sums(): jnp.pad(grad_scores, ((0, 0), (0, 0), (block_rows - 1, 0)))  139 us
    slice x4, local copies, waits for them, and re-layouts, toeplitz_block(): jnp.tile(band, (1, block_rows))[:, :block_rows * width]  134 us
    dot_general x4, matrix products, block_scores(): jnp.einsum('qhd,khd->hqk', query_block, keys_all, preferred_element_type=...  108 us
    all_gather x1, blocking collectives, body(): lax.all_gather(router_weight, ('dp', 'expert'), axis=0, tiled=True)  99.9 us
    unnamed x2, blocking collectives  80.7 us
    reshape x2, other arithmetic, diagonal_sums(): jnp.pad(placed, ((0, 0), (0, block_rows)))  54 us
  transfers between devices with their start and end apart: 8, of which 3 were waited for; matrix products, arithmetic and copies ran while one was open for 75% of the time, Pallas kernels for 0%

commit v1 on v0

v1 whole, which is shorter than its diff:
```python
import functools

import jax
import jax.numpy as jnp
from jax import lax
from jax.experimental import pallas as pl
from jax.experimental.pallas import tpu as pltpu
from jax.sharding import PartitionSpec as P

EPSILON = 1e-06
HIGHEST = lax.Precision.HIGHEST


def smooth_unit(values):
    return jax.nn.gelu(values, approximate=True)


def smooth_slope(values):
    unused_value, pullback = jax.vjp(smooth_unit, values)
    return pullback(jnp.ones_like(values))[0]


def norm_factor(values):
    return lax.rsqrt(jnp.mean(values * values, axis=-1, keepdims=True) + EPSILON)


def norm_backward(grad_rows, values, factor, norm_gain):
    normed = values * factor
    weighted = grad_rows * norm_gain
    gain_grad = jnp.sum(grad_rows * normed, axis=0)
    values_grad = factor * (weighted - normed * jnp.mean(weighted * normed, axis=-1, keepdims=True))
    return (values_grad, gain_grad)


def bucket_table(buckets, rel_bias):
    indices = jnp.arange(rel_bias.shape[0], dtype=jnp.int32)
    return (buckets[:, None] == indices[None, :]).astype(jnp.float32)


def scatter_rows(rows, slot_index, experts, capacity):
    empty = jnp.zeros((experts * capacity, rows.shape[1]), rows.dtype)
    return empty.at[slot_index].set(rows, mode="drop").reshape(experts, 1, capacity, rows.shape[1])


MASK_STEP = 1e30
ROWS = 256
LANES = 128
REACH = 5
bf16, f32 = jnp.bfloat16, jnp.float32
NT = (((1,), (1,)), ((), ()))
NN = (((1,), (0,)), ((), ()))


def dot(left, right, dims):
    return lax.dot_general(left, right, dims, preferred_element_type=f32)


def bias_windows(values, reach):
    heads, offsets = values.shape
    chunks = (offsets + 1) // LANES
    turned = jnp.pad(values[:, ::-1], ((0, 0), (1, 0))).reshape(heads, chunks, LANES)
    middle = chunks // 2
    groups = list(range(-reach, reach + 1))
    first = [middle - g for g in groups]
    here = turned[:, first[-1] : first[0] + 1][:, ::-1]
    before = turned[:, first[-1] - 1 : first[0]][:, ::-1]
    return jnp.concatenate([here, before], axis=2)


def toeplitz_kernel(reach, window_ref, tile_ref):
    for g in range(2 * reach + 1):
        row = window_ref[0, g : g + 1, :]
        full = jnp.broadcast_to(row, (LANES, 2 * LANES))
        turned = pltpu.roll(full, 0, 1, stride=1, stride_axis=0)
        tile_ref[0, g * LANES : (g + 1) * LANES, :] = turned[:, :LANES]


def toeplitz_tiles(windows):
    heads, groups, width = windows.shape
    return pl.pallas_call(
        functools.partial(toeplitz_kernel, groups // 2),
        grid=(heads,),
        in_specs=[pl.BlockSpec((1, groups, width), lambda n: (n, 0, 0))],
        out_specs=pl.BlockSpec((1, groups * LANES, LANES), lambda n: (n, 0, 0)),
        out_shape=jax.ShapeDtypeStruct((heads, groups * LANES, LANES), f32),
        name="toeplitz_tiles",
    )(windows)


def head_lanes(rows, head, head_dim):
    lane = lax.broadcasted_iota(jnp.int32, rows.shape, 1)
    return jnp.where((lane >= head * head_dim) & (lane < (head + 1) * head_dim), rows, jnp.zeros_like(rows))


def bias_tile(bias_ref, head, offset):
    parts = [
        bias_ref[head, pl.ds(pl.multiple_of(offset - LANES * part, LANES), ROWS), :]
        for part in range(ROWS // LANES)
    ]
    return jnp.concatenate(parts, axis=1)


def forward_kernel(head_dim, reach, low_ref, high_ref, q_ref, k_ref, v_ref, qx_ref, kx_ref, bias_ref, mix_ref, lse_ref, vt_ref):
    length, width = q_ref.shape
    heads = width // head_dim
    scale = head_dim ** (-0.5)
    for c in range(width // LANES):
        vt_ref[c * LANES : (c + 1) * LANES, :] = v_ref[:, c * LANES : (c + 1) * LANES].T
    per = LANES // head_dim

    def one_block(qb, unused):
        first = pl.multiple_of(qb * ROWS, ROWS)
        qx = qx_ref[pl.ds(first, ROWS), :]
        queries = []
        for h in range(heads):
            c = h // per
            pair = q_ref[pl.ds(first, ROWS), c * LANES : (c + 1) * LANES] * jnp.asarray(scale, bf16)
            queries.append(jnp.concatenate([head_lanes(pair, h % per, head_dim), qx], axis=1))

        def one_tile(kb, carry):
            keys_at = pl.multiple_of(kb * ROWS, ROWS)
            offset = pl.multiple_of(keys_at - first + LANES * reach, LANES)
            kx = kx_ref[pl.ds(keys_at, ROWS), :]
            out = []
            for h in range(heads):
                c = h // per
                peak, total, mixed = carry[h]
                keys = jnp.concatenate([k_ref[pl.ds(keys_at, ROWS), c * LANES : (c + 1) * LANES], kx], axis=1)
                scores = dot(keys, queries[h], NT) + bias_tile(bias_ref, h, offset)
                new_peak = jnp.maximum(peak, jnp.max(scores, axis=0, keepdims=True))
                weights = jnp.exp(scores - new_peak)
                shrink = jnp.exp(peak - new_peak)
                total = total * shrink + jnp.sum(weights, axis=0, keepdims=True)
                values = vt_ref[h * head_dim : (h + 1) * head_dim, pl.ds(keys_at, ROWS)]
                mixed = mixed * shrink + dot(values, weights.astype(bf16), NN)
                out.append((new_peak, total, mixed))
            return tuple(out)

        start = tuple(
            (jnp.full((1, ROWS), -3e38, f32), jnp.zeros((1, ROWS), f32), jnp.zeros((head_dim, ROWS), f32))
            for h in range(heads)
        )
        done = lax.fori_loop(low_ref[qb], high_ref[qb], one_tile, start)
        for c in range(width // LANES):
            rows = jnp.concatenate([done[h][2] / done[h][1] for h in range(c * per, (c + 1) * per)], axis=0)
            mix_ref[pl.ds(first, ROWS), c * LANES : (c + 1) * LANES] = rows.T.astype(bf16)
        for h in range(heads):
            lse_ref[0, h : h + 1, pl.ds(first, ROWS)] = done[h][0] + jnp.log(done[h][1])
        return unused

    lax.fori_loop(0, length // ROWS, one_block, 0)


def backward_kernel(head_dim, reach, low_ref, high_ref, q_ref, k_ref, v_ref, dmix_ref, mix_ref, qx_ref, kx_ref, bias_ref, lse_ref,
                    grad_ref, diag_ref, kt_ref, dk_ref, dv_ref, along_ref):
    length, width = q_ref.shape
    heads = width // head_dim
    scale = head_dim ** (-0.5)
    per = LANES // head_dim
    for c in range(width // LANES):
        kt_ref[c * LANES : (c + 1) * LANES, :] = k_ref[:, c * LANES : (c + 1) * LANES].T
    dk_ref[...] = jnp.zeros_like(dk_ref)
    dv_ref[...] = jnp.zeros_like(dv_ref)
    along_ref[...] = jnp.zeros_like(along_ref)

    def one_block(qb, unused):
        first = pl.multiple_of(qb * ROWS, ROWS)
        qx = qx_ref[pl.ds(first, ROWS), :]
        queries, d_mixes, deltas = [], [], []
        for h in range(heads):
            c = h // per
            lanes = slice(c * LANES, (c + 1) * LANES)
            queries.append(head_lanes(q_ref[pl.ds(first, ROWS), lanes] * jnp.asarray(scale, bf16), h % per, head_dim))
            d_mix = dmix_ref[pl.ds(first, ROWS), lanes]
            d_mixes.append(head_lanes(d_mix, h % per, head_dim))
            if h % per == 0:
                product = (d_mix.astype(f32) * mix_ref[pl.ds(first, ROWS), lanes].astype(f32)).T
            deltas.append(jnp.sum(product[(h % per) * head_dim : (h % per + 1) * head_dim], axis=0, keepdims=True))
        wide = [jnp.concatenate([queries[h], qx], axis=1) for h in range(heads)]
        lses = [lse_ref[0, h : h + 1, pl.ds(first, ROWS)] for h in range(heads)]

        def one_tile(kb, carry):
            keys_at = pl.multiple_of(kb * ROWS, ROWS)
            offset = pl.multiple_of(keys_at - first + LANES * reach, LANES)
            kx = kx_ref[pl.ds(keys_at, ROWS), :]
            out = []
            low_weights, low_scores = [], []
            for h in range(heads):
                c = h // per
                lanes = slice(c * LANES, (c + 1) * LANES)
                keys = jnp.concatenate([k_ref[pl.ds(keys_at, ROWS), lanes], kx], axis=1)
                scores = dot(keys, wide[h], NT) + bias_tile(bias_ref, h, offset)
                weights = jnp.exp(scores - lses[h])
                d_weights = dot(v_ref[pl.ds(keys_at, ROWS), lanes], d_mixes[h], NT)
                d_scores = weights * (d_weights - deltas[h])
                for part in range(ROWS // LANES):
                    at = pl.ds(pl.multiple_of(offset - LANES * part, LANES), ROWS)
                    along_ref[h, at, :] += d_scores[:, part * LANES : (part + 1) * LANES]
                low_weights.append(weights.astype(bf16))
                low_scores.append(d_scores.astype(bf16))
                out.append(carry[h] + dot(kt_ref[h * head_dim : (h + 1) * head_dim, pl.ds(keys_at, ROWS)], low_scores[h], NN))
            for c in range(width // LANES):
                mine = range(c * per, (c + 1) * per)
                lanes = slice(c * LANES, (c + 1) * LANES)
                dv_ref[pl.ds(keys_at, ROWS), lanes] += dot(
                    jnp.concatenate([low_weights[h] for h in mine], axis=1), jnp.concatenate([d_mixes[h] for h in mine], axis=0), NN)
                dk_ref[pl.ds(keys_at, ROWS), lanes] += dot(
                    jnp.concatenate([low_scores[h] for h in mine], axis=1), jnp.concatenate([queries[h] for h in mine], axis=0), NN)
            return tuple(out)

        start = tuple(jnp.zeros((head_dim, ROWS), f32) for h in range(heads))
        done = lax.fori_loop(low_ref[qb], high_ref[qb], one_tile, start)
        for c in range(width // LANES):
            rows = jnp.concatenate([done[h] for h in range(c * per, (c + 1) * per)], axis=0) * scale
            grad_ref[0, pl.ds(first, ROWS), c * LANES : (c + 1) * LANES] = rows.T.astype(bf16)
        return unused

    lax.fori_loop(0, length // ROWS, one_block, 0)
    grad_ref[1] = dk_ref[...].astype(bf16)
    grad_ref[2] = dv_ref[...].astype(bf16)
    for h in range(heads):
        for g in range(2 * reach + 1):
            tile = along_ref[h, g * LANES : (g + 1) * LANES, :]
            turned = jnp.concatenate([tile, jnp.zeros_like(tile)], axis=1)
            step = LANES // 2
            while step >= 8:
                turned = turned[:step] + pltpu.roll(turned[step:], 2 * LANES - step, 1)
                step //= 2
            while step:
                turned = turned + pltpu.roll(pltpu.roll(turned, 2 * LANES - step, 1), 8 - step, 0)
                step //= 2
            diag_ref[h, g : g + 1, :] = turned[:1]


def tile_bounds(segments):
    length = segments.shape[0]
    blocks = segments.reshape(length // ROWS, ROWS)
    starts = jnp.sum((segments[None, :] < blocks[:, :1]).astype(jnp.int32), axis=1)
    ends = jnp.sum((segments[None, :] <= blocks[:, -1:]).astype(jnp.int32), axis=1)
    return starts // ROWS, (ends + ROWS - 1) // ROWS


def mask_columns(segments, validity, segment_count=8):
    length = segments.shape[0]
    short = 1
    while short * (short + 1) < length:
        short += 1
    at = jnp.arange(length, dtype=jnp.int32)
    lane = jnp.arange(LANES, dtype=jnp.int32)[None, :]
    in_first = (lane >= segment_count) & (lane < segment_count + short)
    in_second = (lane >= segment_count + short) & (lane < segment_count + 2 * short + 1)
    mine = (
        (lane == segments[:, None])
        | (in_first & (lane - segment_count == (at % short)[:, None]))
        | (in_second & (lane - segment_count - short == (at % (short + 1))[:, None]))
    )
    used = lane < segment_count + 2 * short + 1
    query_side = jnp.where(used & ~mine, -MASK_STEP, 0.0).astype(bf16)
    real = (validity == 1)[:, None]
    key_side = jnp.where(mine & jnp.where(real, lane < segment_count, lane >= segment_count), 1.0, 0.0).astype(bf16)
    return query_side, key_side


def attend_forward(packed, query_side, key_side, bounds, tiles, head_dim, heads_step):
    length = packed.shape[0]
    width = packed.shape[1] // 3
    heads = tiles.shape[0]
    reach = tiles.shape[1] // LANES // 2
    block = heads_step * head_dim
    steps = width // block
    grid_spec = pltpu.PrefetchScalarGridSpec(
        num_scalar_prefetch=2,
        grid=(steps,),
        in_specs=[
            pl.BlockSpec((length, block), lambda p, *_: (0, p)),
            pl.BlockSpec((length, block), lambda p, *_: (0, p + steps)),
            pl.BlockSpec((length, block), lambda p, *_: (0, p + 2 * steps)),
            pl.BlockSpec((length, LANES), lambda p, *_: (0, 0)),
            pl.BlockSpec((length, LANES), lambda p, *_: (0, 0)),
            pl.BlockSpec((heads_step, tiles.shape[1], LANES), lambda p, *_: (p, 0, 0)),
        ],
        out_specs=[
            pl.BlockSpec((length, block), lambda p, *_: (0, p)),
            pl.BlockSpec((1, heads_step, length), lambda p, *_: (p, 0, 0)),
        ],
        scratch_shapes=[pltpu.VMEM((block, length), bf16)],
    )
    return pl.pallas_call(
        functools.partial(forward_kernel, head_dim, reach),
        grid_spec=grid_spec,
        out_shape=[
            jax.ShapeDtypeStruct((length, width), bf16),
            jax.ShapeDtypeStruct((steps, heads_step, length), f32),
        ],
        compiler_params=pltpu.CompilerParams(vmem_limit_bytes=48 * 2**20),
        name="attend_forward",
    )(*bounds, packed, packed, packed, query_side, key_side, tiles)


def attend_backward(packed, d_mix, mix, lse, query_side, key_side, bounds, tiles, head_dim, heads_step):
    length = packed.shape[0]
    width = packed.shape[1] // 3
    heads = tiles.shape[0]
    reach = tiles.shape[1] // LANES // 2
    groups = 2 * reach + 1
    block = heads_step * head_dim
    steps = width // block
    grid_spec = pltpu.PrefetchScalarGridSpec(
        num_scalar_prefetch=2,
        grid=(steps,),
        in_specs=[
            pl.BlockSpec((length, block), lambda p, *_: (0, p)),
            pl.BlockSpec((length, block), lambda p, *_: (0, p + steps)),
            pl.BlockSpec((length, block), lambda p, *_: (0, p + 2 * steps)),
            pl.BlockSpec((length, block), lambda p, *_: (0, p)),
            pl.BlockSpec((length, block), lambda p, *_: (0, p)),
            pl.BlockSpec((length, LANES), lambda p, *_: (0, 0)),
            pl.BlockSpec((length, LANES), lambda p, *_: (0, 0)),
            pl.BlockSpec((heads_step, tiles.shape[1], LANES), lambda p, *_: (p, 0, 0)),
            pl.BlockSpec((1, heads_step, length), lambda p, *_: (p, 0, 0)),
        ],
        out_specs=[
            pl.BlockSpec((3, length, block), lambda p, *_: (0, 0, p)),
            pl.BlockSpec((heads_step, groups, 2 * LANES), lambda p, *_: (p, 0, 0)),
        ],
        scratch_shapes=[
            pltpu.VMEM((block, length), bf16),
            pltpu.VMEM((length, block), f32),
            pltpu.VMEM((length, block), f32),
            pltpu.VMEM((heads_step, groups * LANES, LANES), f32),
        ],
    )
    return pl.pallas_call(
        functools.partial(backward_kernel, head_dim, reach),
        grid_spec=grid_spec,
        out_shape=[
            jax.ShapeDtypeStruct((3, length, width), bf16),
            jax.ShapeDtypeStruct((heads, groups, 2 * LANES), f32),
        ],
        compiler_params=pltpu.CompilerParams(vmem_limit_bytes=56 * 2**20),
        name="attend_backward",
    )(*bounds, packed, packed, packed, d_mix, mix, query_side, key_side, tiles, lse)


def body(
    inputs,
    cotangent,
    attn_gain,
    qkv_weight,
    out_weight,
    ffn_gain,
    router_weight,
    rel_bias,
    expert_in,
    expert_out,
    routes,
    positions,
    dropped,
    segment_ids,
    valid_mask,
    buckets,
):
    seq_count, seq_length, model_width = inputs.shape
    tokens = seq_count * seq_length
    dense_full = (
        lax.all_gather(attn_gain, ("dp", "expert"), axis=0, tiled=True),
        lax.all_gather(qkv_weight, ("dp", "expert"), axis=0, tiled=True),
        lax.all_gather(out_weight, ("dp", "expert"), axis=0, tiled=True),
        lax.all_gather(ffn_gain, ("dp", "expert"), axis=0, tiled=True),
        lax.all_gather(router_weight, ("dp", "expert"), axis=0, tiled=True),
    )
    gain_one = dense_full[0].astype(jnp.float32)
    gain_two = dense_full[3].astype(jnp.float32)
    one_hot_buckets = bucket_table(buckets, rel_bias)
    head_bias = jnp.dot(
        one_hot_buckets, rel_bias, precision=HIGHEST, preferred_element_type=jnp.float32
    ).T
    head_count = rel_bias.shape[1]
    head_dim = model_width // head_count
    windows = bias_windows(head_bias, REACH)
    tiles = toeplitz_tiles(windows)
    layer_in = inputs.astype(jnp.float32)
    saved = []
    for seq in range(seq_count):
        factor = norm_factor(layer_in[seq])
        normed = (layer_in[seq] * factor * gain_one).astype(jnp.bfloat16)
        packed = jnp.dot(normed, dense_full[1], preferred_element_type=jnp.float32).astype(jnp.bfloat16)
        masks = mask_columns(segment_ids[seq], valid_mask[seq])
        bounds = tile_bounds(segment_ids[seq])
        mixed, log_totals = attend_forward(packed, *masks, bounds, tiles, head_dim, 2)
        attn_out = jnp.dot(mixed, dense_full[2], preferred_element_type=jnp.float32)
        saved.append((factor, normed, packed, masks, bounds, mixed, log_totals, attn_out))
    mid_rows = (layer_in + jnp.stack([state[-1] for state in saved])).reshape(tokens, model_width)
    experts = dense_full[4].shape[1]
    capacity = 5 * tokens // (4 * experts)
    route_ids = routes.reshape(tokens)
    slot_index = jnp.where(
        dropped.reshape(tokens) == 1,
        experts * capacity,
        route_ids * capacity + positions.reshape(tokens),
    )
    mid_factor = norm_factor(mid_rows)
    ffn_normed = (mid_rows * mid_factor * gain_two).astype(jnp.bfloat16)
    logits = jnp.dot(ffn_normed, dense_full[4], preferred_element_type=jnp.float32)
    router_probs = jax.nn.softmax(logits, axis=-1)
    chosen = (route_ids[:, None] == jnp.arange(experts, dtype=jnp.int32)[None, :]).astype(
        jnp.float32
    )
    gate_value = jnp.sum(router_probs * chosen, axis=-1)
    send_rows = scatter_rows(ffn_normed, slot_index, experts, capacity)
    received = lax.all_to_all(send_rows, "expert", split_axis=0, concat_axis=1, tiled=True)
    pre_act = jnp.einsum("escd,edf->escf", received, expert_in, preferred_element_type=jnp.float32)
    hidden = smooth_unit(pre_act).astype(jnp.bfloat16)
    rows_out = jnp.einsum(
        "escf,efd->escd", hidden, expert_out, preferred_element_type=jnp.float32
    ).astype(jnp.bfloat16)
    returned = lax.all_to_all(rows_out, "expert", split_axis=1, concat_axis=0, tiled=True)
    picked = jnp.take(
        returned.reshape(experts * capacity, model_width),
        slot_index,
        axis=0,
        mode="fill",
        fill_value=0,
    ).astype(jnp.float32)
    final_rows = mid_rows + gate_value[:, None] * picked
    output = final_rows.astype(jnp.bfloat16).reshape(inputs.shape)
    live_rows = valid_mask.reshape(tokens).astype(jnp.float32)
    flat_in = layer_in.reshape(tokens, model_width)
    square_sums = jnp.stack(
        [
            jnp.sum(live_rows[:, None] * flat_in * flat_in),
            jnp.sum(live_rows[:, None] * mid_rows * mid_rows),
            jnp.sum(live_rows[:, None] * final_rows * final_rows),
        ]
    )
    live_count = jnp.sum(live_rows)
    dense_back = (
        lax.all_gather(attn_gain, ("dp", "expert"), axis=0, tiled=True),
        lax.all_gather(qkv_weight, ("dp", "expert"), axis=0, tiled=True),
        lax.all_gather(out_weight, ("dp", "expert"), axis=0, tiled=True),
        lax.all_gather(ffn_gain, ("dp", "expert"), axis=0, tiled=True),
        lax.all_gather(router_weight, ("dp", "expert"), axis=0, tiled=True),
    )
    back_gain_one = dense_back[0].astype(jnp.float32)
    back_gain_two = dense_back[3].astype(jnp.float32)
    grad_final = cotangent.astype(jnp.float32).reshape(tokens, model_width)
    grad_gate = jnp.sum(grad_final * picked, axis=-1)
    grad_rows = (gate_value[:, None] * grad_final).astype(jnp.bfloat16)
    grad_send = scatter_rows(grad_rows, slot_index, experts, capacity)
    grad_rows_out = lax.all_to_all(grad_send, "expert", split_axis=0, concat_axis=1, tiled=True)
    grad_hidden = jnp.einsum(
        "escd,efd->escf", grad_rows_out, expert_out, preferred_element_type=jnp.float32
    )
    grad_pre = (grad_hidden * smooth_slope(pre_act)).astype(jnp.bfloat16)
    grad_rows_in = jnp.einsum(
        "escf,edf->escd", grad_pre, expert_in, preferred_element_type=jnp.float32
    ).astype(jnp.bfloat16)
    grad_back = lax.all_to_all(grad_rows_in, "expert", split_axis=1, concat_axis=0, tiled=True)
    grad_expert_rows = jnp.take(
        grad_back.reshape(experts * capacity, model_width),
        slot_index,
        axis=0,
        mode="fill",
        fill_value=0,
    ).astype(jnp.float32)
    part_in = jnp.einsum("escd,escf->edf", received, grad_pre, preferred_element_type=jnp.float32)
    part_out = jnp.einsum(
        "escf,escd->efd", hidden, grad_rows_out, preferred_element_type=jnp.float32
    )
    grad_expert_in, grad_expert_out = (
        lax.psum_scatter(
            part_in.astype(jnp.bfloat16), "dp", scatter_dimension=2, tiled=True
        ).astype(jnp.float32),
        lax.psum_scatter(
            part_out.astype(jnp.bfloat16), "dp", scatter_dimension=1, tiled=True
        ).astype(jnp.float32),
    )
    grad_logits = (router_probs * (chosen - gate_value[:, None]) * grad_gate[:, None]).astype(
        jnp.bfloat16
    )
    grad_router = jnp.einsum(
        "td,te->de", ffn_normed, grad_logits, preferred_element_type=jnp.float32
    )
    grad_ffn_normed = (
        jnp.einsum("te,de->td", grad_logits, dense_back[4], preferred_element_type=jnp.float32)
        + grad_expert_rows
    )
    grad_mid_norm, grad_gain_two = norm_backward(
        grad_ffn_normed, mid_rows, mid_factor, back_gain_two
    )
    grad_mid = grad_final + grad_mid_norm
    grad_mid_seq = grad_mid.reshape(seq_count, seq_length, model_width)

    one_hot_windows = bias_windows(one_hot_buckets.T, REACH)
    attn_totals, grad_attn_in = None, []
    for seq in range(seq_count):
        factor, normed, packed, masks, bounds, mixed, log_totals, unused = saved[seq]
        grad_attn_low = grad_mid_seq[seq].astype(jnp.bfloat16)
        grad_out_w = jnp.einsum("td,te->de", mixed, grad_attn_low, preferred_element_type=jnp.float32)
        grad_mixed = jnp.einsum("te,de->td", grad_attn_low, dense_back[2], preferred_element_type=jnp.float32)
        grad_parts, grad_diagonals = attend_backward(
            packed, grad_mixed.astype(jnp.bfloat16), mixed, log_totals, *masks, bounds, tiles, head_dim, 2
        )
        grad_buckets = jnp.einsum("hgp,bgp->bh", grad_diagonals, one_hot_windows, precision=HIGHEST)
        grad_qkv_w = jnp.concatenate(
            [jnp.einsum("td,te->de", normed, grad_parts[i], preferred_element_type=jnp.float32) for i in range(3)], axis=1
        )
        w_parts = dense_back[1].reshape(model_width, 3, model_width)
        grad_normed = jnp.einsum("pte,dpe->td", grad_parts, w_parts, preferred_element_type=jnp.float32)
        grad_layer, grad_gain = norm_backward(grad_normed, layer_in[seq], factor, back_gain_one)
        grad_attn_in.append(grad_layer)
        grads_local = (grad_qkv_w, grad_out_w, grad_gain, grad_buckets)
        attn_totals = grads_local if attn_totals is None else jax.tree.map(jnp.add, attn_totals, grads_local)
    input_grad = grad_mid_seq + jnp.stack(grad_attn_in)
    grad_rel_local = attn_totals[3]
    grad_shards = (
        lax.psum_scatter(attn_totals[2], ("dp", "expert"), scatter_dimension=0, tiled=True),
        lax.psum_scatter(attn_totals[0], ("dp", "expert"), scatter_dimension=0, tiled=True),
        lax.psum_scatter(attn_totals[1], ("dp", "expert"), scatter_dimension=0, tiled=True),
        lax.psum_scatter(grad_gain_two, ("dp", "expert"), scatter_dimension=0, tiled=True),
        lax.psum_scatter(grad_router, ("dp", "expert"), scatter_dimension=0, tiled=True),
    )
    totals, count_all, grad_rel = lax.psum(
        (square_sums, live_count, grad_rel_local), ("dp", "expert")
    )
    stats = jnp.sqrt(totals / (count_all * model_width))
    return (
        output,
        input_grad,
        grad_shards[0],
        grad_shards[1],
        grad_shards[2],
        grad_shards[3],
        grad_shards[4],
        grad_rel,
        grad_expert_in,
        grad_expert_out,
        stats,
    )


def solution(mesh):
    in_specs = (
        P(("dp", "expert"), None, None),
        P(("dp", "expert"), None, None),
        P(("dp", "expert")),
        P(("dp", "expert"), None),
        P(("dp", "expert"), None),
        P(("dp", "expert")),
        P(("dp", "expert"), None),
        P(),
        P("expert", None, None),
        P("expert", None, None),
        P(("dp", "expert"), None),
        P(("dp", "expert"), None),
        P(("dp", "expert"), None),
        P(("dp", "expert"), None),
        P(("dp", "expert"), None),
        P(),
    )
    out_specs = (
        P(("dp", "expert"), None, None),
        P(("dp", "expert"), None, None),
        P(("dp", "expert")),
        P(("dp", "expert"), None),
        P(("dp", "expert"), None),
        P(("dp", "expert")),
        P(("dp", "expert"), None),
        P(),
        P("expert", None, "dp"),
        P("expert", "dp", None),
        P(),
    )
    return jax.shard_map(body, mesh=mesh, in_specs=in_specs, out_specs=out_specs, check_vma=False)
```

time: 2100 us -> 787 us (0.37)
  local copies, waits for them, and re-layouts: 1130 us -> 92.2 us
  matrix products: 336 us -> 118 us
  Pallas kernels: 0 us -> 159 us
  other arithmetic: 186 us -> 30.5 us
  waiting for transfers between devices: 107 us -> 73.2 us
  loops' own time: 32.5 us -> 0 us
    reshape x6 -> x0, local copies, waits for them, and re-layouts: 410 us -> none  [the longest x4 271 us: toeplitz_block(): jnp.tile(band, (1, block_rows))[:, :block_rows * width]]
    while x59 -> x0, local copies, waits for them, and re-layouts: 403 us -> none
    dot_general x21 -> x9, matrix products: 254 us -> 37.4 us  [the longest x1 10.8 us: body(): jnp.einsum('pte,dpe->td', grad_parts, w_parts, preferred_element_type=jnp...]
    pallas_call x0 -> x3, Pallas kernels: none -> 159 us  [the longest x1 85.6 us: attend_backward(): pl.pallas_call(functools.partial(backward_kernel, head_dim, reach), grid_...]
    slice x8 -> x3, local copies, waits for them, and re-layouts: 141 us -> 0.13 us  [the longest x1 0.07 us: tile_bounds(): blocks[:, :1]]
    another operation x6 -> x1, local copies, waits for them, and re-layouts: 54.9 us -> 0.01 us  [tile_bounds(): blocks = segments.reshape(length // ROWS, ROWS)]
    reshape x2 -> x0, other arithmetic: 54 us -> none  [diagonal_sums(): jnp.pad(placed, ((0, 0), (0, block_rows)))]
    reduce_sum x4 -> x1, other arithmetic: 49.7 us -> 0.22 us  [tile_bounds(): jnp.sum((segments[None, :] <= blocks[:, -1:]).astype(jnp.int32), axis=1)]
  transfers between devices with their start and end apart: 8 -> 8, of which waited for: 3 -> 3; matrix products, arithmetic and copies ran while one was open for 75% -> 20% of each run, Pallas kernels for 0% -> 20%
where the time goes in v1:
time: 787 us; the launch traced here: 776 us
  blocking collectives  279 us (35%)
  Pallas kernels  159 us (20%)
  matrix products  118 us (15%)
  local copies, waits for them, and re-layouts  92.2 us (12%)
  waiting for transfers between devices  73.2 us (9%)
  other arithmetic  30.5 us (4%)
  between operations  15.5 us (2%)
  starting transfers between devices  9.44 us (1%)
    all_gather x1, blocking collectives, body(): lax.all_gather(router_weight, ('dp', 'expert'), axis=0, tiled=True)  99.9 us
    pallas_call x1, Pallas kernels, attend_backward(): pl.pallas_call(functools.partial(backward_kernel, head_dim, reach), grid_...  85.6 us
    unnamed x2, blocking collectives  81 us
    pallas_call x1, Pallas kernels, attend_forward(): pl.pallas_call(functools.partial(forward_kernel, head_dim, reach), grid_s...  63.5 us
    all_to_all x1, blocking collectives, body(): lax.all_to_all(send_rows, 'expert', split_axis=0, concat_axis=1, tiled=True)  51.2 us
    all_to_all x1, blocking collectives, body(): lax.all_to_all(grad_send, 'expert', split_axis=0, concat_axis=1, tiled=True)  47 us
    unnamed x97, local copies, waits for them, and re-layouts  44.7 us
    all_to_all x1, waiting for transfers between devices, body(): lax.all_to_all(grad_rows_in, 'expert', split_axis=1, concat_axis=0, tiled...  42.9 us
  transfers between devices with their start and end apart: 8, of which 3 were waited for; matrix products, arithmetic and copies ran while one was open for 20% of the time, Pallas kernels for 20%

profile of v1, /device:TPU:0, one launch (start us, length us, event | category | flops | bytes accessed | tf_op | source)
XLA Modules:
  0.0 776.4 jit_solution(4265573589126546908)
XLA Ops:
  16.2 42.1 %all-reduce.8 = (bf16[768]{0:T(1024)(128)(2,1)S(1)}, bf16[768]{0:T(1024)(128)(2,1)S(1)}) all-reduce(bf16[768]{0:T(1024)(128)(2,1)S(1)} %dynamic-update-slice, bf16[768]{0:T(1024)(128)(2,1)S(1)} %dynamic-update-slice.1), channel_id=1, replica_groups=mesh['dp'=4,'expert'=8] {'dp','expert'}, use_global_device_ids=true, to_apply=%add.2 | all-reduce | flops 1536 | bytes 6144
  60.2 9.8 %toeplitz_tiles.1.bias_ref = f32[12,1408,128]{2,1,0:T(8,128)} custom-call(f32[12,11,256]{2,1,0:T(8,128)} %pad_maximum_fusion.1.window_ref), custom_call_target="tpu_custom_call" | custom-call | tf_op jit(solution)/shard_map/toeplitz_tiles/pallas_call | solution.py:80
  74.0 7.8 %convolution_convert_fusion.q_ref.k_ref.v_ref = bf16[1024,2304]{1,0:T(8,128)(2,1)} fusion(bf16[768,2304]{1,0:T(8,128)(2,1)} %all-gather.4.cloned.1.call-done, bf16[1,1024,768]{1,2,0:T(8,128)(2,1)S(1)} %copy.84, f32[768]{0:T(1024)S(1)} %convert_element_type.123, f32[1024]{0:T(1024)S(1)} %add_rsqrt_fusion.1), kind=kOutput, calls=%fused_computation.18 | convolution fusion | flops 3629383680 | bytes 9837568 | tf_op jit(solution)/shard_map/dot_general | solution.py:387
  81.8 63.5 %attend_forward.1 = (bf16[1024,768]{1,0:T(8,128)(2,1)S(1)}, f32[6,2,1024]{2,1,0:T(2,128)S(1)}) custom-call(s32[4]{0:T(128)S(1)} %get-tuple-element.100.low_ref, s32[4]{0:T(128)S(1)} %get-tuple-element.99.high_ref, bf16[1024,2304]{1,0:T(8,128)(2,1)} %convolution_convert_fusion.q_ref.k_ref.v_ref, bf16[1024,2304]{1,0:T(8,128)(2,1)} %convolution_convert_fusion.q_ref.k_ref.v_ref, ...), custom_call_target="tpu_custom_call" | custom-call | tf_op jit(solution)/shard_map/attend_forward/pallas_call | solution.py:288
  153.5 7.2 scatter_custom_fusion
  160.7 51.2 %all_to_all.16 = bf16[8,1,160,768]{3,2,1,0:T(8,128)(2,1)S(1)} all-to-all(bf16[8,1,160,768]{3,2,1,0:T(8,128)(2,1)} %bitcast.175), channel_id=1, replica_groups=mesh['dp'=4,'expert'=8] {'expert'}, dimensions={0} | all-to-all | bytes 3932160 | tf_op jit(solution)/shard_map/all_to_all | solution.py:411
  213.2 8.3 %fusion.19 = f32[8,160,3072]{2,1,0:T(8,128)S(1)} fusion(bf16[1,768,3072]{2,1,0:T(8,128)(2,1)} %param.26, bf16[8,1,160,768]{3,2,1,0:T(8,128)(2,1)S(1)} %all_to_all.16), kind=kOutput, calls=%fused_computation.39 | convolution fusion | flops 6039797760 | bytes 22413312 | tf_op jit(solution)/shard_map/escd,edf->escf/dot_general | solution.py:412
  227.0 10.5 %convert_bitcast_fusion.2 = bf16[1,8,160,768]{3,2,0,1:T(8,128)(2,1)} fusion(bf16[1,3072,768]{2,1,0:T(8,128)(2,1)S(1)} %bitcast.199, f32[8,160,3072]{2,1,0:T(8,128)S(1)} %fusion.19), kind=kOutput, calls=%fused_computation.74 | convolution fusion | flops 6076170240 | bytes 22413312 | tf_op jit(solution)/shard_map/escf,efd->escd/dot_general | solution.py:414
  242.0 99.9 %all-gather = bf16[32,24,8]{1,2,0:T(8,128)(2,1)S(1)} all-gather(bf16[1,24,8]{1,2,0:T(8,128)(2,1)S(1)} %bitcast.195), channel_id=1, replica_groups=mesh['dp'=4,'expert'=8] {'dp','expert'}, dimensions={0}, use_global_device_ids=true | all-gather | bytes 12672 | tf_op jit(solution)/shard_map/all_gather | solution.py:370
  345.1 7.4 gather_fusion
  361.5 7.2 scatter_custom_fusion.1
  368.8 47.0 %all_to_all.17 = bf16[8,1,160,768]{3,2,1,0:T(8,128)(2,1)S(1)} all-to-all(bf16[8,1,160,768]{3,2,1,0:T(8,128)(2,1)} %bitcast.174), channel_id=1, replica_groups=mesh['dp'=4,'expert'=8] {'expert'}, dimensions={0} | all-to-all | bytes 3932160 | tf_op jit(solution)/shard_map/all_to_all | solution.py:450
  417.0 13.3 %fusion.22 = bf16[1,3072,768]{2,1,0:T(8,128)(2,1)} fusion(bf16[8,1,160,768]{3,2,1,0:T(8,128)(2,1)S(1)} %all_to_all.17, f32[8,160,3072]{2,1,0:T(8,128)} %copy-done.33), kind=kOutput, calls=%fused_computation.42 | convolution fusion | flops 6077546496 | bytes 22413312 | tf_op jit(solution)/shard_map/escf,escd->efd/dot_general | solution.py:467
  430.4 21.3 %fusion.7 = bf16[8,160,3072]{2,1,0:T(8,128)(2,1)} fusion(f32[8,160,3072]{2,1,0:T(8,128)} %copy-done.33, bf16[1,3072,768]{2,1,0:T(8,128)(2,1)} %param.27, bf16[8,1,160,768]{3,2,1,0:T(8,128)(2,1)} %copy-done.18), kind=kOutput, calls=%fused_computation.13 | convolution fusion | flops 6114508800 | bytes 30277632 | tf_op jit(solution)/shard_map/escd,efd->escf/dot_general | solution.py:451
  451.7 11.1 %fusion.21 = bf16[1,768,3072]{2,1,0:T(8,128)(2,1)} fusion(bf16[8,160,3072]{2,1,0:T(8,128)(2,1)} %fusion.7, bf16[8,1,160,768]{3,2,1,0:T(8,128)(2,1)S(1)} %copy-done.17), kind=kOutput, calls=%fused_computation.41 | convolution fusion | flops 6042157056 | bytes 14548992 | tf_op jit(solution)/shard_map/escd,escf->edf/dot_general | solution.py:466
  462.9 11.1 %convert_bitcast_fusion.1 = bf16[1,8,160,768]{3,2,0,1:T(8,128)(2,1)} fusion(bf16[8,160,3072]{2,1,0:T(8,128)(2,1)} %fusion.7, bf16[1,768,3072]{2,1,0:T(8,128)(2,1)} %param.26), kind=kOutput, calls=%fused_computation.73 | convolution fusion | flops 6040780800 | bytes 14548992 | tf_op jit(solution)/shard_map/escf,edf->escd/dot_general | solution.py:455
  478.8 42.9 %all-to-all-done.3 = bf16[1,8,160,768]{3,2,0,1:T(8,128)(2,1)} async-done(((bf16[1,8,160,768]{3,2,0,1:T(8,128)(2,1)}), bf16[1,8,160,768]{3,2,0,1:T(8,128)(2,1)}, u32[]{:S(2)}, u32[]{:S(2)}) %all-to-all-start.3) | async-done | bytes 1966112 | tf_op jit(solution)/shard_map/all_to_all | solution.py:458
  521.7 7.4 gather_fusion.1
  548.4 85.6 %attend_backward.1 = (bf16[3,1024,768]{2,1,0:T(8,128)(2,1)}, f32[12,11,256]{2,1,0:T(8,128)}) custom-call(s32[4]{0:T(128)} %copy-done.7, s32[4]{0:T(128)} %copy-done.6, bf16[1024,2304]{1,0:T(8,128)(2,1)} %convolution_convert_fusion.q_ref.k_ref.v_ref, bf16[1024,2304]{1,0:T(8,128)(2,1)} %convolution_convert_fusion.q_ref.k_ref.v_ref, ...), custom_call_target="tpu_custom_call" | custom-call | tf_op jit(solution)/shard_map/attend_backward/pallas_call | solution.py:333
  644.0 8.0 %copy.113 = f32[768,2304]{1,0:T(8,128)} copy(f32[768,2304]{0,1:T(8,128)} %pad_maximum_fusion) | data formatting | bytes 14155776
  653.4 6.4 reverse.1
  671.3 10.8 %fusion.30 = (f32[768]{0:T(1024)S(1)}, f32[1024]{0:T(1024)S(1)}, f32[]{:T(128)}, f32[1024,768,1]{0,1,2:T(8,128)}) fusion(bf16[1,1024,768]{1,2,0:T(8,128)(2,1)S(1)} %copy-done.11, f32[1024]{0:T(1024)S(1)} %copy-done.28, f32[768]{0:T(1024)S(1)} %copy-done.26, f32[1024]{0:T(1024)S(1)} %bitcast.192, bf16[3,1024,768]{2,1,0:T(8,128)(2,1)} %get-tuple-element.18, ...), kind=kOutput, calls=%fused_computation.51 | convolution fusion | flops 3631741184 | bytes 12994564 | tf_op jit(solution)/shard_map/pte,dpe->td/dot_general | solution.py:509
  684.6 38.9 %all-reduce.7 = (f32[768]{0:T(1024)S(1)}, f32[768]{0:T(1024)S(1)}, f32[768,8]{0,1:T(8,128)S(1)}, f32[32,12]{0,1:T(8,128)}, f32[3]{0:T(128)S(1)}, /*index=5*/f32[]{:T(128)}) all-reduce(f32[768]{0:T(1024)S(1)} %get-tuple-element.66, f32[768]{0:T(1024)S(1)} %get-tuple-element.71, ...), channel_id=2, replica_groups=mesh['dp'=4,'expert'=8] {'dp','expert'}, use_global_device_ids=true, to_apply=%region_13.15.clone | all-reduce | flops 8068 | bytes 64544
  742.7 26.7 %reduce-scatter.14.cloned.1.call-done = f32[24,2304]{1,0:T(8,128)} async-done(((f32[768,2304]{1,0:T(8,128)}), f32[24,2304]{1,0:T(8,128)}) %reduce-scatter.14.cloned.1.call-update) | async-done | bytes 221200
  (179 shorter events, 115.7 us)
Async XLA Ops:
  7.2 66.8 %all-gather.4.cloned.1.call-start = ((), (), s32[]{:S(2)}) async-start(), calls=%async_computation.8 | async-start | bytes 3649536 | tf_op jit(solution)/shard_map/all_gather | solution.py:367
  7.9 138.0 %all-gather.6.cloned.1.call-start = ((), (), s32[]{:S(2)}) async-start(), calls=%async_computation.9 | async-start | bytes 1216512 | tf_op jit(solution)/shard_map/all_gather | solution.py:368
  58.2 15.7 %copy-start.25 = (f32[768]{0:T(1024)}, f32[768]{0:T(1024)S(1)}, u32[]{:S(2)}) copy-start(f32[768]{0:T(1024)S(1)} %convert_element_type.123) | copy-start | bytes 9220
  60.2 13.8 %copy-start.10 = (bf16[1,1024,768]{1,2,0:T(8,128)(2,1)}, bf16[1,1024,768]{1,2,0:T(8,128)(2,1)S(1)}, u32[]{:S(2)}) copy-start(bf16[1,1024,768]{1,2,0:T(8,128)(2,1)S(1)} %copy.84) | copy-start | bytes 4718596
  60.2 10.5 %copy-start.21 = (s32[1,1024]{1,0:T(1,128)S(1)}, s32[1,1024]{1,0:T(1,128)}, u32[]{:S(2)}) copy-start(s32[1,1024]{1,0:T(1,128)} %param.28) | copy-start | bytes 12292
  70.6 11.1 %copy-start.6 = (s32[4]{0:T(128)}, s32[4]{0:T(128)S(1)}, u32[]{:S(2)}) copy-start(s32[4]{0:T(128)S(1)} %get-tuple-element.99.high_ref) | copy-start | bytes 52
  70.6 11.1 %copy-start.7 = (s32[4]{0:T(128)}, s32[4]{0:T(128)S(1)}, u32[]{:S(2)}) copy-start(s32[4]{0:T(128)S(1)} %get-tuple-element.100.low_ref) | copy-start | bytes 52
  70.7 11.1 %copy-start.27 = (f32[1024]{0:T(1024)}, f32[1024]{0:T(1024)S(1)}, u32[]{:S(2)}) copy-start(f32[1024]{0:T(1024)S(1)} %add_rsqrt_fusion.1) | copy-start | bytes 12292
  145.9 393.1 %copy-start.4 = (bf16[1024,768]{1,0:T(8,128)(2,1)}, bf16[1024,768]{1,0:T(8,128)(2,1)S(1)}, u32[]{:S(2)}) copy-start(bf16[1024,768]{1,0:T(8,128)(2,1)S(1)} %get-tuple-element.16.mix_ref) | copy-start | bytes 4718596
  160.7 66.3 %slice-start = ((s8[4718592]{0:T(1024)(128)(4,1)}), s8[4194304]{0:T(1024)(128)(4,1)S(1)}, s32[]{:S(2)}) async-start(s8[4718592]{0:T(1024)(128)(4,1)} %bitcast.198), calls=%async_computation.14 | async-start | bytes 8388608
  213.2 13.8 %slice-start.1 = ((s8[4718592]{0:T(1024)(128)(4,1)}), s8[524288]{0:T(1024)(128)(4,1)S(1)}, s32[]{:S(2)}) async-start(s8[4718592]{0:T(1024)(128)(4,1)} %bitcast.198), calls=%async_computation.15 | async-start | bytes 1048576
  237.5 107.6 %all-to-all-start.1 = ((bf16[1,8,160,768]{3,2,0,1:T(8,128)(2,1)}), bf16[1,8,160,768]{3,2,0,1:T(8,128)(2,1)}, u32[]{:S(2)}, u32[]{:S(2)}) async-start(bf16[1,8,160,768]{3,2,0,1:T(8,128)(2,1)} %convert_bitcast_fusion.2), calls=%async_computation.1 | async-start | bytes 3932160 | tf_op jit(solution)/shard_map/all_to_all | solution.py:417
  241.9 495.1 %reduce-scatter.12.cloned.1.call-start = ((), (), s32[]{:S(2)}) async-start(), calls=%async_computation.12 | async-start | bytes 5898240 | tf_op jit(solution)/shard_map/reduce_scatter | solution.py:474
  430.3 309.6 %reduce-scatter.10.cloned.1.call-start = ((), (), s32[]{:S(2)}) async-start(), calls=%async_computation.11 | async-start | bytes 5898240 | tf_op jit(solution)/shard_map/reduce_scatter | solution.py:471
  430.4 21.4 %copy-start.17 = (bf16[8,1,160,768]{3,2,1,0:T(8,128)(2,1)S(1)}, bf16[8,1,160,768]{3,2,1,0:T(8,128)(2,1)}, u32[]{:S(2)}) copy-start(bf16[8,1,160,768]{3,2,1,0:T(8,128)(2,1)} %copy-done.16) | copy-start | bytes 5898244
  474.0 47.7 %all-to-all-start.3 = ((bf16[1,8,160,768]{3,2,0,1:T(8,128)(2,1)}), bf16[1,8,160,768]{3,2,0,1:T(8,128)(2,1)}, u32[]{:S(2)}, u32[]{:S(2)}) async-start(bf16[1,8,160,768]{3,2,0,1:T(8,128)(2,1)} %convert_bitcast_fusion.1), calls=%async_computation.3 | async-start | bytes 3932160 | tf_op jit(solution)/shard_map/all_to_all | solution.py:458
  478.4 264.4 %reduce-scatter.8.cloned.1.call-start = ((), (), s32[]{:S(2)}) async-start(), calls=%async_computation.10 | async-start | bytes 2433024 | tf_op jit(solution)/shard_map/reduce_scatter | solution.py:519
  543.6 225.8 %reduce-scatter.14.cloned.1.call-start = ((), (), s32[]{:S(2)}) async-start(), calls=%async_computation.13 | async-start | bytes 7299072
  548.4 85.6 %copy-start.11 = (bf16[1,1024,768]{1,2,0:T(8,128)(2,1)S(1)}, bf16[1,1024,768]{1,2,0:T(8,128)(2,1)}, u32[]{:S(2)}) copy-start(bf16[1,1024,768]{1,2,0:T(8,128)(2,1)} %copy-done.10) | copy-start | bytes 4718596
  548.4 85.6 %copy-start.26 = (f32[768]{0:T(1024)S(1)}, f32[768]{0:T(1024)}, u32[]{:S(2)}) copy-start(f32[768]{0:T(1024)} %copy-done.25) | copy-start | bytes 9220
  548.4 85.6 %copy-start.28 = (f32[1024]{0:T(1024)S(1)}, f32[1024]{0:T(1024)}, u32[]{:S(2)}) copy-start(f32[1024]{0:T(1024)} %copy-done.27) | copy-start | bytes 12292
  671.3 12.8 %copy-start.19 = (f32[32,11,128]{2,0,1:T(8,128)S(1)}, f32[32,11,128]{2,0,1:T(8,128)}, u32[]{:S(2)}) copy-start(f32[32,11,128]{2,0,1:T(8,128)} %rev.22) | copy-start | bytes 540676
  671.3 12.8 %copy-start.20 = (f32[12,11,256]{2,1,0:T(8,128)S(1)}, f32[12,11,256]{2,1,0:T(8,128)}, u32[]{:S(2)}) copy-start(f32[12,11,256]{2,1,0:T(8,128)} %get-tuple-element.19) | copy-start | bytes 405508
  736.5 32.9 %copy-start.1 = (f32[32,12]{0,1:T(8,128)S(1)}, f32[32,12]{0,1:T(8,128)}, u32[]{:S(2)}) copy-start(f32[32,12]{0,1:T(8,128)} %param.25) | copy-start | bytes 4612
  (20 other events, 97.3 us)
Sparse Core Ops, SparseCore 0:
  10.9 62.9 all-gather.3
  76.9 53.1 all-gather.5
  430.4 45.9 reduce-scatter.11
  479.0 47.8 reduce-scatter.9
  543.7 97.5 reduce-scatter.7
  652.2 117.1 reduce-scatter.13

commit v2 on v1

v2 whole, which is shorter than its diff:
```python
import functools

import jax
import jax.numpy as jnp
from jax import lax
from jax.experimental import pallas as pl
from jax.experimental.pallas import tpu as pltpu
from jax.sharding import PartitionSpec as P

MASK_STEP = 1e30
ROWS = 256
LANES = 128
STEP_HEADS = 4
SMALL_GAINS = 2
bf16, f32 = jnp.bfloat16, jnp.float32
NT = (((1,), (1,)), ((), ()))
NN = (((1,), (0,)), ((), ()))
TN = (((0,), (0,)), ((), ()))


def dot(left, right, dims):
    return lax.dot_general(left, right, dims, preferred_element_type=f32)


def bias_windows(values, reach):
    heads, offsets = values.shape
    chunks = (offsets + 1) // LANES
    turned = jnp.pad(values[:, ::-1], ((0, 0), (1, 0))).reshape(heads, chunks, LANES)
    middle = chunks // 2
    groups = list(range(-reach, reach + 1))
    first = [middle - g for g in groups]
    here = turned[:, first[-1] : first[0] + 1][:, ::-1]
    before = turned[:, first[-1] - 1 : first[0]][:, ::-1]
    return jnp.concatenate([here, before], axis=2)


def toeplitz_kernel(reach, window_ref, tile_ref):
    for g in range(2 * reach + 1):
        row = window_ref[0, g : g + 1, :]
        full = jnp.broadcast_to(row, (LANES, 2 * LANES))
        turned = pltpu.roll(full, 0, 1, stride=1, stride_axis=0)
        tile_ref[0, g * LANES : (g + 1) * LANES, :] = turned[:, :LANES]


def toeplitz_tiles(windows):
    heads, groups, width = windows.shape
    return pl.pallas_call(
        functools.partial(toeplitz_kernel, groups // 2),
        grid=(heads,),
        in_specs=[pl.BlockSpec((1, groups, width), lambda n: (n, 0, 0))],
        out_specs=pl.BlockSpec((1, groups * LANES, LANES), lambda n: (n, 0, 0)),
        out_shape=jax.ShapeDtypeStruct((heads, groups * LANES, LANES), f32),
        name="toeplitz_tiles",
    )(windows)


def head_lanes(rows, head, head_dim):
    lane = lax.broadcasted_iota(jnp.int32, rows.shape, 1)
    return jnp.where((lane >= head * head_dim) & (lane < (head + 1) * head_dim), rows, jnp.zeros_like(rows))


def head_rows(columns, head, head_dim):
    row = lax.broadcasted_iota(jnp.int32, columns.shape, 0)
    return jnp.where((row >= head * head_dim) & (row < (head + 1) * head_dim), columns, jnp.zeros_like(columns))


def bias_tile(bias_ref, head, offset):
    parts = [
        bias_ref[head, pl.ds(pl.multiple_of(offset - LANES * part, LANES), ROWS), :]
        for part in range(ROWS // LANES)
    ]
    return jnp.concatenate(parts, axis=1)


def forward_kernel(head_dim, reach, low_ref, high_ref, q_ref, k_ref, v_ref, qx_ref, kx_ref, bias_ref, unused_ref, mix_ref, lse_ref, vt_ref):
    length, width = q_ref.shape
    heads = width // head_dim
    scale = head_dim ** (-0.5)
    for c in range(width // LANES):
        vt_ref[c * LANES : (c + 1) * LANES, :] = v_ref[:, c * LANES : (c + 1) * LANES].T
    per = LANES // head_dim

    def one_block(qb, unused):
        first = pl.multiple_of(qb * ROWS, ROWS)
        qx = qx_ref[:, pl.ds(first, ROWS)]
        queries = []
        for c in range(width // LANES):
            pair = (q_ref[pl.ds(first, ROWS), c * LANES : (c + 1) * LANES] * jnp.asarray(scale, bf16)).T
            queries += [jnp.concatenate([head_rows(pair, h, head_dim), qx], axis=0) for h in range(per)]

        def one_tile(kb, carry):
            keys_at = pl.multiple_of(kb * ROWS, ROWS)
            offset = pl.multiple_of(keys_at - first + LANES * reach, LANES)
            kx = kx_ref[pl.ds(keys_at, ROWS), :]
            out = []
            all_scores = []
            for h in range(heads):
                c = h // per
                keys = jnp.concatenate([k_ref[pl.ds(keys_at, ROWS), c * LANES : (c + 1) * LANES], kx], axis=1)
                all_scores.append(dot(keys, queries[h], NN))
            soft = []
            for h in range(heads):
                peak, total, mixed = carry[h]
                scores = all_scores[h] + bias_tile(bias_ref, h, offset)
                new_peak = jnp.maximum(peak, jnp.max(scores, axis=0, keepdims=True))
                weights = jnp.exp(scores - new_peak)
                shrink = jnp.exp(peak - new_peak)
                total = total * shrink + jnp.sum(weights, axis=0, keepdims=True)
                soft.append((new_peak, total, shrink, weights.astype(bf16)))
            for h in range(heads):
                new_peak, total, shrink, weights = soft[h]
                values = vt_ref[h * head_dim : (h + 1) * head_dim, pl.ds(keys_at, ROWS)]
                mixed = carry[h][2] * shrink + dot(values, weights, NN)
                out.append((new_peak, total, mixed))
            return tuple(out)

        start = tuple(
            (jnp.full((1, ROWS), -3e38, f32), jnp.zeros((1, ROWS), f32), jnp.zeros((head_dim, ROWS), f32))
            for h in range(heads)
        )
        done = lax.fori_loop(low_ref[qb], high_ref[qb], one_tile, start)
        for c in range(width // LANES):
            rows = jnp.concatenate([done[h][2] / done[h][1] for h in range(c * per, (c + 1) * per)], axis=0)
            mix_ref[pl.ds(first, ROWS), c * LANES : (c + 1) * LANES] = rows.T.astype(bf16)
        for h in range(heads):
            lse_ref[0, h : h + 1, pl.ds(first, ROWS)] = done[h][0] + jnp.log(done[h][1])
        return unused

    lax.fori_loop(0, length // ROWS, one_block, 0)


def diagonal_sums(tiles):
    groups = tiles.shape[0]
    step = LANES // 2
    zero = jnp.zeros((groups, step, LANES), f32)
    turned = jnp.concatenate([tiles[:, :step], zero], axis=2) + pltpu.roll(
        jnp.concatenate([tiles[:, step:], zero], axis=2), 2 * LANES - step, 2
    )
    while step > 8:
        step //= 2
        turned = turned[:, :step] + pltpu.roll(turned[:, step:], 2 * LANES - step, 2)
    while step > 1:
        step //= 2
        turned = turned + pltpu.roll(pltpu.roll(turned, 2 * LANES - step, 2), 8 - step, 1)
    return turned[:, 0]


def backward_kernel(head_dim, reach, low_ref, high_ref, q_ref, k_ref, v_ref, dmix_ref, mix_ref, qx_ref, kx_ref, bias_ref, lse_ref,
                    grad_ref, diag_ref, kt_ref, dk_ref, dv_ref, along_ref):
    length, width = q_ref.shape
    heads = width // head_dim
    scale = head_dim ** (-0.5)
    per = LANES // head_dim
    for c in range(width // LANES):
        kt_ref[c * LANES : (c + 1) * LANES, :] = k_ref[:, c * LANES : (c + 1) * LANES].T
    dk_ref[...] = jnp.zeros_like(dk_ref)
    dv_ref[...] = jnp.zeros_like(dv_ref)
    along_ref[...] = jnp.zeros_like(along_ref)

    def one_block(qb, unused):
        first = pl.multiple_of(qb * ROWS, ROWS)
        qx = qx_ref[:, pl.ds(first, ROWS)]
        queries, d_mixes, deltas, wide, d_turned = [], [], [], [], []
        for c in range(width // LANES):
            lanes = slice(c * LANES, (c + 1) * LANES)
            query = q_ref[pl.ds(first, ROWS), lanes] * jnp.asarray(scale, bf16)
            d_mix = dmix_ref[pl.ds(first, ROWS), lanes]
            product = (d_mix.astype(f32) * mix_ref[pl.ds(first, ROWS), lanes].astype(f32)).T
            query_turned, d_mix_turned = query.T, d_mix.T
            for h in range(per):
                queries.append(head_lanes(query, h, head_dim))
                d_mixes.append(head_lanes(d_mix, h, head_dim))
                wide.append(jnp.concatenate([head_rows(query_turned, h, head_dim), qx], axis=0))
                d_turned.append(head_rows(d_mix_turned, h, head_dim))
                deltas.append(jnp.sum(product[h * head_dim : (h + 1) * head_dim], axis=0, keepdims=True))
        lses = [lse_ref[0, h : h + 1, pl.ds(first, ROWS)] for h in range(heads)]

        def one_tile(kb, carry):
            keys_at = pl.multiple_of(kb * ROWS, ROWS)
            offset = pl.multiple_of(keys_at - first + LANES * reach, LANES)
            kx = kx_ref[pl.ds(keys_at, ROWS), :]
            out = []
            low_weights, low_scores, all_scores, all_weights = [], [], [], []
            for h in range(heads):
                lanes = slice(h // per * LANES, (h // per + 1) * LANES)
                keys = jnp.concatenate([k_ref[pl.ds(keys_at, ROWS), lanes], kx], axis=1)
                all_scores.append(dot(keys, wide[h], NN))
            for h in range(heads):
                lanes = slice(h // per * LANES, (h // per + 1) * LANES)
                all_weights.append(dot(v_ref[pl.ds(keys_at, ROWS), lanes], d_turned[h], NN))
            for h in range(heads):
                weights = jnp.exp(all_scores[h] + bias_tile(bias_ref, h, offset) - lses[h])
                d_scores = weights * (all_weights[h] - deltas[h])
                for part in range(ROWS // LANES):
                    at = pl.ds(pl.multiple_of(offset - LANES * part, LANES), ROWS)
                    along_ref[h, at, :] += d_scores[:, part * LANES : (part + 1) * LANES]
                low_weights.append(weights.astype(bf16))
                low_scores.append(d_scores.astype(bf16))
            for h in range(heads):
                keys_turned = kt_ref[h * head_dim : (h + 1) * head_dim, pl.ds(keys_at, ROWS)]
                out.append(carry[h] + dot(keys_turned, low_scores[h], NN))
            for c in range(width // LANES):
                mine = range(c * per, (c + 1) * per)
                lanes = slice(c * LANES, (c + 1) * LANES)
                dv_ref[pl.ds(keys_at, ROWS), lanes] += dot(
                    jnp.concatenate([low_weights[h] for h in mine], axis=1), jnp.concatenate([d_mixes[h] for h in mine], axis=0), NN)
                dk_ref[pl.ds(keys_at, ROWS), lanes] += dot(
                    jnp.concatenate([low_scores[h] for h in mine], axis=1), jnp.concatenate([queries[h] for h in mine], axis=0), NN)
            return tuple(out)

        start = tuple(jnp.zeros((head_dim, ROWS), f32) for h in range(heads))
        done = lax.fori_loop(low_ref[qb], high_ref[qb], one_tile, start)
        for c in range(width // LANES):
            rows = jnp.concatenate([done[h] for h in range(c * per, (c + 1) * per)], axis=0) * scale
            grad_ref[pl.ds(first, ROWS), c * LANES : (c + 1) * LANES] = rows.T.astype(bf16)
        return unused

    lax.fori_loop(0, length // ROWS, one_block, 0)
    grad_ref[:, width : 2 * width] = dk_ref[...].astype(bf16)
    grad_ref[:, 2 * width :] = dv_ref[...].astype(bf16)
    for h in range(heads):
        diag_ref[h] = diagonal_sums(along_ref[h].reshape(2 * reach + 1, LANES, LANES))


def tile_bounds(segments):
    length = segments.shape[0]
    blocks = segments.reshape(length // ROWS, ROWS)
    starts = jnp.sum((segments[None, :] < blocks[:, :1]).astype(jnp.int32), axis=1)
    ends = jnp.sum((segments[None, :] <= blocks[:, -1:]).astype(jnp.int32), axis=1)
    return starts // ROWS, (ends + ROWS - 1) // ROWS


def mask_columns(segments, validity, segment_count=8):
    length = segments.shape[0]
    short = 1
    while short * (short + 1) < length:
        short += 1
    at = jnp.arange(length, dtype=jnp.int32)
    lane = jnp.arange(LANES, dtype=jnp.int32)[None, :]
    in_first = (lane >= segment_count) & (lane < segment_count + short)
    in_second = (lane >= segment_count + short) & (lane < segment_count + 2 * short + 1)
    mine = (
        (lane == segments[:, None])
        | (in_first & (lane - segment_count == (at % short)[:, None]))
        | (in_second & (lane - segment_count - short == (at % (short + 1))[:, None]))
    )
    used = lane < segment_count + 2 * short + 1
    query_side = jnp.where(used & ~mine, -MASK_STEP, 0.0).astype(bf16).T
    real = (validity == 1)[:, None]
    key_side = jnp.where(mine & jnp.where(real, lane < segment_count, lane >= segment_count), 1.0, 0.0).astype(bf16)
    return query_side, key_side


def attend_forward(packed, query_side, key_side, bounds, tiles, mixed, first, head_dim):
    length = packed.shape[0]
    width = STEP_HEADS * head_dim
    steps = packed.shape[1] // 3 // width
    reach = tiles.shape[1] // LANES // 2
    whole = lambda *_: (0, 0)
    grid_spec = pltpu.PrefetchScalarGridSpec(
        num_scalar_prefetch=2,
        grid=(steps,),
        in_specs=[
            pl.BlockSpec((length, width), lambda p, *_: (0, 3 * p)),
            pl.BlockSpec((length, width), lambda p, *_: (0, 3 * p + 1)),
            pl.BlockSpec((length, width), lambda p, *_: (0, 3 * p + 2)),
            pl.BlockSpec((LANES, length), whole),
            pl.BlockSpec((length, LANES), whole),
            pl.BlockSpec((STEP_HEADS, tiles.shape[1], LANES), lambda p, *_: (first + p, 0, 0)),
            pl.BlockSpec(memory_space=pl.ANY),
        ],
        out_specs=[
            pl.BlockSpec((length, width), lambda p, *_: (0, first + p)),
            pl.BlockSpec((1, STEP_HEADS, length), lambda p, *_: (p, 0, 0)),
        ],
        scratch_shapes=[pltpu.VMEM((width, length), bf16)],
    )
    work = steps * STEP_HEADS * length * length
    return pl.pallas_call(
        functools.partial(forward_kernel, head_dim, reach),
        grid_spec=grid_spec,
        out_shape=[
            jax.ShapeDtypeStruct(mixed.shape, bf16),
            jax.ShapeDtypeStruct((steps, STEP_HEADS, length), f32),
        ],
        input_output_aliases={8: 0},
        compiler_params=pltpu.CompilerParams(vmem_limit_bytes=40 * 2**20),
        cost_estimate=pl.CostEstimate(flops=32 * work * head_dim, bytes_accessed=steps * 36 * 2**20, transcendentals=work),
        name="attend_forward",
    )(*bounds, packed, packed, packed, query_side, key_side, tiles, mixed)


def attend_backward(packed, d_mix, mix, lse, query_side, key_side, bounds, tiles, first, head_dim):
    length = packed.shape[0]
    width = STEP_HEADS * head_dim
    steps = packed.shape[1] // 3 // width
    reach = tiles.shape[1] // LANES // 2
    groups = 2 * reach + 1
    whole = lambda *_: (0, 0)
    grid_spec = pltpu.PrefetchScalarGridSpec(
        num_scalar_prefetch=2,
        grid=(steps,),
        in_specs=[
            pl.BlockSpec((length, width), lambda p, *_: (0, 3 * p)),
            pl.BlockSpec((length, width), lambda p, *_: (0, 3 * p + 1)),
            pl.BlockSpec((length, width), lambda p, *_: (0, 3 * p + 2)),
            pl.BlockSpec((length, width), lambda p, *_: (0, first + p)),
            pl.BlockSpec((length, width), lambda p, *_: (0, first + p)),
            pl.BlockSpec((LANES, length), whole),
            pl.BlockSpec((length, LANES), whole),
            pl.BlockSpec((STEP_HEADS, tiles.shape[1], LANES), lambda p, *_: (first + p, 0, 0)),
            pl.BlockSpec((1, STEP_HEADS, length), lambda p, *_: (p, 0, 0)),
        ],
        out_specs=[
            pl.BlockSpec((length, 3 * width), lambda p, *_: (0, p)),
            pl.BlockSpec((STEP_HEADS, groups, 2 * LANES), lambda p, *_: (p, 0, 0)),
        ],
        scratch_shapes=[
            pltpu.VMEM((width, length), bf16),
            pltpu.VMEM((length, width), f32),
            pltpu.VMEM((length, width), f32),
            pltpu.VMEM((STEP_HEADS, groups * LANES, LANES), f32),
        ],
    )
    work = steps * STEP_HEADS * length * length
    return pl.pallas_call(
        functools.partial(backward_kernel, head_dim, reach),
        grid_spec=grid_spec,
        out_shape=[
            jax.ShapeDtypeStruct((length, 3 * width * steps), bf16),
            jax.ShapeDtypeStruct((steps * STEP_HEADS, groups, 2 * LANES), f32),
        ],
        compiler_params=pltpu.CompilerParams(vmem_limit_bytes=52 * 2**20),
        cost_estimate=pl.CostEstimate(flops=80 * work * head_dim, bytes_accessed=steps * 72 * 2**20, transcendentals=work),
        name="attend_backward",
    )(*bounds, packed, packed, packed, d_mix, mix, query_side, key_side, tiles, lse)


def spread_kernel(groups, width, weight_ref, first_ref, second_ref, router_ref, *outs):
    receivers, count = outs[0].shape[:2]
    steps = weight_ref.shape[1] // (3 * width)
    for (first, many), out_ref in zip(groups, outs):
        for p in range(many):
            for part in range(3):
                at = (part * steps + first + p) * width
                rows = weight_ref[:, at : at + width]
                to = (3 * p + part) * width
                out_ref[:, :, to : to + width] = jnp.broadcast_to(rows[None], (receivers, *rows.shape))
    row = lax.broadcasted_iota(jnp.int32, (count, count), 0)
    same = row == lax.broadcasted_iota(jnp.int32, (count, count), 1)
    columns = [
        jnp.sum(jnp.where(same, jnp.broadcast_to(ref[...].astype(f32), same.shape), 0.0), axis=1, keepdims=True)
        for ref in (first_ref, second_ref)
    ]
    columns.append(router_ref[...].astype(f32))
    used = SMALL_GAINS + router_ref.shape[1]
    columns.append(jnp.zeros((count, -used % LANES), f32))
    rows = jnp.concatenate(columns, axis=1).astype(bf16)
    outs[0][:, :, 3 * groups[0][1] * width :] = jnp.broadcast_to(rows[None], (receivers, *rows.shape))


def spread_shard(weight, first_gain, second_gain, router, groups, width, receivers):
    rows = weight.shape[0]
    small = SMALL_GAINS + router.shape[1]
    small += -small % LANES
    widths = [3 * many * width + (0 if first else small) for first, many in groups]
    return pl.pallas_call(
        functools.partial(spread_kernel, groups, width),
        out_shape=[jax.ShapeDtypeStruct((receivers, rows, columns), bf16) for columns in widths],
        name="spread_shard",
    )(weight, first_gain.reshape(1, rows), second_gain.reshape(1, rows), router)


def expert_kernel(experts, me_ref, rows_ref, in_ref, small_ref, d_hidden_ref, hidden_ref, d_pre_ref, d_rows_ref, d_logits_ref, gate_ref,
                  probs_ref, total_ref, d_gate_ref):
    step = pl.program_id(0)
    lane = lax.broadcasted_iota(jnp.int32, probs_ref.shape, 1)
    chosen = lane == me_ref[0] + SMALL_GAINS

    @pl.when(step == 0)
    def _():
        logits = dot(rows_ref[...], small_ref[...], NN)
        logits = jnp.where((lane >= SMALL_GAINS) & (lane < SMALL_GAINS + experts), logits, -MASK_STEP)
        raised = jnp.exp(logits - jnp.max(logits, axis=1, keepdims=True))
        probs = raised / jnp.sum(raised, axis=1, keepdims=True)
        probs_ref[...] = probs
        gate_ref[...] = jnp.sum(jnp.where(chosen, probs, 0.0), axis=1, keepdims=True)
        total_ref[...] = jnp.zeros_like(total_ref)
        d_gate_ref[...] = jnp.zeros_like(d_gate_ref)

    count = rows_ref.shape[0]
    chunk = 256 if count % 256 == 0 else count
    weights = in_ref[...]
    pres = [dot(rows_ref[at : at + chunk], weights, NN) for at in range(0, count, chunk)]
    lows = []
    for i, at in enumerate(range(0, count, chunk)):
        here = slice(at, at + chunk)
        unit, slope = gelu_and_slope(pres[i])
        hidden = unit.astype(bf16)
        d_hidden = d_hidden_ref[here].astype(f32)
        hidden_ref[here] = hidden
        d_gate_ref[here] += jnp.sum(unit * d_hidden, axis=1, keepdims=True)
        low = (gate_ref[here] * d_hidden * slope).astype(bf16)
        d_pre_ref[here] = low
        lows.append(low)
    for i, at in enumerate(range(0, count, chunk)):
        total_ref[at : at + chunk] += dot(lows[i], weights, NT)

    @pl.when(step == pl.num_programs(0) - 1)
    def _():
        d_logits = (probs_ref[...] * (chosen.astype(f32) - gate_ref[...]) * d_gate_ref[...]).astype(bf16)
        d_logits_ref[...] = d_logits
        d_rows_ref[...] = (total_ref[...] + dot(d_logits, small_ref[...], NT)).astype(bf16)


def run_expert(me, rows, w_in, small, d_hidden, experts):
    count, width = rows.shape
    hidden_width = w_in.shape[1]
    block = 512
    row_blocks = pl.BlockSpec((count, block), lambda f, *_: (0, f))
    whole = lambda f, *_: (0, 0)
    grid_spec = pltpu.PrefetchScalarGridSpec(
        num_scalar_prefetch=1,
        grid=(hidden_width // block,),
        in_specs=[
            pl.BlockSpec((count, width), whole),
            pl.BlockSpec((width, block), lambda f, *_: (0, f)),
            pl.BlockSpec(small.shape, whole),
            row_blocks,
        ],
        out_specs=[
            row_blocks,
            row_blocks,
            pl.BlockSpec((count, width), whole),
            pl.BlockSpec((count, LANES), whole),
            pl.BlockSpec((count, 1), whole),
        ],
        scratch_shapes=[pltpu.VMEM((count, LANES), f32), pltpu.VMEM((count, width), f32), pltpu.VMEM((count, 1), f32)],
    )
    return pl.pallas_call(
        functools.partial(expert_kernel, experts),
        grid_spec=grid_spec,
        out_shape=[
            jax.ShapeDtypeStruct((count, hidden_width), bf16),
            jax.ShapeDtypeStruct((count, hidden_width), bf16),
            jax.ShapeDtypeStruct((count, width), bf16),
            jax.ShapeDtypeStruct((count, LANES), bf16),
            jax.ShapeDtypeStruct((count, 1), f32),
        ],
        compiler_params=pltpu.CompilerParams(vmem_limit_bytes=48 * 2**20),
        cost_estimate=pl.CostEstimate(
            flops=4 * count * width * hidden_width, bytes_accessed=30 * 2**20, transcendentals=count * hidden_width
        ),
        name="run_expert",
    )(me.reshape(1), rows, w_in, small, d_hidden)


EPSILON = 1e-06
HIGHEST = lax.Precision.HIGHEST
SEGMENT_LIMIT = 512
REACH = (SEGMENT_LIMIT + ROWS - LANES) // LANES


def norm_factor(values):
    return lax.rsqrt(jnp.mean(values * values, axis=-1, keepdims=True) + EPSILON)


def distances(axis):
    return [1 << i for i in reversed(range(lax.axis_size(axis).bit_length() - 1))]


def exchange(rows, axis, distance):
    return lax.ppermute(rows, axis, [(i, i ^ distance) for i in range(lax.axis_size(axis))])


def is_high(axis, distance):
    return (lax.axis_index(axis) & distance) != 0


def swap_blocks(blocks):
    return lax.all_to_all(blocks, "expert", split_axis=0, concat_axis=0, tiled=True)


def after(value, *earlier):
    return lax.optimization_barrier((value, *earlier))[0]


def gather_rows(near):
    block = near[None]
    for distance in distances("dp"):
        other = exchange(block, "dp", distance)
        high = is_high("dp", distance)
        block = jnp.stack([jnp.where(high, other, block), jnp.where(high, block, other)], axis=1)
        block = block.reshape(-1, *near.shape)
    return block.reshape(-1, near.shape[-1])


def near_shards(shard):
    count = lax.axis_size("expert")
    return swap_blocks(jnp.broadcast_to(shard[None], (count, *shard.shape)))


def scatter_dp(rows):
    width = rows.shape[1]
    block = rows.reshape(lax.axis_size("dp"), -1, width)
    for distance in distances("dp")[::-1]:
        halves = block.reshape(block.shape[0] // 2, 2, -1, width)
        high = is_high("dp", distance).astype(jnp.int32)
        keep = lax.dynamic_index_in_dim(halves, high, 1, keepdims=False)
        send = lax.dynamic_index_in_dim(halves, 1 - high, 1, keepdims=False)
        block = keep + exchange(send.astype(bf16), "dp", distance).astype(f32)
    return block[0].astype(bf16)


def scatter_near(rows):
    parts = swap_blocks(rows.reshape(lax.axis_size("expert"), -1, rows.shape[1]))
    return jnp.sum(parts.astype(f32), axis=0)


def sum_all(rows):
    for axis in ("dp", "expert"):
        for distance in distances(axis)[::-1]:
            rows = rows + exchange(rows, axis, distance)
    return rows


def gelu_and_slope(values):
    root = 0.7978845608028654
    square = values * values
    share = 0.5 + 0.5 * jnp.tanh(values * (root + root * 0.044715 * square))
    unit = values * share
    slope = share + 2.0 * unit * (1.0 - share) * (root + 3.0 * root * 0.044715 * square)
    return unit, slope


def body(
    inputs,
    cotangent,
    attn_gain,
    qkv_weight,
    out_weight,
    ffn_gain,
    router_weight,
    rel_bias,
    expert_in,
    expert_out,
    routes,
    positions,
    dropped,
    segment_ids,
    valid_mask,
    buckets,
):
    seq_count, seq_length, model_width = inputs.shape
    tokens = seq_count * seq_length
    bucket_count, head_count = rel_bias.shape
    head_dim = model_width // head_count
    experts = router_weight.shape[1]
    capacity = 5 * tokens // (4 * experts)
    slots = experts * capacity
    me = lax.axis_index("expert")

    width = STEP_HEADS * head_dim
    steps = head_count // STEP_HEADS
    groups = [(0, steps - 1), (steps - 1, 1)]
    one_hot_buckets = (buckets[:, None] == jnp.arange(bucket_count, dtype=jnp.int32)[None, :]).astype(f32)
    head_bias = jnp.dot(one_hot_buckets, rel_bias, precision=HIGHEST, preferred_element_type=f32).T
    tiles = toeplitz_tiles(bias_windows(head_bias, REACH))
    one_hot_windows = bias_windows(one_hot_buckets.T, REACH)
    all_masks = [mask_columns(segment_ids[seq], valid_mask[seq]) for seq in range(seq_count)]
    near = []
    for blocks in spread_shard(
        qkv_weight, attn_gain, ffn_gain, router_weight, groups, width, lax.axis_size("expert")
    ):
        near.append(swap_blocks(after(blocks, *near[-1:])))
    near[0], tiles, all_masks = lax.optimization_barrier((near[0], tiles, all_masks))
    gathered = [gather_rows(block) for block in near]
    w_out = lax.all_gather(out_weight, ("dp", "expert"), axis=0, tiled=True)
    w_groups = [gathered[g][:, : 3 * many * width] for g, (first, many) in enumerate(groups)]
    small_all = gathered[0][:, w_groups[0].shape[1] :]
    gain_one = small_all[:, 0].astype(f32)
    gain_two = small_all[:, 1].astype(f32)

    slot_index = jnp.where(
        dropped.reshape(tokens) == 1, slots, routes.reshape(tokens) * capacity + positions.reshape(tokens)
    )
    place = (jnp.arange(slots, dtype=jnp.int32)[:, None] == slot_index[None, :]).astype(bf16)

    def fill_slots(rows):
        return jnp.dot(place, rows, preferred_element_type=f32).astype(bf16)

    def send_slots(rows):
        return swap_blocks(rows.reshape(experts, capacity, model_width)).reshape(slots, model_width)

    def read_slots(rows):
        return lax.dot_general(place, rows, (((0,), (0,)), ((), ())), preferred_element_type=f32)

    layer_in = inputs.astype(f32)

    saved = []
    for seq in range(seq_count):
        factor = norm_factor(layer_in[seq])
        normed = (layer_in[seq] * factor * gain_one).astype(bf16)
        masks = all_masks[seq]
        bounds = tile_bounds(segment_ids[seq])
        packs, lses = [], []
        mixed = jnp.zeros((seq_length, model_width), bf16)
        for g, (first, many) in enumerate(groups):
            packed = jnp.dot(normed, w_groups[g], preferred_element_type=f32).astype(bf16)
            mixed, lse = attend_forward(packed, *masks, bounds, tiles, mixed, first, head_dim)
            packs.append(packed)
            lses.append(lse)
        attn_out = jnp.dot(mixed, w_out, preferred_element_type=f32)
        saved.append((factor, normed, masks, bounds, packs, lses, mixed, attn_out))
    d_final_rows = send_slots(fill_slots(after(cotangent.reshape(tokens, model_width), saved[0][5][0], near[-1])))
    mid_rows = (layer_in + jnp.stack([state[-1] for state in saved])).reshape(tokens, model_width)
    mid_factor = norm_factor(mid_rows)
    mid_normed = mid_rows * mid_factor
    ffn_normed = (mid_normed * gain_two).astype(bf16)
    filled = fill_slots(ffn_normed)
    slot_rows = send_slots(filled)

    w_in, w_back = expert_in[0], expert_out[0]
    d_hidden = dot(after(d_final_rows, filled), w_back, NT).astype(bf16)
    slot_rows, d_hidden = lax.optimization_barrier((slot_rows, d_hidden))
    hidden, d_pre, d_rows, d_logits, gate = run_expert(me, slot_rows, w_in, small_all, d_hidden, experts)
    d_returned = send_slots(d_rows)

    moe_rows = (gate * dot(hidden, w_back, NN)).astype(bf16)
    d_slot_out = (gate * d_final_rows.astype(f32)).astype(bf16)
    grad_router = dot(slot_rows, d_logits, TN)[:, SMALL_GAINS : SMALL_GAINS + experts]
    part_in = dot(slot_rows, d_pre, TN).astype(bf16)
    part_out = dot(hidden, d_slot_out, TN).astype(bf16)
    grad_expert_in = lax.psum_scatter(part_in, "dp", scatter_dimension=1, tiled=True).astype(f32)[None]
    grad_expert_out = lax.psum_scatter(part_out, "dp", scatter_dimension=0, tiled=True).astype(f32)[None]
    d_returned, moe_rows, part_in, part_out = lax.optimization_barrier((d_returned, moe_rows, part_in, part_out))
    d_normed = read_slots(d_returned)
    moe_returned = send_slots(moe_rows)
    moe = read_slots(moe_returned)

    final_rows = mid_rows + moe
    output = final_rows.astype(bf16).reshape(inputs.shape)
    live_rows = valid_mask.reshape(tokens, 1).astype(f32)
    flat_in = layer_in.reshape(tokens, model_width)
    sums = jnp.stack(
        [jnp.sum(live_rows * rows * rows) for rows in (flat_in, mid_rows, final_rows)] + [jnp.sum(live_rows)]
    )

    weighted = d_normed * gain_two
    grad_gain_two = jnp.sum(d_normed * mid_normed, axis=0)
    d_mid = cotangent.astype(f32).reshape(tokens, model_width) + mid_factor * (
        weighted - mid_normed * jnp.mean(weighted * mid_normed, axis=-1, keepdims=True)
    )
    d_attn = d_mid.astype(bf16)
    d_mixed = dot(d_attn, w_out, NT).astype(bf16)
    mixed_all = jnp.concatenate([state[6] for state in saved], axis=0)
    grad_out = dot(mixed_all, d_attn, TN)
    out_half = scatter_dp(grad_out)

    diagonals, grad_groups, halves, dense_qkv = [], [], [], []
    d_normed_one = [jnp.zeros((seq_length, model_width), f32)] * seq_count
    for g, (first, many) in enumerate(groups):
        if g:
            d_mixed, out_half, moe_returned = lax.optimization_barrier((d_mixed, out_half, moe_returned))
            dense_out = scatter_near(out_half)
        grad_group, diagonal = None, None
        for seq in range(seq_count):
            factor, normed, masks, bounds, packs, lses, mixed, unused = saved[seq]
            parts, diagonal_seq = attend_backward(
                packs[g],
                d_mixed[seq * seq_length : (seq + 1) * seq_length],
                mixed,
                lses[g],
                *masks,
                bounds,
                tiles,
                first,
                head_dim,
            )
            if g:
                parts, dense_out, halves[0] = lax.optimization_barrier((parts, dense_out, halves[0]))
            here = dot(normed, parts, TN)
            grad_group = here if grad_group is None else grad_group + here
            diagonal = diagonal_seq if diagonal is None else diagonal + diagonal_seq
            d_normed_one[seq] = d_normed_one[seq] + dot(parts, w_groups[g], NT)
        diagonals.append(diagonal)
        halves.append(scatter_dp(grad_group))
    grad_parts = []
    for g, (first, many) in enumerate(groups):
        total = scatter_near(halves[g])
        grad_parts.append(total.reshape(-1, many, 3, width))
    grad_qkv = jnp.concatenate(grad_parts, axis=1).transpose(0, 2, 1, 3).reshape(-1, 3 * model_width)
    grad_gain_one = jnp.sum(grad_qkv * qkv_weight.astype(f32), axis=1) / attn_gain.astype(f32)

    input_grads = []
    for seq in range(seq_count):
        factor = saved[seq][0]
        normed_in = layer_in[seq] * factor
        weighted = d_normed_one[seq] * gain_one
        input_grads.append(
            d_mid[seq * seq_length : (seq + 1) * seq_length]
            + factor * (weighted - normed_in * jnp.mean(weighted * normed_in, axis=-1, keepdims=True))
        )
    input_grad = jnp.stack(input_grads)

    grad_rel = jnp.einsum("hgp,bgp->bh", jnp.concatenate(diagonals, axis=0), one_hot_windows, precision=HIGHEST)
    shares = [grad_rel, grad_gain_two, grad_router, sums]
    tail = jnp.concatenate([share.reshape(-1) for share in shares])
    tail = jnp.pad(tail, (0, -tail.shape[0] % (8 * LANES))).reshape(-1, LANES)
    tail = sum_all(tail).reshape(-1)
    ends = [0]
    for share in shares:
        ends.append(ends[-1] + share.size)
    grad_rel, grad_gain_two, grad_router, totals = [
        tail[ends[i] : ends[i + 1]].reshape(share.shape) for i, share in enumerate(shares)
    ]
    stats = jnp.sqrt(totals[:3] / (totals[3] * model_width))
    own_rows = attn_gain.shape[0]
    own_first = (lax.axis_index("dp") * lax.axis_size("expert") + me) * own_rows
    return (
        output,
        input_grad,
        grad_gain_one,
        grad_qkv,
        dense_out,
        lax.dynamic_slice_in_dim(grad_gain_two, own_first, own_rows),
        lax.dynamic_slice_in_dim(grad_router, own_first, own_rows),
        grad_rel,
        grad_expert_in,
        grad_expert_out,
        stats,
    )


def solution(mesh):
    in_specs = (
        P(("dp", "expert"), None, None),
        P(("dp", "expert"), None, None),
        P(("dp", "expert")),
        P(("dp", "expert"), None),
        P(("dp", "expert"), None),
        P(("dp", "expert")),
        P(("dp", "expert"), None),
        P(),
        P("expert", None, None),
        P("expert", None, None),
        P(("dp", "expert"), None),
        P(("dp", "expert"), None),
        P(("dp", "expert"), None),
        P(("dp", "expert"), None),
        P(("dp", "expert"), None),
        P(),
    )
    out_specs = (
        P(("dp", "expert"), None, None),
        P(("dp", "expert"), None, None),
        P(("dp", "expert")),
        P(("dp", "expert"), None),
        P(("dp", "expert"), None),
        P(("dp", "expert")),
        P(("dp", "expert"), None),
        P(),
        P("expert", None, "dp"),
        P("expert", "dp", None),
        P(),
    )
    return jax.shard_map(body, mesh=mesh, in_specs=in_specs, out_specs=out_specs, check_vma=False)
```

time: 787 us -> 512 us (0.65)
  blocking collectives: 279 us -> 0 us
  starting transfers between devices: 9.44 us -> 81 us
  Pallas kernels: 159 us -> 106 us
  local copies, waits for them, and re-layouts: 92.2 us -> 39.8 us
  waiting for transfers between devices: 73.2 us -> 125 us
  matrix products: 118 us -> 98.1 us
    all_gather x1 -> x0, blocking collectives: 99.9 us -> none  [body(): lax.all_gather(router_weight, ('dp', 'expert'), axis=0, tiled=True)]
    all_to_all x2 -> x0, blocking collectives: 98.2 us -> none  [the longest x1 51.2 us: body(): lax.all_to_all(send_rows, 'expert', split_axis=0, concat_axis=1, tiled=True)]
    unnamed x2 -> x0, blocking collectives: 81 us -> none
    ppermute x0 -> x15, waiting for transfers between devices: none -> 44.6 us  [exchange(): lax.ppermute(rows, axis, [(i, i ^ distance) for i in range(lax.axis_size(...]
    pallas_call x1 -> x2, Pallas kernels: 63.5 us -> 21.7 us  [attend_forward(): pl.pallas_call(functools.partial(forward_kernel, head_dim, reach), grid_s...]
    all_to_all x2 -> x9, starting transfers between devices: 8.79 us -> 48.1 us  [swap_blocks(): lax.all_to_all(blocks, 'expert', split_axis=0, concat_axis=0, tiled=True)]
    all_to_all x2 -> x9, waiting for transfers between devices: 42.9 us -> 80.6 us  [swap_blocks(): lax.all_to_all(blocks, 'expert', split_axis=0, concat_axis=0, tiled=True)]
    pallas_call x1 -> x2, Pallas kernels: 85.6 us -> 48.9 us  [attend_backward(): pl.pallas_call(functools.partial(backward_kernel, head_dim, reach), grid_...]
  transfers between devices with their start and end apart: 8 -> 27, of which waited for: 3 -> 13; matrix products, arithmetic and copies ran while one was open for 20% -> 31% of each run, Pallas kernels for 20% -> 16%
where the time goes in v2:
time: 512 us; the launch traced here: 501 us
  waiting for transfers between devices  125 us (24%)
  Pallas kernels  106 us (21%)
  matrix products  98.1 us (19%)
  starting transfers between devices  81 us (16%)
  local copies, waits for them, and re-layouts  39.8 us (8%)
  other arithmetic  35 us (7%)
  between operations  16.2 us (3%)
    all_to_all x9, waiting for transfers between devices, swap_blocks(): lax.all_to_all(blocks, 'expert', split_axis=0, concat_axis=0, tiled=True)  80.6 us
    dot_general x10, matrix products, dot(): return lax.dot_general(left, right, dims, preferred_element_type=f32)  64.8 us
    pallas_call x2, Pallas kernels, attend_backward(): pl.pallas_call(functools.partial(backward_kernel, head_dim, reach), grid_...  48.9 us
    all_to_all x9, starting transfers between devices, swap_blocks(): lax.all_to_all(blocks, 'expert', split_axis=0, concat_axis=0, tiled=True)  48.1 us
    ppermute x15, waiting for transfers between devices, exchange(): lax.ppermute(rows, axis, [(i, i ^ distance) for i in range(lax.axis_size(...  44.6 us
    ppermute x15, starting transfers between devices, exchange(): lax.ppermute(rows, axis, [(i, i ^ distance) for i in range(lax.axis_size(...  32.2 us
    unnamed x175, local copies, waits for them, and re-layouts  30.3 us
    pallas_call x1, Pallas kernels, run_expert(): pl.pallas_call(functools.partial(expert_kernel, experts), grid_spec=grid_...  23.9 us
  transfers between devices with their start and end apart: 27, of which 13 were waited for; matrix products, arithmetic and copies ran while one was open for 31% of the time, Pallas kernels for 16%

profile of v2, /device:TPU:0, one launch (start us, length us, event | category | flops | bytes accessed | tf_op | source)
XLA Modules:
  0.0 501.4 jit_solution(11057375307021695300)
XLA Ops:
  10.5 7.3 %all-to-all-start = ((bf16[8,24,1664]{2,1,0:T(8,128)(2,1)}), bf16[8,24,1664]{2,1,0:T(8,128)(2,1)S(1)}, u32[]{:S(2)}, u32[]{:S(2)}) async-start(bf16[8,24,1664]{2,1,0:T(8,128)(2,1)} %get-tuple-element.42), calls=%async_computation | async-start | bytes 1277952 | tf_op jit(solution)/shard_map/all_to_all | solution.py:481
  21.6 9.6 %toeplitz_tiles.1.bias_ref = f32[12,1408,128]{2,1,0:T(8,128)} custom-call(f32[12,11,256]{2,1,0:T(8,128)} %pad_maximum_fusion.2.window_ref), custom_call_target="tpu_custom_call" | custom-call | tf_op jit(solution)/shard_map/toeplitz_tiles/pallas_call | solution.py:47
  37.4 12.3 %collective-permute-done = bf16[1,8,24,1664]{3,2,1,0:T(8,128)(2,1)} collective-permute-done((bf16[1,8,24,1664]{3,2,1,0:T(8,128)(2,1)S(1)}, bf16[1,8,24,1664]{3,2,1,0:T(8,128)(2,1)}, u32[]{:S(2)}, u32[]{:S(2)}) %collective-permute-start) | collective-permute-done | bytes 639008 | tf_op jit(solution)/shard_map/ppermute | solution.py:473
  60.1 10.9 %all-to-all-done.1 = bf16[8,24,768]{2,1,0:T(8,128)(2,1)S(1)} async-done(((bf16[8,24,768]{2,1,0:T(8,128)(2,1)}), bf16[8,24,768]{2,1,0:T(8,128)(2,1)S(1)}, u32[]{:S(2)}, u32[]{:S(2)}) %all-to-all-start.1) | async-done | bytes 294944 | tf_op jit(solution)/shard_map/all_to_all | solution.py:481
  89.8 14.4 %attend_forward.2 = (bf16[1024,768]{1,0:T(8,128)(2,1)S(1)}, f32[2,4,1024]{2,1,0:T(4,128)S(1)}) custom-call(s32[4]{0:T(128)S(1)} %get-tuple-element.148.low_ref, s32[4]{0:T(128)S(1)} %get-tuple-element.147.high_ref, bf16[1024,1536]{1,0:T(8,128)(2,1)S(1)} %convolution_convert_fusion.3.q_ref.k_ref.v_ref, ...), custom_call_target="tpu_custom_call", output_to_operand_aliasing={{0}: (8, {})} | custom-call | flops 17179869184 | bytes 75497472 | tf_op jit(solution)/shard_map/attend_forward/pallas_call | solution.py:279
  108.0 8.8 %all-to-all-start.3 = ((bf16[8,160,768]{2,1,0:T(8,128)(2,1)}), bf16[8,160,768]{2,1,0:T(8,128)(2,1)}, u32[]{:S(2)}, u32[]{:S(2)}) async-start(bf16[8,160,768]{2,1,0:T(8,128)(2,1)} %bitcast.211), calls=%async_computation.3 | async-start | bytes 3932160 | tf_op jit(solution)/shard_map/all_to_all | solution.py:481
  123.7 7.3 %attend_forward.3 = (bf16[1024,768]{1,0:T(8,128)(2,1)S(1)}, f32[1,4,1024]{2,1,0:T(4,128)S(1)}) custom-call(s32[4]{0:T(128)S(1)} %get-tuple-element.148.low_ref, s32[4]{0:T(128)S(1)} %get-tuple-element.147.high_ref, bf16[1024,768]{1,0:T(8,128)(2,1)S(1)} %convolution_convert_fusion.5.q_ref.k_ref.v_ref, ...), custom_call_target="tpu_custom_call", output_to_operand_aliasing={{0}: (8, {})} | custom-call | flops 8589934592 | bytes 37748736 | tf_op jit(solution)/shard_map/attend_forward/pallas_call | solution.py:279
  141.7 19.9 %all-to-all-done.3 = bf16[8,160,768]{2,1,0:T(8,128)(2,1)} async-done(((bf16[8,160,768]{2,1,0:T(8,128)(2,1)}), bf16[8,160,768]{2,1,0:T(8,128)(2,1)}, u32[]{:S(2)}, u32[]{:S(2)}) %all-to-all-start.3) | async-done | bytes 1966112 | tf_op jit(solution)/shard_map/all_to_all | solution.py:481
  169.4 11.0 %convolution_convert_fusion.d_hidden_ref = bf16[1280,3072]{1,0:T(8,128)(2,1)} fusion(bf16[1280,768]{1,0:T(8,128)(2,1)} %bitcast.30, bf16[1,3072,768]{2,1,0:T(8,128)(2,1)} %param.25), kind=kOutput, calls=%fused_computation | convolution fusion | flops 6043729920 | bytes 14548992 | tf_op jit(solution)/shard_map/dot_general | solution.py:22
  180.4 30.7 %all-to-all-done.2 = bf16[8,160,768]{2,1,0:T(8,128)(2,1)S(1)} async-done(((bf16[8,160,768]{2,1,0:T(8,128)(2,1)}), bf16[8,160,768]{2,1,0:T(8,128)(2,1)S(1)}, u32[]{:S(2)}, u32[]{:S(2)}) %all-to-all-start.2) | async-done | bytes 1966112 | tf_op jit(solution)/shard_map/all_to_all | solution.py:481
  211.1 23.9 %run_expert.1 = (bf16[1280,3072]{1,0:T(8,128)(2,1)}, bf16[1280,3072]{1,0:T(8,128)(2,1)}, bf16[1280,768]{1,0:T(8,128)(2,1)S(1)}, bf16[1280,128]{1,0:T(8,128)(2,1)S(1)}, f32[1280,1]{1,0:T(8,128)S(1)}) custom-call(s32[1]{0:T(128)} %bitcast.25.me_ref, bf16[1280,768]{1,0:T(8,128)(2,1)S(1)} %bitcast.194, bf16[768,3072]{1,0:T(8,128)(2,1)} %bitcast.239, ...), custom_call_target="tpu_custom_call" | custom-call | flops 12079595520 | bytes 31457280 | tf_op jit(solution)/shard_map/run_expert/pallas_call | solution.py:440
  242.1 11.1 %convolution_convert_fusion.1 = bf16[3072,768]{1,0:T(8,128)(2,1)} fusion(bf16[1280,3072]{1,0:T(8,128)(2,1)} %get-tuple-element.58, bf16[1280,768]{1,0:T(8,128)(2,1)} %bitcast.30, f32[1280]{0:T(1024)S(1)} %reduce.5), kind=kOutput, calls=%fused_computation.6 | convolution fusion | flops 6045106176 | bytes 14554112 | tf_op jit(solution)/shard_map/dot_general | solution.py:22
  253.2 10.9 %fusion.17 = bf16[1280,768]{1,0:T(8,128)(2,1)} fusion(bf16[1280,3072]{1,0:T(8,128)(2,1)} %get-tuple-element.58, bf16[1,3072,768]{2,1,0:T(8,128)(2,1)} %param.25, f32[1280]{0:T(1024)S(1)} %reduce.5), kind=kOutput, calls=%fused_computation.27 | convolution fusion | flops 6041763840 | bytes 14554112 | tf_op jit(solution)/shard_map/dot_general | solution.py:22
  264.1 11.6 %convolution_convert_fusion.2 = bf16[768,3072]{1,0:T(8,128)(2,1)} fusion(bf16[1280,768]{1,0:T(8,128)(2,1)S(1)} %bitcast.195, bf16[1280,3072]{1,0:T(8,128)(2,1)} %get-tuple-element.59), kind=kOutput, calls=%fused_computation.7 | convolution fusion | flops 6042157056 | bytes 14548992 | tf_op jit(solution)/shard_map/dot_general | solution.py:22
  275.8 10.6 %all-to-all-done.4 = bf16[8,160,768]{2,1,0:T(8,128)(2,1)} async-done(((bf16[8,160,768]{2,1,0:T(8,128)(2,1)}), bf16[8,160,768]{2,1,0:T(8,128)(2,1)}, u32[]{:S(2)}, u32[]{:S(2)}) %all-to-all-start.4) | async-done | bytes 1966112 | tf_op jit(solution)/shard_map/all_to_all | solution.py:481
  291.0 6.4 %multiply_reduce_fusion = (f32[768]{0:T(1024)}, f32[1024]{0:T(1024)S(1)}, f32[]{:T(128)}, f32[1024,768]{0,1:T(8,128)S(1)}) fusion(f32[1024,768]{0,1:T(8,128)} %copy-done.31, f32[1024]{0:T(1024)} %copy-done.58, f32[768]{0:T(1024)S(1)} %copy-done.57, f32[1024]{0:T(1024)} %bitcast.229, bf16[1280,768]{1,0:T(8,128)(2,1)} %bitcast.34, s32[1024]{0:T(1024)} %bitcast.232), kind=kOutput, calls=%fused_computation.43 | convolution fusion | flops 2021652736 | bytes 8280068 | tf_op jit(solution)/shard_map/dot_general | solution.py:596
  301.4 31.3 %attend_backward.2 = (bf16[1024,1536]{1,0:T(8,128)(2,1)}, f32[8,11,256]{2,1,0:T(8,128)S(1)}) custom-call(s32[4]{0:T(128)S(1)} %get-tuple-element.148.low_ref, s32[4]{0:T(128)S(1)} %get-tuple-element.147.high_ref, bf16[1024,1536]{1,0:T(8,128)(2,1)} %copy-done.15, bf16[1024,1536]{1,0:T(8,128)(2,1)} %copy-done.15, bf16[1024,1536]{1,0:T(8,128)(2,1)} %copy-done.15, ...), custom_call_target="tpu_custom_call" | custom-call | flops 42949672960 | bytes 150994944 | tf_op jit(solution)/shard_map/attend_backward/pallas_call | solution.py:326
  348.2 10.7 %collective-permute-start.5 = (bf16[1,192,768]{2,1,0:T(8,128)(2,1)S(1)}, bf16[1,192,768]{2,1,0:T(8,128)(2,1)S(1)}, u32[]{:S(2)}, u32[]{:S(2)}) collective-permute-start(bf16[1,192,768]{2,1,0:T(8,128)(2,1)S(1)} %dynamic-slice_convert_fusion.5), channel_id=1, source_target_pairs={{0,16},{8,24},{16,0},{24,8},{1,17},{9,25},{17,1},{25,9},{2,18},{10... | collective-permute-start | bytes 884744 | tf_op jit(solution)/shard_map/ppermute | solution.py:473
  367.5 15.1 %collective-permute-done.7 = bf16[1,192,1536]{2,1,0:T(8,128)(2,1)S(1)} collective-permute-done((bf16[1,192,1536]{2,1,0:T(8,128)(2,1)S(1)}, bf16[1,192,1536]{2,1,0:T(8,128)(2,1)S(1)}, u32[]{:S(2)}, u32[]{:S(2)}) %collective-permute-start.7) | collective-permute-done | bytes 589856 | tf_op jit(solution)/shard_map/ppermute | solution.py:473
  389.4 17.6 %attend_backward.3 = (bf16[1024,768]{1,0:T(8,128)(2,1)}, f32[4,11,256]{2,1,0:T(8,128)S(1)}) custom-call(s32[4]{0:T(128)S(1)} %get-tuple-element.148.low_ref, s32[4]{0:T(128)S(1)} %get-tuple-element.147.high_ref, bf16[1024,768]{1,0:T(8,128)(2,1)} %copy-done.16, bf16[1024,768]{1,0:T(8,128)(2,1)} %copy-done.16, bf16[1024,768]{1,0:T(8,128)(2,1)} %copy-done.16, ...), custom_call_target="tpu_custom_call" | custom-call | flops 21474836480 | bytes 75497472 | tf_op jit(solution)/shard_map/attend_backward/pallas_call | solution.py:326
  412.4 7.8 %fusion.30 = (f32[]{:T(128)}, f32[1024]{0:T(1024)S(1)}, f32[]{:T(128)}, bf16[1,1024,768]{1,2,0:T(8,128)(2,1)}) fusion(bf16[1,1024,768]{1,2,0:T(8,128)(2,1)S(1)} %copy-done.23, f32[1024]{0:T(1024)S(1)} %bitcast.230, f32[1024,768]{0,1:T(8,128)S(1)} %add_multiply_fusion, f32[1024]{0:T(1024)S(1)} %copy-done.51, f32[1024,768]{0,1:T(8,128)S(1)} %copy-done.33, ...), kind=kOutput, calls=%fused_computation.38 | convolution fusion | flops 2024012800 | bytes 11419656 | tf_op jit(solution)/shard_map/dot_general | solution.py:596
  427.8 6.9 %collective-permute-start.11 = (f32[64,128]{1,0:T(8,128)S(1)}, f32[64,128]{1,0:T(8,128)S(1)}, u32[]{:S(2)}, u32[]{:S(2)}) collective-permute-start(f32[64,128]{1,0:T(8,128)S(1)} %fusion.83), channel_id=1, source_target_pairs={{0,16},{8,24},{16,0},{24,8},{1,17},{9,25},{17,1},{25,9},{2,18},{10... | collective-permute-start | bytes 98312 | tf_op jit(solution)/shard_map/ppermute | solution.py:473
  445.7 7.3 %collective-permute-done.13 = f32[64,128]{1,0:T(8,128)S(1)} collective-permute-done((f32[64,128]{1,0:T(8,128)S(1)}, f32[64,128]{1,0:T(8,128)S(1)}, u32[]{:S(2)}, u32[]{:S(2)}) %collective-permute-start.13) | collective-permute-done | bytes 32800 | tf_op jit(solution)/shard_map/ppermute | solution.py:473
  481.2 6.4 %all-to-all-done.8 = bf16[8,24,768]{2,1,0:T(8,128)(2,1)S(1)} async-done(((bf16[8,24,768]{2,1,0:T(8,128)(2,1)}), bf16[8,24,768]{2,1,0:T(8,128)(2,1)S(1)}, u32[]{:S(2)}, u32[]{:S(2)}) %all-to-all-start.8) | async-done | bytes 294944 | tf_op jit(solution)/shard_map/all_to_all | solution.py:481
  (327 shorter events, 175.3 us)
Async XLA Ops:
  10.5 24.2 %all-to-all-start = ((bf16[8,24,1664]{2,1,0:T(8,128)(2,1)}), bf16[8,24,1664]{2,1,0:T(8,128)(2,1)S(1)}, u32[]{:S(2)}, u32[]{:S(2)}) async-start(bf16[8,24,1664]{2,1,0:T(8,128)(2,1)} %get-tuple-element.42), calls=%async_computation | async-start | bytes 1277952 | tf_op jit(solution)/shard_map/all_to_all | solution.py:481
  17.7 114.4 %all-gather.2.cloned.1.call-start = ((), (), s32[]{:S(2)}) async-start(), calls=%async_computation.11 | async-start | bytes 1216512 | tf_op jit(solution)/shard_map/all_gather | solution.py:578
  34.7 15.0 %collective-permute-start = (bf16[1,8,24,1664]{3,2,1,0:T(8,128)(2,1)S(1)}, bf16[1,8,24,1664]{3,2,1,0:T(8,128)(2,1)}, u32[]{:S(2)}, u32[]{:S(2)}) collective-permute-start(bf16[1,8,24,1664]{3,2,1,0:T(8,128)(2,1)S(1)} %bitcast.207), channel_id=1, source_target_pairs={{0,16},{8,24},{16,0},{24,8},{1,17},{9,25},{17,1},{25,9},{2,18},{10... | collective-permute-start | bytes 1916936 | tf_op jit(solution)/shard_map/ppermute | solution.py:473
  52.2 30.3 %collective-permute-start.1 = (bf16[2,8,24,1664]{3,2,1,0:T(8,128)(2,1)}, bf16[2,8,24,1664]{3,2,1,0:T(8,128)(2,1)}, u32[]{:S(2)}, u32[]{:S(2)}) collective-permute-start(bf16[2,8,24,1664]{3,2,1,0:T(8,128)(2,1)} %maximum_bitcast_fusion), channel_id=1, source_target_pairs={{0,8},{8,0},{16,24},{24,16},{1,9},{9,1},{17,25},{25,17},{2,10},{10... | collective-permute-start | bytes 3833864 | tf_op jit(solution)/shard_map/ppermute | solution.py:473
  54.2 16.8 %all-to-all-start.1 = ((bf16[8,24,768]{2,1,0:T(8,128)(2,1)}), bf16[8,24,768]{2,1,0:T(8,128)(2,1)S(1)}, u32[]{:S(2)}, u32[]{:S(2)}) async-start(bf16[8,24,768]{2,1,0:T(8,128)(2,1)} %get-tuple-element.45), calls=%async_computation.1 | async-start | bytes 589824 | tf_op jit(solution)/shard_map/all_to_all | solution.py:481
  71.0 9.6 %collective-permute-start.2 = (bf16[1,8,24,768]{3,2,1,0:T(8,128)(2,1)S(1)}, bf16[1,8,24,768]{3,2,1,0:T(8,128)(2,1)}, u32[]{:S(2)}, u32[]{:S(2)}) collective-permute-start(bf16[1,8,24,768]{3,2,1,0:T(8,128)(2,1)S(1)} %bitcast.218), channel_id=1, source_target_pairs={{0,16},{8,24},{16,0},{24,8},{1,17},{9,25},{17,1},{25,9},{2,18},{10... | collective-permute-start | bytes 884744 | tf_op jit(solution)/shard_map/ppermute | solution.py:473
  108.0 53.6 %all-to-all-start.3 = ((bf16[8,160,768]{2,1,0:T(8,128)(2,1)}), bf16[8,160,768]{2,1,0:T(8,128)(2,1)}, u32[]{:S(2)}, u32[]{:S(2)}) async-start(bf16[8,160,768]{2,1,0:T(8,128)(2,1)} %bitcast.211), calls=%async_computation.3 | async-start | bytes 3932160 | tf_op jit(solution)/shard_map/all_to_all | solution.py:481
  161.7 49.4 %all-to-all-start.2 = ((bf16[8,160,768]{2,1,0:T(8,128)(2,1)}), bf16[8,160,768]{2,1,0:T(8,128)(2,1)S(1)}, u32[]{:S(2)}, u32[]{:S(2)}) async-start(bf16[8,160,768]{2,1,0:T(8,128)(2,1)} %bitcast.210), calls=%async_computation.2 | async-start | bytes 3932160 | tf_op jit(solution)/shard_map/all_to_all | solution.py:481
  237.0 49.4 %all-to-all-start.4 = ((bf16[8,160,768]{2,1,0:T(8,128)(2,1)}), bf16[8,160,768]{2,1,0:T(8,128)(2,1)}, u32[]{:S(2)}, u32[]{:S(2)}) async-start(bf16[8,160,768]{2,1,0:T(8,128)(2,1)} %bitcast.201), calls=%async_computation.4 | async-start | bytes 3932160 | tf_op jit(solution)/shard_map/all_to_all | solution.py:481
  241.4 247.3 %reduce-scatter.5.cloned.1.call-start = ((), (), s32[]{:S(2)}) async-start(), calls=%async_computation.13 | async-start | bytes 5898240 | tf_op jit(solution)/shard_map/reduce_scatter | solution.py:635
  286.4 97.2 %all-to-all-start.5 = ((bf16[8,160,768]{2,1,0:T(8,128)(2,1)}), bf16[8,160,768]{2,1,0:T(8,128)(2,1)}, u32[]{:S(2)}, u32[]{:S(2)}) async-start(bf16[8,160,768]{2,1,0:T(8,128)(2,1)} %bitcast.209), calls=%async_computation.5 | async-start | bytes 3932160 | tf_op jit(solution)/shard_map/all_to_all | solution.py:481
  290.7 200.8 %reduce-scatter.3.cloned.1.call-start = ((), (), s32[]{:S(2)}) async-start(), calls=%async_computation.12 | async-start | bytes 5898240 | tf_op jit(solution)/shard_map/reduce_scatter | solution.py:634
  338.9 20.0 %collective-permute-start.6 = (bf16[2,192,1536]{2,1,0:T(8,128)(2,1)}, bf16[2,192,1536]{2,1,0:T(8,128)(2,1)}, u32[]{:S(2)}, u32[]{:S(2)}) collective-permute-start(bf16[2,192,1536]{2,1,0:T(8,128)(2,1)} %fusion.52), channel_id=1, source_target_pairs={{0,8},{8,0},{16,24},{24,16},{1,9},{9,1},{17,25},{25,17},{2,10},{10... | collective-permute-start | bytes 3538952 | tf_op jit(solution)/shard_map/ppermute | solution.py:473
  348.2 18.5 %collective-permute-start.5 = (bf16[1,192,768]{2,1,0:T(8,128)(2,1)S(1)}, bf16[1,192,768]{2,1,0:T(8,128)(2,1)S(1)}, u32[]{:S(2)}, u32[]{:S(2)}) collective-permute-start(bf16[1,192,768]{2,1,0:T(8,128)(2,1)S(1)} %dynamic-slice_convert_fusion.5), channel_id=1, source_target_pairs={{0,16},{8,24},{16,0},{24,8},{1,17},{9,25},{17,1},{25,9},{2,18},{10... | collective-permute-start | bytes 884744 | tf_op jit(solution)/shard_map/ppermute | solution.py:473
  361.8 20.8 %collective-permute-start.7 = (bf16[1,192,1536]{2,1,0:T(8,128)(2,1)S(1)}, bf16[1,192,1536]{2,1,0:T(8,128)(2,1)S(1)}, u32[]{:S(2)}, u32[]{:S(2)}) collective-permute-start(bf16[1,192,1536]{2,1,0:T(8,128)(2,1)S(1)} %dynamic-slice_convert_fusion.2), channel_id=1, source_target_pairs={{0,16},{8,24},{16,0},{24,8},{1,17},{9,25},{17,1},{25,9},{2,18},{10... | collective-permute-start | bytes 1769480 | tf_op jit(solution)/shard_map/ppermute | solution.py:473
  383.6 24.0 %all-to-all-start.6 = ((bf16[8,24,768]{2,1,0:T(8,128)(2,1)}), bf16[8,24,768]{2,1,0:T(8,128)(2,1)S(1)}, u32[]{:S(2)}, u32[]{:S(2)}) async-start(bf16[8,24,768]{2,1,0:T(8,128)(2,1)} %bitcast.42), calls=%async_computation.6 | async-start | bytes 589824 | tf_op jit(solution)/shard_map/all_to_all | solution.py:481
  427.2 30.6 %collective-permute-start.8 = (bf16[2,192,768]{2,1,0:T(8,128)(2,1)S(1)}, bf16[2,192,768]{2,1,0:T(8,128)(2,1)}, u32[]{:S(2)}, u32[]{:S(2)}) collective-permute-start(bf16[2,192,768]{2,1,0:T(8,128)(2,1)S(1)} %fusion.58), channel_id=1, source_target_pairs={{0,8},{8,0},{16,24},{24,16},{1,9},{9,1},{17,25},{25,17},{2,10},{10... | collective-permute-start | bytes 1769480 | tf_op jit(solution)/shard_map/ppermute | solution.py:473
  427.8 8.8 %collective-permute-start.11 = (f32[64,128]{1,0:T(8,128)S(1)}, f32[64,128]{1,0:T(8,128)S(1)}, u32[]{:S(2)}, u32[]{:S(2)}) collective-permute-start(f32[64,128]{1,0:T(8,128)S(1)} %fusion.83), channel_id=1, source_target_pairs={{0,16},{8,24},{16,0},{24,8},{1,17},{9,25},{17,1},{25,9},{2,18},{10... | collective-permute-start | bytes 98312 | tf_op jit(solution)/shard_map/ppermute | solution.py:473
  436.6 6.9 %collective-permute-start.12 = (f32[64,128]{1,0:T(8,128)S(1)}, f32[64,128]{1,0:T(8,128)S(1)}, u32[]{:S(2)}, u32[]{:S(2)}) collective-permute-start(f32[64,128]{1,0:T(8,128)S(1)} %fusion.108), channel_id=1, source_target_pairs={{0,1},{1,0},{2,3},{3,2},{4,5},{5,4},{6,7},{7,6},{8,9},{9,8},{10,11... | collective-permute-start | bytes 98312 | tf_op jit(solution)/shard_map/ppermute | solution.py:473
  438.8 36.9 %all-to-all-start.7 = ((bf16[8,24,1536]{2,1,0:T(8,128)(2,1)}), bf16[8,24,1536]{2,1,0:T(8,128)(2,1)S(1)}, u32[]{:S(2)}, u32[]{:S(2)}) async-start(bf16[8,24,1536]{2,1,0:T(8,128)(2,1)} %bitcast.51), calls=%async_computation.7 | async-start | bytes 1179648 | tf_op jit(solution)/shard_map/all_to_all | solution.py:481
  443.6 9.4 %collective-permute-start.13 = (f32[64,128]{1,0:T(8,128)S(1)}, f32[64,128]{1,0:T(8,128)S(1)}, u32[]{:S(2)}, u32[]{:S(2)}) collective-permute-start(f32[64,128]{1,0:T(8,128)S(1)} %add.176), channel_id=1, source_target_pairs={{0,2},{1,3},{2,0},{3,1},{4,6},{5,7},{6,4},{7,5},{8,10},{9,11},{10,... | collective-permute-start | bytes 98312 | tf_op jit(solution)/shard_map/ppermute | solution.py:473
  453.0 18.6 %collective-permute-start.14 = (f32[64,128]{1,0:T(8,128)S(1)}, f32[64,128]{1,0:T(8,128)S(1)}, u32[]{:S(2)}, u32[]{:S(2)}) collective-permute-start(f32[64,128]{1,0:T(8,128)S(1)} %add.177), channel_id=1, source_target_pairs={{0,4},{1,5},{2,6},{3,7},{4,0},{5,1},{6,2},{7,3},{8,12},{9,13},{10,... | collective-permute-start | bytes 98312 | tf_op jit(solution)/shard_map/ppermute | solution.py:473
  460.1 13.8 %collective-permute-start.9 = (bf16[1,192,768]{2,1,0:T(8,128)(2,1)}, bf16[1,192,768]{2,1,0:T(8,128)(2,1)}, u32[]{:S(2)}, u32[]{:S(2)}) collective-permute-start(bf16[1,192,768]{2,1,0:T(8,128)(2,1)} %dynamic-slice_convert_fusion.4), channel_id=1, source_target_pairs={{0,16},{8,24},{16,0},{24,8},{1,17},{9,25},{17,1},{25,9},{2,18},{10... | collective-permute-start | bytes 884744 | tf_op jit(solution)/shard_map/ppermute | solution.py:473
  475.7 11.9 %all-to-all-start.8 = ((bf16[8,24,768]{2,1,0:T(8,128)(2,1)}), bf16[8,24,768]{2,1,0:T(8,128)(2,1)S(1)}, u32[]{:S(2)}, u32[]{:S(2)}) async-start(bf16[8,24,768]{2,1,0:T(8,128)(2,1)} %bitcast.57), calls=%async_computation.8 | async-start | bytes 589824 | tf_op jit(solution)/shard_map/all_to_all | solution.py:481
  (81 other events, 904.2 us)
Sparse Core Ops, SparseCore 0:
  36.3 54.5 all-gather.1
  253.3 49.3 reduce-scatter.4
  345.4 59.8 reduce-scatter.2

commit v3 on v2

--- a/solution.py
+++ b/solution.py
@@ -7,10 +7,12 @@
 from jax.experimental.pallas import tpu as pltpu
 from jax.sharding import PartitionSpec as P
 
+EPSILON = 1e-06
 MASK_STEP = 1e30
 ROWS = 256
 LANES = 128
 STEP_HEADS = 4
+VMEM_BYTES = 60 * 2**20
 SMALL_GAINS = 2
 bf16, f32 = jnp.bfloat16, jnp.float32
 NT = (((1,), (1,)), ((), ()))
@@ -18,20 +20,21 @@
 TN = (((0,), (0,)), ((), ()))
 
 
+def cost(microseconds):
+    return pl.CostEstimate(flops=int(microseconds * 1.1e9), bytes_accessed=0, transcendentals=0)
+
+
 def dot(left, right, dims):
     return lax.dot_general(left, right, dims, preferred_element_type=f32)
 
 
-def bias_windows(values, reach):
-    heads, offsets = values.shape
-    chunks = (offsets + 1) // LANES
-    turned = jnp.pad(values[:, ::-1], ((0, 0), (1, 0))).reshape(heads, chunks, LANES)
+def offset_windows(values, reach):
+    chunks = (values.shape[0] + 1) // LANES
+    turned = jnp.pad(values[::-1], (1, 0)).reshape(chunks, LANES)
     middle = chunks // 2
-    groups = list(range(-reach, reach + 1))
-    first = [middle - g for g in groups]
-    here = turned[:, first[-1] : first[0] + 1][:, ::-1]
-    before = turned[:, first[-1] - 1 : first[0]][:, ::-1]
-    return jnp.concatenate([here, before], axis=2)
+    return jnp.stack(
+        [jnp.concatenate([turned[middle - g], turned[middle - g - 1]]) for g in range(-reach, reach + 1)]
+    )
 
 
 def toeplitz_kernel(reach, window_ref, tile_ref):
@@ -50,6 +53,8 @@
         in_specs=[pl.BlockSpec((1, groups, width), lambda n: (n, 0, 0))],
         out_specs=pl.BlockSpec((1, groups * LANES, LANES), lambda n: (n, 0, 0)),
         out_shape=jax.ShapeDtypeStruct((heads, groups * LANES, LANES), f32),
+        compiler_params=pltpu.CompilerParams(vmem_limit_bytes=VMEM_BYTES),
+        cost_estimate=cost(9),
         name="toeplitz_tiles",
     )(windows)
 
@@ -72,7 +77,8 @@
     return jnp.concatenate(parts, axis=1)
 
 
-def forward_kernel(head_dim, reach, low_ref, high_ref, q_ref, k_ref, v_ref, qx_ref, kx_ref, bias_ref, unused_ref, mix_ref, lse_ref, vt_ref):
+def forward_kernel(head_dim, reach, low_ref, high_ref, q_ref, k_ref, v_ref, qx_ref, kx_ref, bias_ref, *refs):
+    mix_ref, lse_ref, vt_ref = refs[-3:]
     length, width = q_ref.shape
     heads = width // head_dim
     scale = head_dim ** (-0.5)
@@ -256,6 +262,7 @@
     width = STEP_HEADS * head_dim
     steps = packed.shape[1] // 3 // width
     reach = tiles.shape[1] // LANES // 2
+    shared = [] if mixed is None else [mixed]
     whole = lambda *_: (0, 0)
     grid_spec = pltpu.PrefetchScalarGridSpec(
         num_scalar_prefetch=2,
@@ -267,27 +274,26 @@
             pl.BlockSpec((LANES, length), whole),
             pl.BlockSpec((length, LANES), whole),
             pl.BlockSpec((STEP_HEADS, tiles.shape[1], LANES), lambda p, *_: (first + p, 0, 0)),
-            pl.BlockSpec(memory_space=pl.ANY),
-        ],
+        ]
+        + [pl.BlockSpec(memory_space=pl.ANY)] * len(shared),
         out_specs=[
             pl.BlockSpec((length, width), lambda p, *_: (0, first + p)),
             pl.BlockSpec((1, STEP_HEADS, length), lambda p, *_: (p, 0, 0)),
         ],
         scratch_shapes=[pltpu.VMEM((width, length), bf16)],
     )
-    work = steps * STEP_HEADS * length * length
     return pl.pallas_call(
         functools.partial(forward_kernel, head_dim, reach),
         grid_spec=grid_spec,
         out_shape=[
-            jax.ShapeDtypeStruct(mixed.shape, bf16),
+            jax.ShapeDtypeStruct((length, tiles.shape[0] * head_dim), bf16),
             jax.ShapeDtypeStruct((steps, STEP_HEADS, length), f32),
         ],
-        input_output_aliases={8: 0},
-        compiler_params=pltpu.CompilerParams(vmem_limit_bytes=40 * 2**20),
-        cost_estimate=pl.CostEstimate(flops=32 * work * head_dim, bytes_accessed=steps * 36 * 2**20, transcendentals=work),
+        input_output_aliases={8: 0} if shared else {},
+        compiler_params=pltpu.CompilerParams(vmem_limit_bytes=56 * 2**20),
+        cost_estimate=cost(1),
         name="attend_forward",
-    )(*bounds, packed, packed, packed, query_side, key_side, tiles, mixed)
+    )(*bounds, packed, packed, packed, query_side, key_side, tiles, *shared)
 
 
 def attend_backward(packed, d_mix, mix, lse, query_side, key_side, bounds, tiles, first, head_dim):
@@ -330,22 +336,15 @@
             jax.ShapeDtypeStruct((length, 3 * width * steps), bf16),
             jax.ShapeDtypeStruct((steps * STEP_HEADS, groups, 2 * LANES), f32),
         ],
-        compiler_params=pltpu.CompilerParams(vmem_limit_bytes=52 * 2**20),
-        cost_estimate=pl.CostEstimate(flops=80 * work * head_dim, bytes_accessed=steps * 72 * 2**20, transcendentals=work),
+        compiler_params=pltpu.CompilerParams(vmem_limit_bytes=56 * 2**20),
+        cost_estimate=cost(20 * steps),
         name="attend_backward",
     )(*bounds, packed, packed, packed, d_mix, mix, query_side, key_side, tiles, lse)
 
 
-def spread_kernel(groups, width, weight_ref, first_ref, second_ref, router_ref, *outs):
+def spread_kernel(width, near_steps, weight_ref, out_weight_ref, first_ref, second_ref, router_ref, *outs):
     receivers, count = outs[0].shape[:2]
     steps = weight_ref.shape[1] // (3 * width)
-    for (first, many), out_ref in zip(groups, outs):
-        for p in range(many):
-            for part in range(3):
-                at = (part * steps + first + p) * width
-                rows = weight_ref[:, at : at + width]
-                to = (3 * p + part) * width
-                out_ref[:, :, to : to + width] = jnp.broadcast_to(rows[None], (receivers, *rows.shape))
     row = lax.broadcasted_iota(jnp.int32, (count, count), 0)
     same = row == lax.broadcasted_iota(jnp.int32, (count, count), 1)
     columns = [
@@ -355,20 +354,35 @@
     columns.append(router_ref[...].astype(f32))
     used = SMALL_GAINS + router_ref.shape[1]
     columns.append(jnp.zeros((count, -used % LANES), f32))
-    rows = jnp.concatenate(columns, axis=1).astype(bf16)
-    outs[0][:, :, 3 * groups[0][1] * width :] = jnp.broadcast_to(rows[None], (receivers, *rows.shape))
-
-
-def spread_shard(weight, first_gain, second_gain, router, groups, width, receivers):
-    rows = weight.shape[0]
+    pieces = [
+        weight_ref[:, (part * steps + p) * width : (part * steps + p + 1) * width] for p in range(steps) for part in range(3)
+    ]
+    groups = [
+        pieces[: 3 * near_steps] + [jnp.concatenate(columns, axis=1).astype(bf16)],
+        pieces[3 * near_steps :] + [out_weight_ref[...]],
+    ]
+    for group, out_ref in zip(groups, outs):
+        at = 0
+        for piece in group:
+            out_ref[:, :, at : at + piece.shape[1]] = jnp.broadcast_to(piece[None], (receivers, *piece.shape))
+            at += piece.shape[1]
+
+
+def spread_shard(weight, out_weight, first_gain, second_gain, router, width, near_steps, receivers):
+    rows, columns = weight.shape
     small = SMALL_GAINS + router.shape[1]
     small += -small % LANES
-    widths = [3 * many * width + (0 if first else small) for first, many in groups]
-    return pl.pallas_call(
-        functools.partial(spread_kernel, groups, width),
-        out_shape=[jax.ShapeDtypeStruct((receivers, rows, columns), bf16) for columns in widths],
+    near = 3 * width * near_steps
+    return pl.pallas_call(
+        functools.partial(spread_kernel, width, near_steps),
+        out_shape=[
+            jax.ShapeDtypeStruct((receivers, rows, near + small), bf16),
+            jax.ShapeDtypeStruct((receivers, rows, columns - near + out_weight.shape[1]), bf16),
+        ],
+        compiler_params=pltpu.CompilerParams(vmem_limit_bytes=VMEM_BYTES),
+        cost_estimate=cost(2),
         name="spread_shard",
-    )(weight, first_gain.reshape(1, rows), second_gain.reshape(1, rows), router)
+    )(weight, out_weight, first_gain.reshape(1, rows), second_gain.reshape(1, rows), router)
 
 
 def expert_kernel(experts, me_ref, rows_ref, in_ref, small_ref, d_hidden_ref, hidden_ref, d_pre_ref, d_rows_ref, d_logits_ref, gate_ref,
@@ -413,7 +427,7 @@
         d_rows_ref[...] = (total_ref[...] + dot(d_logits, small_ref[...], NT)).astype(bf16)
 
 
-def run_expert(me, rows, w_in, small, d_hidden, experts):
+def run_expert(me, rows, w_in, weights, small_at, d_hidden, experts):
     count, width = rows.shape
     hidden_width = w_in.shape[1]
     block = 512
@@ -425,7 +439,7 @@
         in_specs=[
             pl.BlockSpec((count, width), whole),
             pl.BlockSpec((width, block), lambda f, *_: (0, f)),
-            pl.BlockSpec(small.shape, whole),
+            pl.BlockSpec((width, LANES), lambda f, *_: (0, small_at)),
             row_blocks,
         ],
         out_specs=[
@@ -447,15 +461,325 @@
             jax.ShapeDtypeStruct((count, LANES), bf16),
             jax.ShapeDtypeStruct((count, 1), f32),
         ],
-        compiler_params=pltpu.CompilerParams(vmem_limit_bytes=48 * 2**20),
-        cost_estimate=pl.CostEstimate(
-            flops=4 * count * width * hidden_width, bytes_accessed=30 * 2**20, transcendentals=count * hidden_width
-        ),
+        compiler_params=pltpu.CompilerParams(vmem_limit_bytes=VMEM_BYTES),
+        cost_estimate=cost(25),
         name="run_expert",
-    )(me.reshape(1), rows, w_in, small, d_hidden)
-
-
-EPSILON = 1e-06
+    )(me.reshape(1), rows, w_in, weights, d_hidden)
+
+
+def expert_grads_kernel(gate_ref, rows_ref, hidden_ref, d_pre_ref, d_slots_ref, back_ref, d_logits_ref, part_in_ref, part_out_ref,
+                        moe_ref, router_ref, turned_ref, d_out_ref, total_ref):
+    step = pl.program_id(0)
+
+    @pl.when(step == 0)
+    def _():
+        turned_ref[...] = rows_ref[...].T
+        d_out_ref[...] = (gate_ref[...] * d_slots_ref[...].astype(f32)).astype(bf16)
+        total_ref[...] = jnp.zeros_like(total_ref)
+        router_ref[...] = dot(turned_ref[...], d_logits_ref[...], NN)
+
+    hidden = hidden_ref[...]
+    part_in_ref[...] = dot(turned_ref[...], d_pre_ref[...], NN).astype(bf16)
+    part_out_ref[...] = dot(hidden, d_out_ref[...], TN).astype(bf16)
+    total_ref[...] += dot(hidden, back_ref[...], NN)
+
+    @pl.when(step == pl.num_programs(0) - 1)
+    def _():
+        moe_ref[...] = (gate_ref[...] * total_ref[...]).astype(bf16)
+
+
+def expert_grads(gate, rows, hidden, d_pre, d_slots, w_back, d_logits):
+    count, width = rows.shape
+    hidden_width = hidden.shape[1]
+    block = 512
+    whole = lambda f: (0, 0)
+    row_blocks = pl.BlockSpec((count, block), lambda f: (0, f))
+    full = pl.BlockSpec((count, width), whole)
+    return pl.pallas_call(
+        expert_grads_kernel,
+        grid=(hidden_width // block,),
+        in_specs=[
+            pl.BlockSpec((count, 1), whole),
+            full,
+            row_blocks,
+            row_blocks,
+            full,
+            pl.BlockSpec((block, width), lambda f: (f, 0)),
+            pl.BlockSpec((count, LANES), whole),
+        ],
+        out_specs=[
+            pl.BlockSpec((width, block), lambda f: (0, f)),
+            pl.BlockSpec((block, width), lambda f: (f, 0)),
+            full,
+            pl.BlockSpec((width, LANES), whole),
+        ],
+        out_shape=[
+            jax.ShapeDtypeStruct((width, hidden_width), bf16),
+            jax.ShapeDtypeStruct((hidden_width, width), bf16),
+            jax.ShapeDtypeStruct((count, width), bf16),
+            jax.ShapeDtypeStruct((width, LANES), f32),
+        ],
+        scratch_shapes=[pltpu.VMEM((width, count), bf16), pltpu.VMEM((count, width), bf16), pltpu.VMEM((count, width), f32)],
+        compiler_params=pltpu.CompilerParams(vmem_limit_bytes=VMEM_BYTES),
+        cost_estimate=cost(27),
+        name="expert_grads",
+    )(gate, rows, hidden, d_pre, d_slots, w_back, d_logits)
+
+
+def row_factor(rows):
+    return lax.rsqrt(jnp.mean(rows * rows, axis=1, keepdims=True) + EPSILON)
+
+
+def middle_kernel(row_steps, mixed_ref, weight_ref, in_ref, gain_ref, slot_ref, rows_ref, slots_ref, normed_ref):
+    step = pl.program_id(0)
+
+    @pl.when(step < row_steps)
+    def _():
+        count = in_ref.shape[0]
+        first = pl.multiple_of(step * count, count)
+        chunks = [slice(at, at + ROWS) for at in range(0, count, ROWS)]
+        gain = gain_ref[...]
+        projected = [dot(mixed_ref[here], weight_ref[...], NN) for here in chunks]
+        for here, attn in zip(chunks, projected):
+            rows = in_ref[here].astype(f32) + attn
+            rows_ref[here] = rows
+            normed_ref[pl.ds(first + here.start, ROWS)] = (rows * row_factor(rows) * gain).astype(bf16)
+
+    @pl.when(step >= row_steps)
+    def _():
+        fill_kernel(slot_ref, normed_ref, slots_ref, (step - row_steps) * slots_ref.shape[0])
+
+
+def fill_kernel(slot_ref, rows_ref, slots_ref, first=0):
+    slots, count = slots_ref.shape[0], rows_ref.shape[0]
+    chunk = ROWS if slots % ROWS == 0 else slots
+    for at in range(0, slots, chunk):
+        slot = lax.broadcasted_iota(jnp.int32, (chunk, count), 0) + (first + at)
+        place = jnp.where(slot == slot_ref[...], 1.0, 0.0).astype(bf16)
+        slots_ref[at : at + chunk] = dot(place, rows_ref[...], NN).astype(bf16)
+
+
+def read_slots(slot_ref, here, blocks_ref):
+    slots = blocks_ref.shape[0]
+    slot = lax.broadcasted_iota(jnp.int32, (ROWS, slots), 1)
+    place = jnp.where(slot == slot_ref[here], 1.0, 0.0).astype(bf16)
+    return dot(place, blocks_ref[...], NN)
+
+
+def fill_slots(slot_row, rows, slots):
+    return pl.pallas_call(
+        fill_kernel,
+        out_shape=jax.ShapeDtypeStruct((slots, rows.shape[1]), bf16),
+        compiler_params=pltpu.CompilerParams(vmem_limit_bytes=VMEM_BYTES),
+        cost_estimate=cost(3.5),
+        name="fill_slots",
+    )(slot_row, rows)
+
+
+def run_middle(mixed, weights, at, rows_in, gain, slot_row, slots):
+    count, width = rows_in.shape
+    whole = lambda i: (0, 0)
+    row_steps = 2 if count % (2 * ROWS) == 0 else 1
+    slot_steps = 2 if slots % 32 == 0 else 1
+    part = pl.BlockSpec((count // row_steps, width), lambda i: (jnp.minimum(i, row_steps - 1), 0))
+    return pl.pallas_call(
+        functools.partial(middle_kernel, row_steps),
+        grid=(row_steps + slot_steps,),
+        in_specs=[
+            part,
+            pl.BlockSpec((width, width), lambda i: (0, at)),
+            part,
+            pl.BlockSpec((1, width), whole),
+            pl.BlockSpec((1, count), whole),
+        ],
+        out_specs=[part, pl.BlockSpec((slots // slot_steps, width), lambda i: (jnp.maximum(i - row_steps, 0), 0))],
+        out_shape=[jax.ShapeDtypeStruct((count, width), f32), jax.ShapeDtypeStruct((slots, width), bf16)],
+        scratch_shapes=[pltpu.VMEM((count, width), bf16)],
+        compiler_params=pltpu.CompilerParams(vmem_limit_bytes=VMEM_BYTES),
+        cost_estimate=cost(5),
+        name="run_middle",
+    )(mixed, weights, rows_in, gain, slot_row)
+
+
+def middle_back_kernel(blocks_ref, slot_ref, rows_ref, gain_ref, top_ref, weight_ref, d_mid_ref, d_attn_ref, d_mixed_ref, d_gain_ref):
+    gain = gain_ref[...]
+    d_normed = read_slots(slot_ref, slice(None), blocks_ref)
+    rows = rows_ref[...]
+    factor = row_factor(rows)
+    normed = rows * factor
+    weighted = d_normed * gain
+    product = d_normed * normed
+    d_mid = top_ref[...].astype(f32) + factor * (weighted - normed * jnp.mean(product * gain, axis=1, keepdims=True))
+    d_mid_ref[...] = d_mid
+    d_attn = d_mid.astype(bf16)
+    d_attn_ref[...] = d_attn
+    d_mixed_ref[...] = dot(d_attn, weight_ref[...], NT).astype(bf16)
+
+    @pl.when(pl.program_id(0) == 0)
+    def _():
+        d_gain_ref[...] = jnp.zeros_like(d_gain_ref)
+
+    d_gain_ref[...] += jnp.sum(product, axis=0, keepdims=True)
+
+
+def run_middle_back(blocks, slot_column, rows, gain, top, weights, at):
+    count, width = rows.shape
+    whole = lambda *_: (0, 0)
+    part = pl.BlockSpec((ROWS, width), lambda i: (i, 0))
+    return pl.pallas_call(
+        middle_back_kernel,
+        grid=(count // ROWS,),
+        in_specs=[
+            pl.BlockSpec(blocks.shape, whole),
+            pl.BlockSpec((ROWS, 1), lambda i: (i, 0)),
+            part,
+            pl.BlockSpec((1, width), whole),
+            part,
+            pl.BlockSpec((width, width), lambda i: (0, at)),
+        ],
+        out_specs=[part, part, part, pl.BlockSpec((1, width), whole)],
+        out_shape=[
+            jax.ShapeDtypeStruct((count, width), f32),
+            jax.ShapeDtypeStruct((count, width), bf16),
+            jax.ShapeDtypeStruct((count, width), bf16),
+            jax.ShapeDtypeStruct((1, width), f32),
+        ],
+        compiler_params=pltpu.CompilerParams(vmem_limit_bytes=VMEM_BYTES),
+        cost_estimate=cost(7),
+        name="run_middle_back",
+    )(blocks, slot_column, rows, gain, top, weights)
+
+
+def first_back_kernel(count, in_ref, gain_ref, d_mid_ref, *refs):
+    d_in_ref = refs[2 * count]
+    total = 0.0
+    for part_ref, weight_ref in zip(refs[:count], refs[count:]):
+        total = total + dot(part_ref[...], weight_ref[:, : part_ref.shape[1]], NT)
+    rows = in_ref[...].astype(f32)
+    factor = row_factor(rows)
+    normed = rows * factor
+    weighted = total * gain_ref[...]
+    d_in_ref[...] = d_mid_ref[...] + factor * (weighted - normed * jnp.mean(weighted * normed, axis=1, keepdims=True))
+
+
+def run_first_back(rows_in, gain, d_mid, parts, weights):
+    count, width = rows_in.shape
+    whole = lambda *_: (0, 0)
+    part = pl.BlockSpec((ROWS, width), lambda i: (i, 0))
+    return pl.pallas_call(
+        functools.partial(first_back_kernel, len(parts)),
+        grid=(count // ROWS,),
+        in_specs=[part, pl.BlockSpec((1, width), whole), part]
+        + [pl.BlockSpec((ROWS, columns.shape[1]), lambda i: (i, 0)) for columns in parts]
+        + [pl.BlockSpec(weight.shape, whole) for weight in weights],
+        out_specs=part,
+        out_shape=jax.ShapeDtypeStruct(rows_in.shape, f32),
+        compiler_params=pltpu.CompilerParams(vmem_limit_bytes=VMEM_BYTES),
+        cost_estimate=cost(8),
+        name="run_first_back",
+    )(rows_in, gain, d_mid, *parts, *weights)
+
+
+def output_kernel(blocks_ref, slot_ref, rows_ref, in_ref, live_ref, out_ref, sums_ref):
+    rows = rows_ref[...]
+    final = rows + read_slots(slot_ref, slice(None), blocks_ref)
+    out_ref[...] = final.astype(bf16)
+    live = live_ref[...]
+    lane = lax.broadcasted_iota(jnp.int32, (1, LANES), 1)
+    sums = jnp.where(lane == 3, jnp.sum(live, axis=0, keepdims=True), 0.0)
+    for i, part in enumerate((in_ref[...].astype(f32), rows, final)):
+        per_row = live * jnp.sum(part * part, axis=1, keepdims=True)
+        sums = jnp.where(lane == i, jnp.sum(per_row, axis=0, keepdims=True), sums)
+
+    @pl.when(pl.program_id(0) == 0)
+    def _():
+        sums_ref[...] = jnp.zeros_like(sums_ref)
+
+    sums_ref[...] += sums
+
+
+def run_output(blocks, slot_column, rows, rows_in, live):
+    count, width = rows.shape
+    whole = lambda *_: (0, 0)
+    part = pl.BlockSpec((ROWS, width), lambda i: (i, 0))
+    column = pl.BlockSpec((ROWS, 1), lambda i: (i, 0))
+    return pl.pallas_call(
+        output_kernel,
+        grid=(count // ROWS,),
+        in_specs=[pl.BlockSpec(blocks.shape, whole), column, part, part, column],
+        out_specs=[part, pl.BlockSpec((1, LANES), whole)],
+        out_shape=[jax.ShapeDtypeStruct((count, width), bf16), jax.ShapeDtypeStruct((1, LANES), f32)],
+        compiler_params=pltpu.CompilerParams(vmem_limit_bytes=VMEM_BYTES),
+        cost_estimate=cost(4),
+        name="run_output",
+    )(blocks, slot_column, rows, rows_in, live)
+
+
+def out_grad_kernel(mixed_ref, d_attn_ref, router_ref, gain_ref, grad_ref):
+    width = mixed_ref.shape[1]
+    grad_ref[:, :width] = dot(mixed_ref[...], d_attn_ref[...], TN)
+    column = jnp.broadcast_to(gain_ref[...], (LANES, width)).T
+    lane = lax.broadcasted_iota(jnp.int32, column.shape, 1)
+    grad_ref[:, width:] = jnp.where(lane == 1, column, router_ref[...])
+
+
+def run_out_grad(mixed, d_attn, grad_router, grad_gain):
+    width = mixed.shape[1]
+    return pl.pallas_call(
+        out_grad_kernel,
+        out_shape=jax.ShapeDtypeStruct((width, width + LANES), f32),
+        compiler_params=pltpu.CompilerParams(vmem_limit_bytes=VMEM_BYTES),
+        cost_estimate=cost(3),
+        name="run_out_grad",
+    )(mixed, d_attn, grad_router, grad_gain)
+
+
+def widen_kernel(*refs):
+    half = len(refs) // 2
+    for in_ref, out_ref in zip(refs[:half], refs[half:]):
+        out_ref[...] = in_ref[...].astype(f32)
+
+
+def widen(*arrays):
+    rows, columns = arrays[0].shape
+    part = pl.BlockSpec((rows // 3, columns), lambda i: (i, 0))
+    return pl.pallas_call(
+        widen_kernel,
+        grid=(3,),
+        in_specs=[part] * len(arrays),
+        out_specs=[part] * len(arrays),
+        out_shape=[jax.ShapeDtypeStruct(array.shape, f32) for array in arrays],
+        cost_estimate=cost(2),
+        name="widen",
+    )(*arrays)
+
+
+def project_kernel(in_ref, gain_ref, weight_ref, packed_ref, normed_ref):
+    rows = in_ref[...].astype(f32)
+    normed = (rows * row_factor(rows) * gain_ref[...]).astype(bf16)
+    normed_ref[...] = normed
+    packed_ref[...] = dot(normed, weight_ref[...], NN).astype(bf16)
+
+
+def run_project(rows_in, gain, weights, columns):
+    count, width = rows_in.shape
+    whole = lambda i: (0, 0)
+    return pl.pallas_call(
+        project_kernel,
+        grid=(count // ROWS,),
+        in_specs=[
+            pl.BlockSpec((ROWS, width), lambda i: (i, 0)),
+            pl.BlockSpec((1, width), whole),
+            pl.BlockSpec((width, columns), whole),
+        ],
+        out_specs=[pl.BlockSpec((ROWS, columns), lambda i: (i, 0)), pl.BlockSpec((ROWS, width), lambda i: (i, 0))],
+        out_shape=[jax.ShapeDtypeStruct((count, columns), bf16), jax.ShapeDtypeStruct((count, width), bf16)],
+        compiler_params=pltpu.CompilerParams(vmem_limit_bytes=VMEM_BYTES),
+        cost_estimate=cost(4),
+        name="run_project",
+    )(rows_in, gain, weights)
+
+
 HIGHEST = lax.Precision.HIGHEST
 SEGMENT_LIMIT = 512
 REACH = (SEGMENT_LIMIT + ROWS - LANES) // LANES
@@ -485,43 +809,52 @@
     return lax.optimization_barrier((value, *earlier))[0]
 
 
-def gather_rows(near):
-    block = near[None]
+def both(mine, other, axis, distance, at=0):
+    high = is_high(axis, distance)
+    return jnp.stack([jnp.where(high, other, mine), jnp.where(high, mine, other)], axis=at)
+
+
+def start_gather(near):
+    return near[None], exchange(near[None], "dp", distances("dp")[0])
+
+
+def finish_gather(terms):
+    block, other = terms
+    shape = block.shape[1:]
     for distance in distances("dp"):
-        other = exchange(block, "dp", distance)
-        high = is_high("dp", distance)
-        block = jnp.stack([jnp.where(high, other, block), jnp.where(high, block, other)], axis=1)
-        block = block.reshape(-1, *near.shape)
-    return block.reshape(-1, near.shape[-1])
-
-
-def near_shards(shard):
-    count = lax.axis_size("expert")
-    return swap_blocks(jnp.broadcast_to(shard[None], (count, *shard.shape)))
+        if other is None:
+            other = exchange(block, "dp", distance)
+        block = both(block, other, "dp", distance, 1).reshape(-1, *shape)
+        other = None
+    return block.reshape(-1, shape[-1])
 
 
 def scatter_dp(rows):
     width = rows.shape[1]
     block = rows.reshape(lax.axis_size("dp"), -1, width)
-    for distance in distances("dp")[::-1]:
+    order = distances("dp")[::-1]
+    for distance in order:
         halves = block.reshape(block.shape[0] // 2, 2, -1, width)
         high = is_high("dp", distance).astype(jnp.int32)
         keep = lax.dynamic_index_in_dim(halves, high, 1, keepdims=False)
         send = lax.dynamic_index_in_dim(halves, 1 - high, 1, keepdims=False)
-        block = keep + exchange(send.astype(bf16), "dp", distance).astype(f32)
-    return block[0].astype(bf16)
-
-
-def scatter_near(rows):
-    parts = swap_blocks(rows.reshape(lax.axis_size("expert"), -1, rows.shape[1]))
-    return jnp.sum(parts.astype(f32), axis=0)
-
-
-def sum_all(rows):
-    for axis in ("dp", "expert"):
-        for distance in distances(axis)[::-1]:
-            rows = rows + exchange(rows, axis, distance)
-    return rows
+        received = exchange(send.astype(bf16), "dp", distance)
+        if distance != order[-1]:
+            block = keep + received.astype(f32)
+    return keep, received
+
+
+def finish_dp(terms):
+    keep, received = terms
+    return (keep + received.astype(f32))[0].astype(bf16)
+
+
+def join(parts):
+    return parts[0] if len(parts) == 1 else jnp.concatenate(parts, axis=0)
+
+
+def near_parts(rows):
+    return swap_blocks(rows.reshape(lax.axis_size("expert"), -1, rows.shape[1]))
 
 
 def gelu_and_slope(values):
@@ -563,171 +896,158 @@
     width = STEP_HEADS * head_dim
     steps = head_count // STEP_HEADS
     groups = [(0, steps - 1), (steps - 1, 1)]
-    one_hot_buckets = (buckets[:, None] == jnp.arange(bucket_count, dtype=jnp.int32)[None, :]).astype(f32)
-    head_bias = jnp.dot(one_hot_buckets, rel_bias, precision=HIGHEST, preferred_element_type=f32).T
-    tiles = toeplitz_tiles(bias_windows(head_bias, REACH))
-    one_hot_windows = bias_windows(one_hot_buckets.T, REACH)
+    small_at = 3 * (steps - 1) * width // LANES
+    out_at = 3 * width // model_width
+
+    bucket_windows = offset_windows(buckets, REACH)
+    one_hot_windows = (bucket_windows[..., None] == jnp.arange(bucket_count, dtype=jnp.int32)).astype(f32)
+    windows = jnp.einsum("gpb,bh->hgp", one_hot_windows, rel_bias, precision=HIGHEST)
+    tiles = toeplitz_tiles(windows)
     all_masks = [mask_columns(segment_ids[seq], valid_mask[seq]) for seq in range(seq_count)]
-    near = []
-    for blocks in spread_shard(
-        qkv_weight, attn_gain, ffn_gain, router_weight, groups, width, lax.axis_size("expert")
-    ):
-        near.append(swap_blocks(after(blocks, *near[-1:])))
-    near[0], tiles, all_masks = lax.optimization_barrier((near[0], tiles, all_masks))
-    gathered = [gather_rows(block) for block in near]
-    w_out = lax.all_gather(out_weight, ("dp", "expert"), axis=0, tiled=True)
-    w_groups = [gathered[g][:, : 3 * many * width] for g, (first, many) in enumerate(groups)]
-    small_all = gathered[0][:, w_groups[0].shape[1] :]
-    gain_one = small_all[:, 0].astype(f32)
-    gain_two = small_all[:, 1].astype(f32)
-
     slot_index = jnp.where(
         dropped.reshape(tokens) == 1, slots, routes.reshape(tokens) * capacity + positions.reshape(tokens)
     )
-    place = (jnp.arange(slots, dtype=jnp.int32)[:, None] == slot_index[None, :]).astype(bf16)
-
-    def fill_slots(rows):
-        return jnp.dot(place, rows, preferred_element_type=f32).astype(bf16)
+    slot_row, slot_column = slot_index.reshape(1, tokens), slot_index.reshape(tokens, 1)
+    live = valid_mask.reshape(tokens, 1).astype(f32)
+    rows_in = inputs.reshape(tokens, model_width)
+    top = cotangent.reshape(tokens, model_width)
 
     def send_slots(rows):
         return swap_blocks(rows.reshape(experts, capacity, model_width)).reshape(slots, model_width)
 
-    def read_slots(rows):
-        return lax.dot_general(place, rows, (((0,), (0,)), ((), ())), preferred_element_type=f32)
-
-    layer_in = inputs.astype(f32)
-
-    saved = []
-    for seq in range(seq_count):
-        factor = norm_factor(layer_in[seq])
-        normed = (layer_in[seq] * factor * gain_one).astype(bf16)
-        masks = all_masks[seq]
-        bounds = tile_bounds(segment_ids[seq])
-        packs, lses = [], []
-        mixed = jnp.zeros((seq_length, model_width), bf16)
-        for g, (first, many) in enumerate(groups):
-            packed = jnp.dot(normed, w_groups[g], preferred_element_type=f32).astype(bf16)
-            mixed, lse = attend_forward(packed, *masks, bounds, tiles, mixed, first, head_dim)
-            packs.append(packed)
-            lses.append(lse)
-        attn_out = jnp.dot(mixed, w_out, preferred_element_type=f32)
-        saved.append((factor, normed, masks, bounds, packs, lses, mixed, attn_out))
-    d_final_rows = send_slots(fill_slots(after(cotangent.reshape(tokens, model_width), saved[0][5][0], near[-1])))
-    mid_rows = (layer_in + jnp.stack([state[-1] for state in saved])).reshape(tokens, model_width)
-    mid_factor = norm_factor(mid_rows)
-    mid_normed = mid_rows * mid_factor
-    ffn_normed = (mid_normed * gain_two).astype(bf16)
-    filled = fill_slots(ffn_normed)
+    near, rest = spread_shard(
+        qkv_weight, out_weight, attn_gain, ffn_gain, router_weight, width, steps - 1, lax.axis_size("expert")
+    )
+    near = swap_blocks(near)
+    near, rest, tiles, all_masks = lax.optimization_barrier((near, rest, tiles, all_masks))
+    rest = swap_blocks(rest)
+    filled_cotangent = fill_slots(slot_row, top, slots)
+    terms = start_gather(near)
+    terms, filled_cotangent, rest = lax.optimization_barrier((terms, filled_cotangent, rest))
+    weights = [finish_gather(terms)]
+    small = weights[0][:, small_at * LANES : small_at * LANES + SMALL_GAINS].astype(f32)
+    gain_one, gain_two = small[:, 0][None], small[:, 1][None]
+
+    bounds = [tile_bounds(segment_ids[seq]) for seq in range(seq_count)]
+    packs, lses = [], []
+    mixes = [None] * seq_count
+    for g, (first, many) in enumerate(groups):
+        if g == 0:
+            packed, normed = run_project(rows_in, gain_one, weights[0], 3 * many * width)
+        else:
+            packed = jnp.dot(normed, weights[g][:, : 3 * many * width], preferred_element_type=f32).astype(bf16)
+        packs.append([packed[seq * seq_length : (seq + 1) * seq_length] for seq in range(seq_count)])
+        if g == 0:
+            terms = start_gather(rest)
+            packs[0], filled_cotangent = lax.optimization_barrier((packs[0], filled_cotangent))
+            d_final_rows = send_slots(filled_cotangent)
+        lses.append([])
+        for seq in range(seq_count):
+            mixes[seq], lse = attend_forward(
+                packs[g][seq], *all_masks[seq], bounds[seq], tiles, mixes[seq], first, head_dim
+            )
+            lses[g].append(lse)
+        if g == 0:
+            terms, mixes, lses = lax.optimization_barrier((terms, mixes, lses))
+            weights.append(finish_gather(terms))
+    mixed = join(mixes)
+    mixed, d_final_rows = lax.optimization_barrier((mixed, d_final_rows))
+    mid_rows, filled = run_middle(mixed, weights[1], out_at, rows_in, gain_two, slot_row, slots)
     slot_rows = send_slots(filled)
 
     w_in, w_back = expert_in[0], expert_out[0]
     d_hidden = dot(after(d_final_rows, filled), w_back, NT).astype(bf16)
     slot_rows, d_hidden = lax.optimization_barrier((slot_rows, d_hidden))
-    hidden, d_pre, d_rows, d_logits, gate = run_expert(me, slot_rows, w_in, small_all, d_hidden, experts)
+    hidden, d_pre, d_rows, d_logits, gate = run_expert(me, slot_rows, w_in, weights[0], small_at, d_hidden, experts)
     d_returned = send_slots(d_rows)
 
-    moe_rows = (gate * dot(hidden, w_back, NN)).astype(bf16)
-    d_slot_out = (gate * d_final_rows.astype(f32)).astype(bf16)
-    grad_router = dot(slot_rows, d_logits, TN)[:, SMALL_GAINS : SMALL_GAINS + experts]
-    part_in = dot(slot_rows, d_pre, TN).astype(bf16)
-    part_out = dot(hidden, d_slot_out, TN).astype(bf16)
-    grad_expert_in = lax.psum_scatter(part_in, "dp", scatter_dimension=1, tiled=True).astype(f32)[None]
-    grad_expert_out = lax.psum_scatter(part_out, "dp", scatter_dimension=0, tiled=True).astype(f32)[None]
-    d_returned, moe_rows, part_in, part_out = lax.optimization_barrier((d_returned, moe_rows, part_in, part_out))
-    d_normed = read_slots(d_returned)
+    part_in, part_out, moe_rows, grad_router = expert_grads(
+        gate, slot_rows, hidden, d_pre, d_final_rows, w_back, d_logits
+    )
+    d_returned, moe_rows, part_in, part_out, grad_router = lax.optimization_barrier(
+        (d_returned, moe_rows, part_in, part_out, grad_router)
+    )
+    grad_expert_in = lax.psum_scatter(part_in, "dp", scatter_dimension=1, tiled=True)
+    grad_expert_out = lax.psum_scatter(part_out, "dp", scatter_dimension=0, tiled=True)
+    d_mid, d_attn, d_mixed, grad_gain_two = run_middle_back(
+        d_returned, slot_column, mid_rows, gain_two, top, weights[1], out_at
+    )
     moe_returned = send_slots(moe_rows)
-    moe = read_slots(moe_returned)
-
-    final_rows = mid_rows + moe
-    output = final_rows.astype(bf16).reshape(inputs.shape)
-    live_rows = valid_mask.reshape(tokens, 1).astype(f32)
-    flat_in = layer_in.reshape(tokens, model_width)
-    sums = jnp.stack(
-        [jnp.sum(live_rows * rows * rows) for rows in (flat_in, mid_rows, final_rows)] + [jnp.sum(live_rows)]
-    )
-
-    weighted = d_normed * gain_two
-    grad_gain_two = jnp.sum(d_normed * mid_normed, axis=0)
-    d_mid = cotangent.astype(f32).reshape(tokens, model_width) + mid_factor * (
-        weighted - mid_normed * jnp.mean(weighted * mid_normed, axis=-1, keepdims=True)
-    )
-    d_attn = d_mid.astype(bf16)
-    d_mixed = dot(d_attn, w_out, NT).astype(bf16)
-    mixed_all = jnp.concatenate([state[6] for state in saved], axis=0)
-    grad_out = dot(mixed_all, d_attn, TN)
-    out_half = scatter_dp(grad_out)
-
-    diagonals, grad_groups, halves, dense_qkv = [], [], [], []
-    d_normed_one = [jnp.zeros((seq_length, model_width), f32)] * seq_count
+
+    grad_out = run_out_grad(mixed, d_attn, grad_router, grad_gain_two)
+    diagonals, all_parts, near_terms = [], [], []
+    terms, waits = scatter_dp(grad_out), [moe_returned]
     for g, (first, many) in enumerate(groups):
-        if g:
-            d_mixed, out_half, moe_returned = lax.optimization_barrier((d_mixed, out_half, moe_returned))
-            dense_out = scatter_near(out_half)
-        grad_group, diagonal = None, None
+        parts, diagonal = [], None
         for seq in range(seq_count):
-            factor, normed, masks, bounds, packs, lses, mixed, unused = saved[seq]
-            parts, diagonal_seq = attend_backward(
-                packs[g],
-                d_mixed[seq * seq_length : (seq + 1) * seq_length],
-                mixed,
-                lses[g],
-                *masks,
-                bounds,
-                tiles,
-                first,
-                head_dim,
+            at = slice(seq * seq_length, (seq + 1) * seq_length)
+            part, here = attend_backward(
+                packs[g][seq], d_mixed[at], mixed[at], lses[g][seq], *all_masks[seq], bounds[seq], tiles, first, head_dim
             )
-            if g:
-                parts, dense_out, halves[0] = lax.optimization_barrier((parts, dense_out, halves[0]))
-            here = dot(normed, parts, TN)
+            parts.append(part)
+            diagonal = here if diagonal is None else diagonal + here
+        parts, diagonal, terms, waits = lax.optimization_barrier((parts, diagonal, terms, waits))
+        if g == 0:
+            moe_returned = waits[0]
+        else:
+            near_terms.append(waits[0])
+        diagonals.append(diagonal)
+        all_parts.append(join(parts))
+        half = finish_dp(terms)
+        grad_group = None
+        for seq in range(seq_count):
+            here = dot(normed[seq * seq_length : (seq + 1) * seq_length], parts[seq], TN)
             grad_group = here if grad_group is None else grad_group + here
-            diagonal = diagonal_seq if diagonal is None else diagonal + diagonal_seq
-            d_normed_one[seq] = d_normed_one[seq] + dot(parts, w_groups[g], NT)
-        diagonals.append(diagonal)
-        halves.append(scatter_dp(grad_group))
-    grad_parts = []
-    for g, (first, many) in enumerate(groups):
-        total = scatter_near(halves[g])
-        grad_parts.append(total.reshape(-1, many, 3, width))
+        waits = [near_parts(half)]
+        terms = scatter_dp(grad_group)
+        if g < len(groups) - 1:
+            output, sums = run_output(moe_returned, slot_column, mid_rows, rows_in, live)
+            d_mixed = after(d_mixed, half, output)
+    all_parts = lax.optimization_barrier((all_parts, terms[0]))[0]
+    input_grad = run_first_back(rows_in, gain_one, d_mid, all_parts, weights)
+    input_grad, terms, waits = lax.optimization_barrier((input_grad, terms, waits))
+    near_terms.append(waits[0])
+    grad_expert_in, grad_expert_out = widen(grad_expert_in, grad_expert_out)
+    grad_rel = jnp.einsum("hgp,gpb->bh", jnp.concatenate(diagonals, axis=0), one_hot_windows, precision=HIGHEST)
+
+    tail = jnp.concatenate([grad_rel.reshape(-1), sums[0, :4]])
+    tail_size = tail.shape[0]
+    tail = jnp.pad(tail, (0, -tail_size % model_width)).reshape(-1, model_width)
+    for distance in distances("dp")[::-1]:
+        tail = tail + exchange(tail, "dp", distance)
+    pieces = []
+    for unused in range(3):
+        pieces.append(tail.astype(bf16))
+        tail = tail - pieces[-1].astype(f32)
+    receivers = lax.axis_size("expert")
+    half = finish_dp(terms).reshape(receivers, -1, 3 * width)
+    own_rows = half.shape[1]
+    half = jnp.concatenate([half] + [jnp.broadcast_to(piece[None], (receivers, *piece.shape)) for piece in pieces], axis=1)
+    last_near, grad_expert_in, grad_expert_out = lax.optimization_barrier(
+        (swap_blocks(half), grad_expert_in, grad_expert_out)
+    )
+    near_terms.append(last_near[:, :own_rows])
+    tail = jnp.sum(last_near[:, own_rows:].astype(f32), axis=0).reshape(3, -1)
+    tail = (tail[0] + tail[1]) + tail[2]
+    grad_rel = tail[: bucket_count * head_count].reshape(bucket_count, head_count)
+    totals = tail[bucket_count * head_count : tail_size]
+    stats = jnp.sqrt(totals[:3] / (totals[3] * model_width))
+
+    dense_out, *dense_qkv = [jnp.sum(block.astype(f32), axis=0) for block in near_terms]
+    grad_parts = [total.reshape(-1, many, 3, width) for total, (first, many) in zip(dense_qkv, groups)]
     grad_qkv = jnp.concatenate(grad_parts, axis=1).transpose(0, 2, 1, 3).reshape(-1, 3 * model_width)
     grad_gain_one = jnp.sum(grad_qkv * qkv_weight.astype(f32), axis=1) / attn_gain.astype(f32)
-
-    input_grads = []
-    for seq in range(seq_count):
-        factor = saved[seq][0]
-        normed_in = layer_in[seq] * factor
-        weighted = d_normed_one[seq] * gain_one
-        input_grads.append(
-            d_mid[seq * seq_length : (seq + 1) * seq_length]
-            + factor * (weighted - normed_in * jnp.mean(weighted * normed_in, axis=-1, keepdims=True))
-        )
-    input_grad = jnp.stack(input_grads)
-
-    grad_rel = jnp.einsum("hgp,bgp->bh", jnp.concatenate(diagonals, axis=0), one_hot_windows, precision=HIGHEST)
-    shares = [grad_rel, grad_gain_two, grad_router, sums]
-    tail = jnp.concatenate([share.reshape(-1) for share in shares])
-    tail = jnp.pad(tail, (0, -tail.shape[0] % (8 * LANES))).reshape(-1, LANES)
-    tail = sum_all(tail).reshape(-1)
-    ends = [0]
-    for share in shares:
-        ends.append(ends[-1] + share.size)
-    grad_rel, grad_gain_two, grad_router, totals = [
-        tail[ends[i] : ends[i + 1]].reshape(share.shape) for i, share in enumerate(shares)
-    ]
-    stats = jnp.sqrt(totals[:3] / (totals[3] * model_width))
-    own_rows = attn_gain.shape[0]
-    own_first = (lax.axis_index("dp") * lax.axis_size("expert") + me) * own_rows
     return (
-        output,
-        input_grad,
+        output.reshape(inputs.shape),
+        input_grad.reshape(inputs.shape),
         grad_gain_one,
         grad_qkv,
-        dense_out,
-        lax.dynamic_slice_in_dim(grad_gain_two, own_first, own_rows),
-        lax.dynamic_slice_in_dim(grad_router, own_first, own_rows),
+        dense_out[:, :model_width],
+        dense_out[:, model_width + 1],
+        dense_out[:, model_width + SMALL_GAINS : model_width + SMALL_GAINS + experts],
         grad_rel,
-        grad_expert_in,
-        grad_expert_out,
+        grad_expert_in[None],
+        grad_expert_out[None],
         stats,
     )
 

time: 512 us -> 438 us (0.86)
  Pallas kernels: 106 us -> 221 us
  matrix products: 98.1 us -> 22.8 us
  waiting for transfers between devices: 125 us -> 78.4 us
  starting transfers between devices: 81 us -> 51.4 us
  local copies, waits for them, and re-layouts: 39.8 us -> 22.8 us
  other arithmetic: 35 us -> 18.8 us
    pallas_call x1 -> x10, Pallas kernels: 1.9 us -> 86.4 us  [the longest x1 26.9 us: expert_grads(): pl.pallas_call(expert_grads_kernel, grid=(hidden_width // block,), in_spe...]
    dot_general x10 -> x3, matrix products: 64.8 us -> 19.7 us  [dot(): return lax.dot_general(left, right, dims, preferred_element_type=f32)]
    ppermute x15 -> x12, waiting for transfers between devices: 44.6 us -> 11.3 us  [exchange(): lax.ppermute(rows, axis, [(i, i ^ distance) for i in range(lax.axis_size(...]
    dot_general x9 -> x3, matrix products: 32.5 us -> 3.11 us  [the longest x1 2.54 us: body(): jnp.dot(normed, weights[g][:, :3 * many * width], preferred_element_type=...]
    ppermute x15 -> x12, starting transfers between devices: 32.2 us -> 6.76 us  [exchange(): lax.ppermute(rows, axis, [(i, i ^ distance) for i in range(lax.axis_size(...]
    unnamed x175 -> x60, local copies, waits for them, and re-layouts: 30.3 us -> 11.1 us
    pallas_call x2, Pallas kernels: 21.7 us -> 36.8 us  [attend_forward(): pl.pallas_call(functools.partial(forward_kernel, head_dim, reach), grid_s...]
    pallas_call x2, Pallas kernels: 48.9 us -> 63.3 us  [attend_backward(): pl.pallas_call(functools.partial(backward_kernel, head_dim, reach), grid_...]
  transfers between devices with their start and end apart: 27 -> 23, of which waited for: 13 -> 8; matrix products, arithmetic and copies ran while one was open for 31% -> 12% of each run, Pallas kernels for 16% -> 43%
where the time goes in v3:
time: 438 us; the launch traced here: 431 us
  Pallas kernels  221 us (50%)
  waiting for transfers between devices  78.4 us (18%)
  starting transfers between devices  51.4 us (12%)
  local copies, waits for them, and re-layouts  22.8 us (5%)
  matrix products  22.8 us (5%)
  other arithmetic  18.8 us (4%)
  between operations  15.9 us (4%)
    all_to_all x9, waiting for transfers between devices, swap_blocks(): lax.all_to_all(blocks, 'expert', split_axis=0, concat_axis=0, tiled=True)  66.6 us
    pallas_call x2, Pallas kernels, attend_backward(): pl.pallas_call(functools.partial(backward_kernel, head_dim, reach), grid_...  63.3 us
    all_to_all x9, starting transfers between devices, swap_blocks(): lax.all_to_all(blocks, 'expert', split_axis=0, concat_axis=0, tiled=True)  44.1 us
    pallas_call x2, Pallas kernels, attend_forward(): pl.pallas_call(functools.partial(forward_kernel, head_dim, reach), grid_s...  36.8 us
    pallas_call x1, Pallas kernels, expert_grads(): pl.pallas_call(expert_grads_kernel, grid=(hidden_width // block,), in_spe...  26.9 us
    pallas_call x1, Pallas kernels, run_expert(): pl.pallas_call(functools.partial(expert_kernel, experts), grid_spec=grid_...  24.9 us
    dot_general x3, matrix products, dot(): return lax.dot_general(left, right, dims, preferred_element_type=f32)  19.7 us
    pallas_call x1, Pallas kernels, run_middle_back(): pl.pallas_call(middle_back_kernel, grid=(count // ROWS,), in_specs=[pl.Bl...  11.4 us
  transfers between devices with their start and end apart: 23, of which 8 were waited for; matrix products, arithmetic and copies ran while one was open for 12% of the time, Pallas kernels for 43%

profile of v3, /device:TPU:0, one launch (start us, length us, event | category | flops | bytes accessed | tf_op | source)
XLA Modules:
  0.0 431.2 jit_solution(279497619909109017)
XLA Ops:
  10.6 7.4 %all-to-all-start = ((bf16[8,24,1664]{2,1,0:T(8,128)(2,1)}), bf16[8,24,1664]{2,1,0:T(8,128)(2,1)S(1)}, u32[]{:S(2)}, u32[]{:S(2)}) async-start(bf16[8,24,1664]{2,1,0:T(8,128)(2,1)} %get-tuple-element.87), calls=%async_computation | async-start | bytes 1277952 | tf_op jit(solution)/shard_map/all_to_all | solution.py:805
  23.0 9.6 %toeplitz_tiles.1.bias_ref = f32[12,1408,128]{2,1,0:T(8,128)} custom-call(f32[12,11,256]{2,1,0:T(8,128)} %bitcast.137), custom_call_target="tpu_custom_call" | custom-call | flops 9900000256 | tf_op jit(solution)/shard_map/toeplitz_tiles/pallas_call | solution.py:50
  40.7 4.9 %fill_slots.1 = bf16[1280,768]{1,0:T(8,128)(2,1)} custom-call(s32[1,1024]{1,0:T(1,128)} %compare_select_fusion.slot_ref, bf16[1024,768]{1,0:T(8,128)(2,1)} %bitcast.157), custom_call_target="tpu_custom_call" | custom-call | flops 3849999872 | tf_op jit(solution)/shard_map/fill_slots/pallas_call | solution.py:570
  45.6 9.0 %collective-permute-done = bf16[1,8,24,1664]{3,2,1,0:T(8,128)(2,1)S(1)} collective-permute-done((bf16[1,8,24,1664]{3,2,1,0:T(8,128)(2,1)S(1)}, bf16[1,8,24,1664]{3,2,1,0:T(8,128)(2,1)S(1)}, u32[]{:S(2)}, u32[]{:S(2)}) %collective-permute-start) | collective-permute-done | bytes 639008 | tf_op jit(solution)/shard_map/ppermute | solution.py:797
  61.4 6.6 %run_project.1 = (bf16[1024,1536]{1,0:T(8,128)(2,1)}, bf16[1024,768]{1,0:T(8,128)(2,1)}) custom-call(bf16[1024,768]{1,0:T(8,128)(2,1)} %bitcast.159, f32[1,768]{1,0:T(1,128)} %broadcast_in_dim_squeeze.7.gain_ref, bf16[768,1664]{1,0:T(8,128)(2,1)} %bitcast.113), custom_call_target="tpu_custom_call" | custom-call | flops 4400000000 | tf_op jit(solution)/shard_map/run_project/pallas_call | solution.py:767
  68.0 6.3 %all-to-all-start.2 = ((bf16[8,160,768]{2,1,0:T(8,128)(2,1)}), bf16[8,160,768]{2,1,0:T(8,128)(2,1)}, u32[]{:S(2)}, u32[]{:S(2)}) async-start(bf16[8,160,768]{2,1,0:T(8,128)(2,1)} %bitcast.124), calls=%async_computation.2 | async-start | bytes 3932160 | tf_op jit(solution)/shard_map/all_to_all | solution.py:805
  74.8 23.2 %attend_forward.2 = (bf16[1024,768]{1,0:T(8,128)(2,1)}, f32[2,4,1024]{2,1,0:T(4,128)}) custom-call(s32[4]{0:T(128)} %get-tuple-element.272.low_ref, s32[4]{0:T(128)} %get-tuple-element.271.high_ref, bf16[1024,1536]{1,0:T(8,128)(2,1)} %get-tuple-element.95.q_ref.k_ref.v_ref, bf16[1024,1536]{1,0:T(8,128)(2,1)} %get-tuple-element.95.q_ref.k_ref.v_ref, ...), custom_call_target="tpu_custom_call" | custom-call | flops 1100000000 | tf_op jit(solution)/shard_map/attend_forward/pallas_call | solution.py:285
  107.3 13.5 %attend_forward.3 = (bf16[1024,768]{1,0:T(8,128)(2,1)}, f32[1,4,1024]{2,1,0:T(4,128)}) custom-call(s32[4]{0:T(128)} %get-tuple-element.272.low_ref, s32[4]{0:T(128)} %get-tuple-element.271.high_ref, bf16[1024,768]{1,0:T(8,128)(2,1)} %convolution_convert_fusion.1.q_ref.k_ref.v_ref, ...), custom_call_target="tpu_custom_call", output_to_operand_aliasing={{0}: (8, {})} | custom-call | flops 1100000000 | tf_op jit(solution)/shard_map/attend_forward/pallas_call | solution.py:285
  120.8 7.7 %run_middle.1 = (f32[1024,768]{1,0:T(8,128)}, bf16[1280,768]{1,0:T(8,128)(2,1)}) custom-call(bf16[1024,768]{1,0:T(8,128)(2,1)} %get-tuple-element.108.mixed_ref.mix_ref, bf16[768,1536]{1,0:T(8,128)(2,1)} %bitcast.121, bf16[1024,768]{1,0:T(8,128)(2,1)} %bitcast.160, f32[1,768]{1,0:T(1,128)} %broadcast_in_dim_squeeze.8.gain_ref, ...), custom_call_target="tpu_custom_call" | custom-call | flops 5500000256 | tf_op jit(solution)/shard_map/run_middle/pallas_call | solution.py:585
  128.6 5.3 %all-to-all-start.3 = ((bf16[8,160,768]{2,1,0:T(8,128)(2,1)}), bf16[8,160,768]{2,1,0:T(8,128)(2,1)S(1)}, u32[]{:S(2)}, u32[]{:S(2)}) async-start(bf16[8,160,768]{2,1,0:T(8,128)(2,1)} %bitcast.130), calls=%async_computation.3 | async-start | bytes 3932160 | tf_op jit(solution)/shard_map/all_to_all | solution.py:805
  133.9 11.1 %convolution_convert_fusion.d_hidden_ref = bf16[1280,3072]{1,0:T(8,128)(2,1)} fusion(bf16[1280,768]{1,0:T(8,128)(2,1)} %bitcast.36.d_slots_ref, bf16[1,3072,768]{2,1,0:T(8,128)(2,1)} %param.25), kind=kOutput, calls=%fused_computation | convolution fusion | flops 6043729920 | bytes 14548992 | tf_op jit(solution)/shard_map/dot_general | solution.py:28
  145.0 35.0 %all-to-all-done.3 = bf16[8,160,768]{2,1,0:T(8,128)(2,1)S(1)} async-done(((bf16[8,160,768]{2,1,0:T(8,128)(2,1)}), bf16[8,160,768]{2,1,0:T(8,128)(2,1)S(1)}, u32[]{:S(2)}, u32[]{:S(2)}) %all-to-all-start.3) | async-done | bytes 1966112 | tf_op jit(solution)/shard_map/all_to_all | solution.py:805
  181.2 24.9 %run_expert.1 = (bf16[1280,3072]{1,0:T(8,128)(2,1)}, bf16[1280,3072]{1,0:T(8,128)(2,1)}, bf16[1280,768]{1,0:T(8,128)(2,1)}, bf16[1280,128]{1,0:T(8,128)(2,1)}, f32[1280,1]{1,0:T(8,128)}) custom-call(s32[1]{0:T(128)} %bitcast.27.me_ref, bf16[1280,768]{1,0:T(8,128)(2,1)} %bitcast.127, bf16[768,3072]{1,0:T(8,128)(2,1)} %bitcast.155, ...), custom_call_target="tpu_custom_call" | custom-call | flops 27499999232 | tf_op jit(solution)/shard_map/run_expert/pallas_call | solution.py:454
  210.1 26.9 %expert_grads.1 = (bf16[768,3072]{1,0:T(8,128)(2,1)}, bf16[3072,768]{1,0:T(8,128)(2,1)}, bf16[1280,768]{1,0:T(8,128)(2,1)}, f32[768,128]{1,0:T(8,128)}) custom-call(f32[1280,1]{1,0:T(8,128)} %get-tuple-element.115.gate_ref, bf16[1280,768]{1,0:T(8,128)(2,1)} %bitcast.128, bf16[1280,3072]{1,0:T(8,128)(2,1)} %get-tuple-element.116.hidden_ref, ...), custom_call_target="tpu_custom_call" | custom-call | flops 29699999744 | tf_op jit(solution)/shard_map/expert_grads/pallas_call | solution.py:498
  236.9 18.5 %all-to-all-done.4 = bf16[8,160,768]{2,1,0:T(8,128)(2,1)S(1)} async-done(((bf16[8,160,768]{2,1,0:T(8,128)(2,1)}), bf16[8,160,768]{2,1,0:T(8,128)(2,1)S(1)}, u32[]{:S(2)}, u32[]{:S(2)}) %all-to-all-start.4) | async-done | bytes 1966112 | tf_op jit(solution)/shard_map/all_to_all | solution.py:805
  257.8 11.4 %run_middle_back.1 = (f32[1024,768]{1,0:T(8,128)}, bf16[1024,768]{1,0:T(8,128)(2,1)}, bf16[1024,768]{1,0:T(8,128)(2,1)}, f32[1,768]{1,0:T(1,128)}) custom-call(bf16[1280,768]{1,0:T(8,128)(2,1)} %bitcast.126, s32[1024,1]{1,0:T(8,128)} %copy.101.slot_ref, f32[1024,768]{1,0:T(8,128)} %get-tuple-element.124.rows_ref, f32[1,768]{1,0:T(1,128)} %broadcast_in_dim_squeeze.8.gain_ref, ...), custom_call_target="tpu_custom_call" | custom-call | flops 7699999744 | tf_op jit(solution)/shard_map/run_middle_back/pallas_call | solution.py:629
  269.2 5.0 %run_out_grad.1 = f32[768,896]{1,0:T(8,128)} custom-call(bf16[1024,768]{1,0:T(8,128)(2,1)} %get-tuple-element.108.mixed_ref.mix_ref, bf16[1024,768]{1,0:T(8,128)(2,1)} %get-tuple-element.129.d_attn_ref, f32[768,128]{1,0:T(8,128)} %get-tuple-element.130.router_ref, f32[1,768]{1,0:T(1,128)} %get-tuple-element.131.gain_ref), custom_call_target="tpu_custom_call" | custom-call | flops 3300000000 | tf_op jit(solution)/shard_map/run_out_grad/pallas_call | solution.py:728
  282.4 40.9 %attend_backward.2 = (bf16[1024,1536]{1,0:T(8,128)(2,1)}, f32[8,11,256]{2,1,0:T(8,128)}) custom-call(s32[4]{0:T(128)} %get-tuple-element.272.low_ref, s32[4]{0:T(128)} %get-tuple-element.271.high_ref, bf16[1024,1536]{1,0:T(8,128)(2,1)} %get-tuple-element.95.q_ref.k_ref.v_ref, bf16[1024,1536]{1,0:T(8,128)(2,1)} %get-tuple-element.95.q_ref.k_ref.v_ref, ...), custom_call_target="tpu_custom_call" | custom-call | flops 44000002048 | tf_op jit(solution)/shard_map/attend_backward/pallas_call | solution.py:332
  325.5 5.7 %fusion.27 = f32[768,1536]{1,0:T(8,128)S(1)} fusion(bf16[1024,768]{1,0:T(8,128)(2,1)} %get-tuple-element.96, bf16[1024,1536]{1,0:T(8,128)(2,1)} %get-tuple-element.144.refs_0_), kind=kOutput, calls=%fused_computation.122 | convolution fusion | flops 2415919104 | bytes 9437184 | tf_op jit(solution)/shard_map/dot_general | solution.py:28
  334.8 7.4 %run_output.1 = (bf16[1024,768]{1,0:T(8,128)(2,1)}, f32[1,128]{1,0:T(1,128)}) custom-call(bf16[1280,768]{1,0:T(8,128)(2,1)} %bitcast.125, s32[1024,1]{1,0:T(8,128)} %copy.101.slot_ref, f32[1024,768]{1,0:T(8,128)} %get-tuple-element.124.rows_ref, bf16[1024,768]{1,0:T(8,128)(2,1)} %bitcast.161, f32[1024,1]{1,0:T(8,128)} %copy.103.live_ref), custom_call_target="tpu_custom_call" | custom-call | flops 4400000000 | tf_op jit(solution)/shard_map/run_output/pallas_call | solution.py:706
  351.6 22.4 %attend_backward.3 = (bf16[1024,768]{1,0:T(8,128)(2,1)}, f32[4,11,256]{2,1,0:T(8,128)}) custom-call(s32[4]{0:T(128)} %get-tuple-element.272.low_ref, s32[4]{0:T(128)} %get-tuple-element.271.high_ref, bf16[1024,768]{1,0:T(8,128)(2,1)} %convolution_convert_fusion.1.q_ref.k_ref.v_ref, bf16[1024,768]{1,0:T(8,128)(2,1)} %convolution_convert_fusion.1.q_ref.k_ref.v_ref, ...), custom_call_target="tpu_custom_call" | custom-call | flops 22000001024 | tf_op jit(solution)/shard_map/attend_backward/pallas_call | solution.py:332
  381.3 6.5 %all-to-all-start.7 = ((bf16[8,24,1536]{2,1,0:T(8,128)(2,1)}), bf16[8,24,1536]{2,1,0:T(8,128)(2,1)S(1)}, u32[]{:S(2)}, u32[]{:S(2)}) async-start(bf16[8,24,1536]{2,1,0:T(8,128)(2,1)} %bitcast.58), calls=%async_computation.7 | async-start | bytes 1179648 | tf_op jit(solution)/shard_map/all_to_all | solution.py:805
  390.0 10.3 %run_first_back.1 = f32[1024,768]{1,0:T(8,128)} custom-call(bf16[1024,768]{1,0:T(8,128)(2,1)} %bitcast.162, f32[1,768]{1,0:T(1,128)} %broadcast_in_dim_squeeze.7.gain_ref, f32[1024,768]{1,0:T(8,128)} %get-tuple-element.135.d_mid_ref, bf16[1024,1536]{1,0:T(8,128)(2,1)} %get-tuple-element.144.refs_0_, bf16[1024,768]{1,0:T(8,128)(2,1)} %get-tuple-element.145.refs_1_, ...), custom_call_target="tpu_custom_call" | custom-call | flops 8800000000 | tf_op jit(solution)/shard_map/run_first_back/pallas_call | solution.py:669
  414.9 5.3 %all-to-all-done.8 = bf16[8,27,768]{2,1,0:T(8,128)(2,1)S(1)} async-done(((bf16[8,27,768]{2,1,0:T(8,128)(2,1)}), bf16[8,27,768]{2,1,0:T(8,128)(2,1)S(1)}, u32[]{:S(2)}, u32[]{:S(2)}) %all-to-all-start.8) | async-done | bytes 331808 | tf_op jit(solution)/shard_map/all_to_all | solution.py:805
  (200 shorter events, 90.5 us)
Async XLA Ops:
  10.6 24.4 %all-to-all-start = ((bf16[8,24,1664]{2,1,0:T(8,128)(2,1)}), bf16[8,24,1664]{2,1,0:T(8,128)(2,1)S(1)}, u32[]{:S(2)}, u32[]{:S(2)}) async-start(bf16[8,24,1664]{2,1,0:T(8,128)(2,1)} %get-tuple-element.87), calls=%async_computation | async-start | bytes 1277952 | tf_op jit(solution)/shard_map/all_to_all | solution.py:805
  35.0 19.7 %all-to-all-start.1 = ((bf16[8,24,1536]{2,1,0:T(8,128)(2,1)}), bf16[8,24,1536]{2,1,0:T(8,128)(2,1)S(1)}, u32[]{:S(2)}, u32[]{:S(2)}) async-start(bf16[8,24,1536]{2,1,0:T(8,128)(2,1)} %get-tuple-element.90), calls=%async_computation.1 | async-start | bytes 1179648 | tf_op jit(solution)/shard_map/all_to_all | solution.py:805
  38.6 16.0 %collective-permute-start = (bf16[1,8,24,1664]{3,2,1,0:T(8,128)(2,1)S(1)}, bf16[1,8,24,1664]{3,2,1,0:T(8,128)(2,1)S(1)}, u32[]{:S(2)}, u32[]{:S(2)}) collective-permute-start(bf16[1,8,24,1664]{3,2,1,0:T(8,128)(2,1)S(1)} %bitcast.116), channel_id=1, source_target_pairs={{0,16},{8,24},{16,0},{24,8},{1,17},{9,25},{17,1},{25,9},{2,18},{10... | collective-permute-start | bytes 1916936 | tf_op jit(solution)/shard_map/ppermute | solution.py:797
  56.0 3.2 collective-permute-start.1
  57.7 40.4 %collective-permute-start.2 = (bf16[1,8,24,1536]{3,2,1,0:T(8,128)(2,1)S(1)}, bf16[1,8,24,1536]{3,2,1,0:T(8,128)(2,1)}, u32[]{:S(2)}, u32[]{:S(2)}) collective-permute-start(bf16[1,8,24,1536]{3,2,1,0:T(8,128)(2,1)S(1)} %bitcast.118), channel_id=1, source_target_pairs={{0,16},{8,24},{16,0},{24,8},{1,17},{9,25},{17,1},{25,9},{2,18},{10... | collective-permute-start | bytes 1769480 | tf_op jit(solution)/shard_map/ppermute | solution.py:797
  68.0 52.8 %all-to-all-start.2 = ((bf16[8,160,768]{2,1,0:T(8,128)(2,1)}), bf16[8,160,768]{2,1,0:T(8,128)(2,1)}, u32[]{:S(2)}, u32[]{:S(2)}) async-start(bf16[8,160,768]{2,1,0:T(8,128)(2,1)} %bitcast.124), calls=%async_computation.2 | async-start | bytes 3932160 | tf_op jit(solution)/shard_map/all_to_all | solution.py:805
  99.3 2.9 collective-permute-start.3
  128.6 51.4 %all-to-all-start.3 = ((bf16[8,160,768]{2,1,0:T(8,128)(2,1)}), bf16[8,160,768]{2,1,0:T(8,128)(2,1)S(1)}, u32[]{:S(2)}, u32[]{:S(2)}) async-start(bf16[8,160,768]{2,1,0:T(8,128)(2,1)} %bitcast.130), calls=%async_computation.3 | async-start | bytes 3932160 | tf_op jit(solution)/shard_map/all_to_all | solution.py:805
  206.2 49.3 %all-to-all-start.4 = ((bf16[8,160,768]{2,1,0:T(8,128)(2,1)}), bf16[8,160,768]{2,1,0:T(8,128)(2,1)S(1)}, u32[]{:S(2)}, u32[]{:S(2)}) async-start(bf16[8,160,768]{2,1,0:T(8,128)(2,1)} %bitcast.129), calls=%async_computation.4 | async-start | bytes 3932160 | tf_op jit(solution)/shard_map/all_to_all | solution.py:805
  209.8 200.8 %reduce-scatter.3.cloned.1.call-start = ((), (), s32[]{:S(2)}) async-start(), calls=%async_computation.11 | async-start | bytes 5898240 | tf_op jit(solution)/shard_map/reduce_scatter | solution.py:970
  275.5 4.5 %collective-permute-start.4 = (bf16[2,192,896]{2,1,0:T(8,128)(2,1)S(1)}, bf16[2,192,896]{2,1,0:T(8,128)(2,1)S(1)}, u32[]{:S(2)}, u32[]{:S(2)}) collective-permute-start(bf16[2,192,896]{2,1,0:T(8,128)(2,1)S(1)} %fusion.2), channel_id=1, source_target_pairs={{0,8},{8,0},{16,24},{24,16},{1,9},{9,1},{17,25},{25,17},{2,10},{10... | collective-permute-start | bytes 2064392 | tf_op jit(solution)/shard_map/ppermute | solution.py:797
  275.6 49.9 %all-to-all-start.5 = ((bf16[8,160,768]{2,1,0:T(8,128)(2,1)}), bf16[8,160,768]{2,1,0:T(8,128)(2,1)S(1)}, u32[]{:S(2)}, u32[]{:S(2)}) async-start(bf16[8,160,768]{2,1,0:T(8,128)(2,1)} %bitcast.47), calls=%async_computation.5 | async-start | bytes 3932160 | tf_op jit(solution)/shard_map/all_to_all | solution.py:805
  279.2 131.4 %reduce-scatter.5.cloned.1.call-start = ((), (), s32[]{:S(2)}) async-start(), calls=%async_computation.12 | async-start | bytes 5898240 | tf_op jit(solution)/shard_map/reduce_scatter | solution.py:971
  281.6 41.8 %collective-permute-start.5 = (bf16[1,192,896]{2,1,0:T(8,128)(2,1)S(1)}, bf16[1,192,896]{2,1,0:T(8,128)(2,1)S(1)}, u32[]{:S(2)}, u32[]{:S(2)}) collective-permute-start(bf16[1,192,896]{2,1,0:T(8,128)(2,1)S(1)} %dynamic-slice_convert_fusion.4), channel_id=1, source_target_pairs={{0,16},{8,24},{16,0},{24,8},{1,17},{9,25},{17,1},{25,9},{2,18},{10... | collective-permute-start | bytes 1032200 | tf_op jit(solution)/shard_map/ppermute | solution.py:797
  333.6 13.4 %collective-permute-start.6 = (bf16[2,192,1536]{2,1,0:T(8,128)(2,1)S(1)}, bf16[2,192,1536]{2,1,0:T(8,128)(2,1)}, u32[]{:S(2)}, u32[]{:S(2)}) collective-permute-start(bf16[2,192,1536]{2,1,0:T(8,128)(2,1)S(1)} %fusion), channel_id=1, source_target_pairs={{0,8},{8,0},{16,24},{24,16},{1,9},{9,1},{17,25},{25,17},{2,10},{10... | collective-permute-start | bytes 3538952 | tf_op jit(solution)/shard_map/ppermute | solution.py:797
  342.9 31.2 %all-to-all-start.6 = ((bf16[8,24,896]{2,1,0:T(8,128)(2,1)}), bf16[8,24,896]{2,1,0:T(8,128)(2,1)S(1)}, u32[]{:S(2)}, u32[]{:S(2)}) async-start(bf16[8,24,896]{2,1,0:T(8,128)(2,1)} %bitcast.54), calls=%async_computation.6 | async-start | bytes 688128 | tf_op jit(solution)/shard_map/all_to_all | solution.py:805
  350.3 23.9 %collective-permute-start.7 = (bf16[1,192,1536]{2,1,0:T(8,128)(2,1)}, bf16[1,192,1536]{2,1,0:T(8,128)(2,1)}, u32[]{:S(2)}, u32[]{:S(2)}) collective-permute-start(bf16[1,192,1536]{2,1,0:T(8,128)(2,1)} %dynamic-slice_convert_fusion.3), channel_id=1, source_target_pairs={{0,16},{8,24},{16,0},{24,8},{1,17},{9,25},{17,1},{25,9},{2,18},{10... | collective-permute-start | bytes 1769480 | tf_op jit(solution)/shard_map/ppermute | solution.py:797
  351.6 22.4 %copy-start.26 = (f32[1,128]{1,0:T(1,128)S(1)}, f32[1,128]{1,0:T(1,128)}, u32[]{:S(2)}) copy-start(f32[1,128]{1,0:T(1,128)} %get-tuple-element.154) | copy-start | bytes 1540
  375.5 3.6 collective-permute-start.10
  378.5 9.3 %collective-permute-start.8 = (bf16[2,192,768]{2,1,0:T(8,128)(2,1)S(1)}, bf16[2,192,768]{2,1,0:T(8,128)(2,1)S(1)}, u32[]{:S(2)}, u32[]{:S(2)}) collective-permute-start(bf16[2,192,768]{2,1,0:T(8,128)(2,1)S(1)} %fusion.3), channel_id=1, source_target_pairs={{0,8},{8,0},{16,24},{24,16},{1,9},{9,1},{17,25},{25,17},{2,10},{10... | collective-permute-start | bytes 1769480 | tf_op jit(solution)/shard_map/ppermute | solution.py:797
  379.1 8.8 %collective-permute-start.11 = (f32[1,768]{1,0:T(1,128)S(1)}, f32[1,768]{1,0:T(1,128)S(1)}, u32[]{:S(2)}, u32[]{:S(2)}) collective-permute-start(f32[1,768]{1,0:T(1,128)S(1)} %reshape_add_fusion), channel_id=1, source_target_pairs={{0,16},{8,24},{16,0},{24,8},{1,17},{9,25},{17,1},{25,9},{2,18},{10... | collective-permute-start | bytes 9224 | tf_op jit(solution)/shard_map/ppermute | solution.py:797
  381.3 22.4 %all-to-all-start.7 = ((bf16[8,24,1536]{2,1,0:T(8,128)(2,1)}), bf16[8,24,1536]{2,1,0:T(8,128)(2,1)S(1)}, u32[]{:S(2)}, u32[]{:S(2)}) async-start(bf16[8,24,1536]{2,1,0:T(8,128)(2,1)} %bitcast.58), calls=%async_computation.7 | async-start | bytes 1179648 | tf_op jit(solution)/shard_map/all_to_all | solution.py:805
  389.4 10.9 %collective-permute-start.9 = (bf16[1,192,768]{2,1,0:T(8,128)(2,1)S(1)}, bf16[1,192,768]{2,1,0:T(8,128)(2,1)S(1)}, u32[]{:S(2)}, u32[]{:S(2)}) collective-permute-start(bf16[1,192,768]{2,1,0:T(8,128)(2,1)S(1)} %dynamic-slice_convert_fusion.5), channel_id=1, source_target_pairs={{0,16},{8,24},{16,0},{24,8},{1,17},{9,25},{17,1},{25,9},{2,18},{10... | collective-permute-start | bytes 884744 | tf_op jit(solution)/shard_map/ppermute | solution.py:797
  404.7 15.5 %all-to-all-start.8 = ((bf16[8,27,768]{2,1,0:T(8,128)(2,1)}), bf16[8,27,768]{2,1,0:T(8,128)(2,1)S(1)}, u32[]{:S(2)}, u32[]{:S(2)}) async-start(bf16[8,27,768]{2,1,0:T(8,128)(2,1)} %pad_maximum_fusion.2), calls=%async_computation.8 | async-start | bytes 786432 | tf_op jit(solution)/shard_map/all_to_all | solution.py:805
  (26 other events, 163.9 us)
Sparse Core Ops, SparseCore 0:
  255.6 53.8 reduce-scatter.2
  312.1 53.1 reduce-scatter.4

commit v4 on v3

--- a/solution.py
+++ b/solution.py
@@ -77,11 +77,23 @@
     return jnp.concatenate(parts, axis=1)
 
 
-def forward_kernel(head_dim, reach, low_ref, high_ref, q_ref, k_ref, v_ref, qx_ref, kx_ref, bias_ref, *refs):
-    mix_ref, lse_ref, vt_ref = refs[-3:]
-    length, width = q_ref.shape
+def forward_kernel(head_dim, reach, low_ref, high_ref, in_ref, small_ref, weight_ref, qx_ref, kx_ref, bias_ref, *refs):
+    packed_ref, mix_ref, lse_ref, normed_ref, vt_ref = refs[-5:]
+    length, width = mix_ref.shape
     heads = width // head_dim
     scale = head_dim ** (-0.5)
+    chunks = [slice(at, at + ROWS) for at in range(0, length, ROWS)]
+
+    @pl.when(pl.program_id(0) == 0)
+    def _():
+        gain = gain_row(small_ref, 0)
+        for here in chunks:
+            rows = in_ref[here].astype(f32)
+            normed_ref[here] = (rows * row_factor(rows) * gain).astype(bf16)
+
+    for here in chunks:
+        packed_ref[here] = dot(normed_ref[here], weight_ref[...], NN).astype(bf16)
+    q_ref, k_ref, v_ref = [packed_ref.at[:, part * width : (part + 1) * width] for part in range(3)]
     for c in range(width // LANES):
         vt_ref[c * LANES : (c + 1) * LANES, :] = v_ref[:, c * LANES : (c + 1) * LANES].T
     per = LANES // head_dim
@@ -135,6 +147,40 @@
     lax.fori_loop(0, length // ROWS, one_block, 0)
 
 
+def probs_kernel(head_dim, reach, low_ref, high_ref, q_ref, k_ref, qx_ref, kx_ref, bias_ref, lse_ref, probs_ref):
+    length, width = q_ref.shape
+    heads = width // head_dim
+    scale = head_dim ** (-0.5)
+    per = LANES // head_dim
+
+    def one_block(qb, unused):
+        first = pl.multiple_of(qb * ROWS, ROWS)
+        qx = qx_ref[:, pl.ds(first, ROWS)]
+        queries = []
+        for c in range(width // LANES):
+            pair = (q_ref[pl.ds(first, ROWS), c * LANES : (c + 1) * LANES] * jnp.asarray(scale, bf16)).T
+            queries += [jnp.concatenate([head_rows(pair, h, head_dim), qx], axis=0) for h in range(per)]
+        lses = [lse_ref[0, h : h + 1, pl.ds(first, ROWS)] for h in range(heads)]
+
+        def one_tile(kb, unused):
+            keys_at = pl.multiple_of(kb * ROWS, ROWS)
+            offset = pl.multiple_of(keys_at - first + LANES * reach, LANES)
+            kx = kx_ref[pl.ds(keys_at, ROWS), :]
+            all_scores = []
+            for h in range(heads):
+                c = h // per
+                keys = jnp.concatenate([k_ref[pl.ds(keys_at, ROWS), c * LANES : (c + 1) * LANES], kx], axis=1)
+                all_scores.append(dot(keys, queries[h], NN))
+            for h in range(heads):
+                weights = jnp.exp(all_scores[h] + bias_tile(bias_ref, h, offset) - lses[h])
+                probs_ref[h, qb, pl.ds(keys_at, ROWS), :] = weights.astype(bf16)
+            return unused
+
+        return lax.fori_loop(low_ref[qb], high_ref[qb], one_tile, unused)
+
+    lax.fori_loop(0, length // ROWS, one_block, 0)
+
+
 def diagonal_sums(tiles):
     groups = tiles.shape[0]
     step = LANES // 2
@@ -151,7 +197,7 @@
     return turned[:, 0]
 
 
-def backward_kernel(head_dim, reach, low_ref, high_ref, q_ref, k_ref, v_ref, dmix_ref, mix_ref, qx_ref, kx_ref, bias_ref, lse_ref,
+def backward_kernel(head_dim, reach, low_ref, high_ref, q_ref, k_ref, v_ref, dmix_ref, mix_ref, probs_ref,
                     grad_ref, diag_ref, kt_ref, dk_ref, dv_ref, along_ref):
     length, width = q_ref.shape
     heads = width // head_dim
@@ -165,42 +211,34 @@
 
     def one_block(qb, unused):
         first = pl.multiple_of(qb * ROWS, ROWS)
-        qx = qx_ref[:, pl.ds(first, ROWS)]
-        queries, d_mixes, deltas, wide, d_turned = [], [], [], [], []
+        queries, d_mixes, deltas, d_turned = [], [], [], []
         for c in range(width // LANES):
             lanes = slice(c * LANES, (c + 1) * LANES)
             query = q_ref[pl.ds(first, ROWS), lanes] * jnp.asarray(scale, bf16)
             d_mix = dmix_ref[pl.ds(first, ROWS), lanes]
             product = (d_mix.astype(f32) * mix_ref[pl.ds(first, ROWS), lanes].astype(f32)).T
-            query_turned, d_mix_turned = query.T, d_mix.T
+            d_mix_turned = d_mix.T
             for h in range(per):
                 queries.append(head_lanes(query, h, head_dim))
                 d_mixes.append(head_lanes(d_mix, h, head_dim))
-                wide.append(jnp.concatenate([head_rows(query_turned, h, head_dim), qx], axis=0))
                 d_turned.append(head_rows(d_mix_turned, h, head_dim))
                 deltas.append(jnp.sum(product[h * head_dim : (h + 1) * head_dim], axis=0, keepdims=True))
-        lses = [lse_ref[0, h : h + 1, pl.ds(first, ROWS)] for h in range(heads)]
 
         def one_tile(kb, carry):
             keys_at = pl.multiple_of(kb * ROWS, ROWS)
             offset = pl.multiple_of(keys_at - first + LANES * reach, LANES)
-            kx = kx_ref[pl.ds(keys_at, ROWS), :]
             out = []
-            low_weights, low_scores, all_scores, all_weights = [], [], [], []
-            for h in range(heads):
-                lanes = slice(h // per * LANES, (h // per + 1) * LANES)
-                keys = jnp.concatenate([k_ref[pl.ds(keys_at, ROWS), lanes], kx], axis=1)
-                all_scores.append(dot(keys, wide[h], NN))
+            low_weights, low_scores, all_weights = [], [], []
             for h in range(heads):
                 lanes = slice(h // per * LANES, (h // per + 1) * LANES)
                 all_weights.append(dot(v_ref[pl.ds(keys_at, ROWS), lanes], d_turned[h], NN))
             for h in range(heads):
-                weights = jnp.exp(all_scores[h] + bias_tile(bias_ref, h, offset) - lses[h])
-                d_scores = weights * (all_weights[h] - deltas[h])
+                weights = probs_ref[h, qb, pl.ds(keys_at, ROWS), :]
+                d_scores = weights.astype(f32) * (all_weights[h] - deltas[h])
                 for part in range(ROWS // LANES):
                     at = pl.ds(pl.multiple_of(offset - LANES * part, LANES), ROWS)
                     along_ref[h, at, :] += d_scores[:, part * LANES : (part + 1) * LANES]
-                low_weights.append(weights.astype(bf16))
+                low_weights.append(weights)
                 low_scores.append(d_scores.astype(bf16))
             for h in range(heads):
                 keys_turned = kt_ref[h * head_dim : (h + 1) * head_dim, pl.ds(keys_at, ROWS)]
@@ -257,10 +295,9 @@
     return query_side, key_side
 
 
-def attend_forward(packed, query_side, key_side, bounds, tiles, mixed, first, head_dim):
-    length = packed.shape[0]
+def attend_forward(rows_in, smalls, small_at, weights, query_side, key_side, bounds, tiles, mixed, first, steps, head_dim):
+    length, model_width = rows_in.shape
     width = STEP_HEADS * head_dim
-    steps = packed.shape[1] // 3 // width
     reach = tiles.shape[1] // LANES // 2
     shared = [] if mixed is None else [mixed]
     whole = lambda *_: (0, 0)
@@ -268,17 +305,19 @@
         num_scalar_prefetch=2,
         grid=(steps,),
         in_specs=[
-            pl.BlockSpec((length, width), lambda p, *_: (0, 3 * p)),
-            pl.BlockSpec((length, width), lambda p, *_: (0, 3 * p + 1)),
-            pl.BlockSpec((length, width), lambda p, *_: (0, 3 * p + 2)),
+            pl.BlockSpec((length, model_width), whole),
+            pl.BlockSpec((model_width, LANES), lambda p, *_: (0, small_at)),
+            pl.BlockSpec((model_width, 3 * width), lambda p, *_: (0, p)),
             pl.BlockSpec((LANES, length), whole),
             pl.BlockSpec((length, LANES), whole),
             pl.BlockSpec((STEP_HEADS, tiles.shape[1], LANES), lambda p, *_: (first + p, 0, 0)),
         ]
         + [pl.BlockSpec(memory_space=pl.ANY)] * len(shared),
         out_specs=[
+            pl.BlockSpec((length, 3 * width), lambda p, *_: (0, p)),
             pl.BlockSpec((length, width), lambda p, *_: (0, first + p)),
             pl.BlockSpec((1, STEP_HEADS, length), lambda p, *_: (p, 0, 0)),
+            pl.BlockSpec((length, model_width), whole),
         ],
         scratch_shapes=[pltpu.VMEM((width, length), bf16)],
     )
@@ -286,22 +325,52 @@
         functools.partial(forward_kernel, head_dim, reach),
         grid_spec=grid_spec,
         out_shape=[
+            jax.ShapeDtypeStruct((length, 3 * width * steps), bf16),
             jax.ShapeDtypeStruct((length, tiles.shape[0] * head_dim), bf16),
             jax.ShapeDtypeStruct((steps, STEP_HEADS, length), f32),
-        ],
-        input_output_aliases={8: 0} if shared else {},
-        compiler_params=pltpu.CompilerParams(vmem_limit_bytes=56 * 2**20),
+            jax.ShapeDtypeStruct((length, model_width), bf16),
+        ],
+        input_output_aliases={8: 1} if shared else {},
+        compiler_params=pltpu.CompilerParams(vmem_limit_bytes=VMEM_BYTES),
         cost_estimate=cost(1),
         name="attend_forward",
-    )(*bounds, packed, packed, packed, query_side, key_side, tiles, *shared)
-
-
-def attend_backward(packed, d_mix, mix, lse, query_side, key_side, bounds, tiles, first, head_dim):
+    )(*bounds, rows_in, smalls, weights, query_side, key_side, tiles, *shared)
+
+
+def attend_probs(packed, lse, query_side, key_side, bounds, tiles, first, head_dim):
     length = packed.shape[0]
     width = STEP_HEADS * head_dim
     steps = packed.shape[1] // 3 // width
     reach = tiles.shape[1] // LANES // 2
-    groups = 2 * reach + 1
+    whole = lambda *_: (0, 0)
+    blocks = length // ROWS
+    grid_spec = pltpu.PrefetchScalarGridSpec(
+        num_scalar_prefetch=2,
+        grid=(steps,),
+        in_specs=[
+            pl.BlockSpec((length, width), lambda p, *_: (0, 3 * p)),
+            pl.BlockSpec((length, width), lambda p, *_: (0, 3 * p + 1)),
+            pl.BlockSpec((LANES, length), whole),
+            pl.BlockSpec((length, LANES), whole),
+            pl.BlockSpec((STEP_HEADS, tiles.shape[1], LANES), lambda p, *_: (first + p, 0, 0)),
+            pl.BlockSpec((1, STEP_HEADS, length), lambda p, *_: (p, 0, 0)),
+        ],
+        out_specs=pl.BlockSpec((STEP_HEADS, blocks, length, ROWS), lambda p, *_: (p, 0, 0, 0)),
+    )
+    return pl.pallas_call(
+        functools.partial(probs_kernel, head_dim, reach),
+        grid_spec=grid_spec,
+        out_shape=jax.ShapeDtypeStruct((steps * STEP_HEADS, blocks, length, ROWS), bf16),
+        compiler_params=pltpu.CompilerParams(vmem_limit_bytes=56 * 2**20),
+        cost_estimate=cost(9 * steps),
+        name="attend_probs",
+    )(*bounds, packed, packed, query_side, key_side, tiles, lse)
+
+
+def attend_backward(packed, d_mix, mix, probs, bounds, groups, first, head_dim):
+    length = packed.shape[0]
+    width = STEP_HEADS * head_dim
+    steps = packed.shape[1] // 3 // width
     whole = lambda *_: (0, 0)
     grid_spec = pltpu.PrefetchScalarGridSpec(
         num_scalar_prefetch=2,
@@ -312,10 +381,7 @@
             pl.BlockSpec((length, width), lambda p, *_: (0, 3 * p + 2)),
             pl.BlockSpec((length, width), lambda p, *_: (0, first + p)),
             pl.BlockSpec((length, width), lambda p, *_: (0, first + p)),
-            pl.BlockSpec((LANES, length), whole),
-            pl.BlockSpec((length, LANES), whole),
-            pl.BlockSpec((STEP_HEADS, tiles.shape[1], LANES), lambda p, *_: (first + p, 0, 0)),
-            pl.BlockSpec((1, STEP_HEADS, length), lambda p, *_: (p, 0, 0)),
+            pl.BlockSpec((STEP_HEADS, *probs.shape[1:]), lambda p, *_: (p, 0, 0, 0)),
         ],
         out_specs=[
             pl.BlockSpec((length, 3 * width), lambda p, *_: (0, p)),
@@ -328,18 +394,17 @@
             pltpu.VMEM((STEP_HEADS, groups * LANES, LANES), f32),
         ],
     )
-    work = steps * STEP_HEADS * length * length
-    return pl.pallas_call(
-        functools.partial(backward_kernel, head_dim, reach),
+    return pl.pallas_call(
+        functools.partial(backward_kernel, head_dim, groups // 2),
         grid_spec=grid_spec,
         out_shape=[
             jax.ShapeDtypeStruct((length, 3 * width * steps), bf16),
             jax.ShapeDtypeStruct((steps * STEP_HEADS, groups, 2 * LANES), f32),
         ],
-        compiler_params=pltpu.CompilerParams(vmem_limit_bytes=56 * 2**20),
-        cost_estimate=cost(20 * steps),
+        compiler_params=pltpu.CompilerParams(vmem_limit_bytes=40 * 2**20),
+        cost_estimate=cost(15 * steps),
         name="attend_backward",
-    )(*bounds, packed, packed, packed, d_mix, mix, query_side, key_side, tiles, lse)
+    )(*bounds, packed, packed, packed, d_mix, mix, probs)
 
 
 def spread_kernel(width, near_steps, weight_ref, out_weight_ref, first_ref, second_ref, router_ref, *outs):
@@ -351,8 +416,8 @@
         jnp.sum(jnp.where(same, jnp.broadcast_to(ref[...].astype(f32), same.shape), 0.0), axis=1, keepdims=True)
         for ref in (first_ref, second_ref)
     ]
-    columns.append(router_ref[...].astype(f32))
-    used = SMALL_GAINS + router_ref.shape[1]
+    columns.append(dot(jnp.where(same, 1.0, 0.0).astype(bf16), router_ref[...], NT))
+    used = SMALL_GAINS + router_ref.shape[0]
     columns.append(jnp.zeros((count, -used % LANES), f32))
     pieces = [
         weight_ref[:, (part * steps + p) * width : (part * steps + p + 1) * width] for p in range(steps) for part in range(3)
@@ -382,10 +447,10 @@
         compiler_params=pltpu.CompilerParams(vmem_limit_bytes=VMEM_BYTES),
         cost_estimate=cost(2),
         name="spread_shard",
-    )(weight, out_weight, first_gain.reshape(1, rows), second_gain.reshape(1, rows), router)
-
-
-def expert_kernel(experts, me_ref, rows_ref, in_ref, small_ref, d_hidden_ref, hidden_ref, d_pre_ref, d_rows_ref, d_logits_ref, gate_ref,
+    )(weight, out_weight, first_gain.reshape(1, rows), second_gain.reshape(1, rows), router.T)
+
+
+def expert_kernel(experts, me_ref, rows_ref, in_ref, small_ref, d_hidden_ref, d_rows_ref, d_logits_ref, gate_ref,
                   probs_ref, total_ref, d_gate_ref):
     step = pl.program_id(0)
     lane = lax.broadcasted_iota(jnp.int32, probs_ref.shape, 1)
@@ -410,13 +475,9 @@
     for i, at in enumerate(range(0, count, chunk)):
         here = slice(at, at + chunk)
         unit, slope = gelu_and_slope(pres[i])
-        hidden = unit.astype(bf16)
         d_hidden = d_hidden_ref[here].astype(f32)
-        hidden_ref[here] = hidden
         d_gate_ref[here] += jnp.sum(unit * d_hidden, axis=1, keepdims=True)
-        low = (gate_ref[here] * d_hidden * slope).astype(bf16)
-        d_pre_ref[here] = low
-        lows.append(low)
+        lows.append((d_hidden * slope).astype(bf16))
     for i, at in enumerate(range(0, count, chunk)):
         total_ref[at : at + chunk] += dot(lows[i], weights, NT)
 
@@ -424,14 +485,13 @@
     def _():
         d_logits = (probs_ref[...] * (chosen.astype(f32) - gate_ref[...]) * d_gate_ref[...]).astype(bf16)
         d_logits_ref[...] = d_logits
-        d_rows_ref[...] = (total_ref[...] + dot(d_logits, small_ref[...], NT)).astype(bf16)
+        d_rows_ref[...] = (gate_ref[...] * total_ref[...] + dot(d_logits, small_ref[...], NT)).astype(bf16)
 
 
 def run_expert(me, rows, w_in, weights, small_at, d_hidden, experts):
     count, width = rows.shape
     hidden_width = w_in.shape[1]
     block = 512
-    row_blocks = pl.BlockSpec((count, block), lambda f, *_: (0, f))
     whole = lambda f, *_: (0, 0)
     grid_spec = pltpu.PrefetchScalarGridSpec(
         num_scalar_prefetch=1,
@@ -440,11 +500,9 @@
             pl.BlockSpec((count, width), whole),
             pl.BlockSpec((width, block), lambda f, *_: (0, f)),
             pl.BlockSpec((width, LANES), lambda f, *_: (0, small_at)),
-            row_blocks,
+            pl.BlockSpec((count, block), lambda f, *_: (0, f)),
         ],
         out_specs=[
-            row_blocks,
-            row_blocks,
             pl.BlockSpec((count, width), whole),
             pl.BlockSpec((count, LANES), whole),
             pl.BlockSpec((count, 1), whole),
@@ -455,32 +513,38 @@
         functools.partial(expert_kernel, experts),
         grid_spec=grid_spec,
         out_shape=[
-            jax.ShapeDtypeStruct((count, hidden_width), bf16),
-            jax.ShapeDtypeStruct((count, hidden_width), bf16),
             jax.ShapeDtypeStruct((count, width), bf16),
             jax.ShapeDtypeStruct((count, LANES), bf16),
             jax.ShapeDtypeStruct((count, 1), f32),
         ],
         compiler_params=pltpu.CompilerParams(vmem_limit_bytes=VMEM_BYTES),
-        cost_estimate=cost(25),
+        cost_estimate=cost(18),
         name="run_expert",
     )(me.reshape(1), rows, w_in, weights, d_hidden)
 
 
-def expert_grads_kernel(gate_ref, rows_ref, hidden_ref, d_pre_ref, d_slots_ref, back_ref, d_logits_ref, part_in_ref, part_out_ref,
-                        moe_ref, router_ref, turned_ref, d_out_ref, total_ref):
+def expert_grads_kernel(gate_ref, rows_ref, in_ref, d_hidden_ref, d_slots_ref, back_ref, d_logits_ref, parts_ref,
+                        moe_ref, router_ref, d_out_ref, total_ref):
     step = pl.program_id(0)
 
     @pl.when(step == 0)
     def _():
-        turned_ref[...] = rows_ref[...].T
         d_out_ref[...] = (gate_ref[...] * d_slots_ref[...].astype(f32)).astype(bf16)
         total_ref[...] = jnp.zeros_like(total_ref)
-        router_ref[...] = dot(turned_ref[...], d_logits_ref[...], NN)
-
-    hidden = hidden_ref[...]
-    part_in_ref[...] = dot(turned_ref[...], d_pre_ref[...], NN).astype(bf16)
-    part_out_ref[...] = dot(hidden, d_out_ref[...], TN).astype(bf16)
+        router_ref[...] = dot(rows_ref[...], d_logits_ref[...], TN)
+
+    count = rows_ref.shape[0]
+    chunk = 256 if count % 256 == 0 else count
+    pres = [dot(rows_ref[at : at + chunk], in_ref[...], NN) for at in range(0, count, chunk)]
+    units, lows = [], []
+    for i, at in enumerate(range(0, count, chunk)):
+        here = slice(at, at + chunk)
+        unit, slope = gelu_and_slope(pres[i])
+        units.append(unit.astype(bf16))
+        lows.append((gate_ref[here] * d_hidden_ref[here].astype(f32) * slope).astype(bf16))
+    hidden = jnp.concatenate(units, axis=0)
+    parts_ref[0, 0] = dot(jnp.concatenate(lows, axis=0), rows_ref[...], TN).astype(bf16)
+    parts_ref[0, 1] = dot(hidden, d_out_ref[...], TN).astype(bf16)
     total_ref[...] += dot(hidden, back_ref[...], NN)
 
     @pl.when(step == pl.num_programs(0) - 1)
@@ -488,49 +552,49 @@
         moe_ref[...] = (gate_ref[...] * total_ref[...]).astype(bf16)
 
 
-def expert_grads(gate, rows, hidden, d_pre, d_slots, w_back, d_logits):
+def expert_grads(gate, rows, w_in, d_hidden, d_slots, w_back, d_logits, owners):
     count, width = rows.shape
-    hidden_width = hidden.shape[1]
-    block = 512
+    block = w_in.shape[1] // owners
     whole = lambda f: (0, 0)
-    row_blocks = pl.BlockSpec((count, block), lambda f: (0, f))
     full = pl.BlockSpec((count, width), whole)
     return pl.pallas_call(
         expert_grads_kernel,
-        grid=(hidden_width // block,),
+        grid=(owners,),
         in_specs=[
             pl.BlockSpec((count, 1), whole),
             full,
-            row_blocks,
-            row_blocks,
+            pl.BlockSpec((width, block), lambda f: (0, f)),
+            pl.BlockSpec((count, block), lambda f: (0, f)),
             full,
             pl.BlockSpec((block, width), lambda f: (f, 0)),
             pl.BlockSpec((count, LANES), whole),
         ],
         out_specs=[
-            pl.BlockSpec((width, block), lambda f: (0, f)),
-            pl.BlockSpec((block, width), lambda f: (f, 0)),
+            pl.BlockSpec((1, 2, block, width), lambda f: (f, 0, 0, 0)),
             full,
             pl.BlockSpec((width, LANES), whole),
         ],
         out_shape=[
-            jax.ShapeDtypeStruct((width, hidden_width), bf16),
-            jax.ShapeDtypeStruct((hidden_width, width), bf16),
+            jax.ShapeDtypeStruct((owners, 2, block, width), bf16),
             jax.ShapeDtypeStruct((count, width), bf16),
             jax.ShapeDtypeStruct((width, LANES), f32),
         ],
-        scratch_shapes=[pltpu.VMEM((width, count), bf16), pltpu.VMEM((count, width), bf16), pltpu.VMEM((count, width), f32)],
+        scratch_shapes=[pltpu.VMEM((count, width), bf16), pltpu.VMEM((count, width), f32)],
         compiler_params=pltpu.CompilerParams(vmem_limit_bytes=VMEM_BYTES),
-        cost_estimate=cost(27),
+        cost_estimate=cost(35),
         name="expert_grads",
-    )(gate, rows, hidden, d_pre, d_slots, w_back, d_logits)
+    )(gate, rows, w_in, d_hidden, d_slots, w_back, d_logits)
+
+
+def gain_row(small_ref, lane):
+    return small_ref[...].astype(f32).T[lane : lane + 1]
 
 
 def row_factor(rows):
     return lax.rsqrt(jnp.mean(rows * rows, axis=1, keepdims=True) + EPSILON)
 
 
-def middle_kernel(row_steps, mixed_ref, weight_ref, in_ref, gain_ref, slot_ref, rows_ref, slots_ref, normed_ref):
+def middle_kernel(row_steps, mixed_ref, weight_ref, in_ref, small_ref, slot_ref, rows_ref, slots_ref, normed_ref):
     step = pl.program_id(0)
 
     @pl.when(step < row_steps)
@@ -538,7 +602,7 @@
         count = in_ref.shape[0]
         first = pl.multiple_of(step * count, count)
         chunks = [slice(at, at + ROWS) for at in range(0, count, ROWS)]
-        gain = gain_ref[...]
+        gain = gain_row(small_ref, 1)
         projected = [dot(mixed_ref[here], weight_ref[...], NN) for here in chunks]
         for here, attn in zip(chunks, projected):
             rows = in_ref[here].astype(f32) + attn
@@ -559,11 +623,15 @@
         slots_ref[at : at + chunk] = dot(place, rows_ref[...], NN).astype(bf16)
 
 
-def read_slots(slot_ref, here, blocks_ref):
+def across(row):
+    return jnp.broadcast_to(row.astype(f32), (LANES, row.shape[1])).T
+
+
+def read_slots(slot_ref, blocks_ref):
     slots = blocks_ref.shape[0]
-    slot = lax.broadcasted_iota(jnp.int32, (ROWS, slots), 1)
-    place = jnp.where(slot == slot_ref[here], 1.0, 0.0).astype(bf16)
-    return dot(place, blocks_ref[...], NN)
+    mine = jnp.concatenate([across(slot_ref[...])] * pl.cdiv(slots, LANES), axis=1)[:, :slots]
+    slot = lax.broadcasted_iota(jnp.int32, mine.shape, 1).astype(f32)
+    return dot(jnp.where(slot == mine, 1.0, 0.0).astype(bf16), blocks_ref[...], NN)
 
 
 def fill_slots(slot_row, rows, slots):
@@ -576,7 +644,7 @@
     )(slot_row, rows)
 
 
-def run_middle(mixed, weights, at, rows_in, gain, slot_row, slots):
+def run_middle(mixed, weights, at, rows_in, smalls, small_at, slot_row, slots):
     count, width = rows_in.shape
     whole = lambda i: (0, 0)
     row_steps = 2 if count % (2 * ROWS) == 0 else 1
@@ -589,7 +657,7 @@
             part,
             pl.BlockSpec((width, width), lambda i: (0, at)),
             part,
-            pl.BlockSpec((1, width), whole),
+            pl.BlockSpec((width, LANES), lambda i: (0, small_at)),
             pl.BlockSpec((1, count), whole),
         ],
         out_specs=[part, pl.BlockSpec((slots // slot_steps, width), lambda i: (jnp.maximum(i - row_steps, 0), 0))],
@@ -598,22 +666,21 @@
         compiler_params=pltpu.CompilerParams(vmem_limit_bytes=VMEM_BYTES),
         cost_estimate=cost(5),
         name="run_middle",
-    )(mixed, weights, rows_in, gain, slot_row)
-
-
-def middle_back_kernel(blocks_ref, slot_ref, rows_ref, gain_ref, top_ref, weight_ref, d_mid_ref, d_attn_ref, d_mixed_ref, d_gain_ref):
-    gain = gain_ref[...]
-    d_normed = read_slots(slot_ref, slice(None), blocks_ref)
+    )(mixed, weights, rows_in, smalls, slot_row)
+
+
+def middle_back_kernel(blocks_ref, slot_ref, rows_ref, small_ref, top_ref, weight_ref, d_mid_ref, d_mixed_ref, d_gain_ref):
+    gain = gain_row(small_ref, 1)
+    d_normed = read_slots(slot_ref, blocks_ref)
     rows = rows_ref[...]
     factor = row_factor(rows)
     normed = rows * factor
     weighted = d_normed * gain
     product = d_normed * normed
     d_mid = top_ref[...].astype(f32) + factor * (weighted - normed * jnp.mean(product * gain, axis=1, keepdims=True))
+    d_mid = d_mid.astype(bf16)
     d_mid_ref[...] = d_mid
-    d_attn = d_mid.astype(bf16)
-    d_attn_ref[...] = d_attn
-    d_mixed_ref[...] = dot(d_attn, weight_ref[...], NT).astype(bf16)
+    d_mixed_ref[...] = dot(d_mid, weight_ref[...], NT).astype(bf16)
 
     @pl.when(pl.program_id(0) == 0)
     def _():
@@ -622,7 +689,7 @@
     d_gain_ref[...] += jnp.sum(product, axis=0, keepdims=True)
 
 
-def run_middle_back(blocks, slot_column, rows, gain, top, weights, at):
+def run_middle_back(blocks, slot_row, rows, smalls, small_at, top, weights, at):
     count, width = rows.shape
     whole = lambda *_: (0, 0)
     part = pl.BlockSpec((ROWS, width), lambda i: (i, 0))
@@ -631,15 +698,14 @@
         grid=(count // ROWS,),
         in_specs=[
             pl.BlockSpec(blocks.shape, whole),
-            pl.BlockSpec((ROWS, 1), lambda i: (i, 0)),
+            pl.BlockSpec((1, ROWS), lambda i: (0, i)),
             part,
-            pl.BlockSpec((1, width), whole),
+            pl.BlockSpec((width, LANES), lambda i: (0, small_at)),
             part,
             pl.BlockSpec((width, width), lambda i: (0, at)),
         ],
-        out_specs=[part, part, part, pl.BlockSpec((1, width), whole)],
+        out_specs=[part, part, pl.BlockSpec((1, width), whole)],
         out_shape=[
-            jax.ShapeDtypeStruct((count, width), f32),
             jax.ShapeDtypeStruct((count, width), bf16),
             jax.ShapeDtypeStruct((count, width), bf16),
             jax.ShapeDtypeStruct((1, width), f32),
@@ -647,10 +713,10 @@
         compiler_params=pltpu.CompilerParams(vmem_limit_bytes=VMEM_BYTES),
         cost_estimate=cost(7),
         name="run_middle_back",
-    )(blocks, slot_column, rows, gain, top, weights)
-
-
-def first_back_kernel(count, in_ref, gain_ref, d_mid_ref, *refs):
+    )(blocks, slot_row, rows, smalls, top, weights)
+
+
+def first_back_kernel(count, small_at, in_ref, d_mid_ref, *refs):
     d_in_ref = refs[2 * count]
     total = 0.0
     for part_ref, weight_ref in zip(refs[:count], refs[count:]):
@@ -658,18 +724,18 @@
     rows = in_ref[...].astype(f32)
     factor = row_factor(rows)
     normed = rows * factor
-    weighted = total * gain_ref[...]
-    d_in_ref[...] = d_mid_ref[...] + factor * (weighted - normed * jnp.mean(weighted * normed, axis=1, keepdims=True))
-
-
-def run_first_back(rows_in, gain, d_mid, parts, weights):
+    weighted = total * gain_row(refs[count].at[:, small_at * LANES : (small_at + 1) * LANES], 0)
+    d_in_ref[...] = d_mid_ref[...].astype(f32) + factor * (weighted - normed * jnp.mean(weighted * normed, axis=1, keepdims=True))
+
+
+def run_first_back(rows_in, small_at, d_mid, parts, weights):
     count, width = rows_in.shape
     whole = lambda *_: (0, 0)
     part = pl.BlockSpec((ROWS, width), lambda i: (i, 0))
     return pl.pallas_call(
-        functools.partial(first_back_kernel, len(parts)),
+        functools.partial(first_back_kernel, len(parts), small_at),
         grid=(count // ROWS,),
-        in_specs=[part, pl.BlockSpec((1, width), whole), part]
+        in_specs=[part, part]
         + [pl.BlockSpec((ROWS, columns.shape[1]), lambda i: (i, 0)) for columns in parts]
         + [pl.BlockSpec(weight.shape, whole) for weight in weights],
         out_specs=part,
@@ -677,14 +743,14 @@
         compiler_params=pltpu.CompilerParams(vmem_limit_bytes=VMEM_BYTES),
         cost_estimate=cost(8),
         name="run_first_back",
-    )(rows_in, gain, d_mid, *parts, *weights)
+    )(rows_in, d_mid, *parts, *weights)
 
 
 def output_kernel(blocks_ref, slot_ref, rows_ref, in_ref, live_ref, out_ref, sums_ref):
     rows = rows_ref[...]
-    final = rows + read_slots(slot_ref, slice(None), blocks_ref)
+    final = rows + read_slots(slot_ref, blocks_ref)
     out_ref[...] = final.astype(bf16)
-    live = live_ref[...]
+    live = across(live_ref[...])[:, :1]
     lane = lax.broadcasted_iota(jnp.int32, (1, LANES), 1)
     sums = jnp.where(lane == 3, jnp.sum(live, axis=0, keepdims=True), 0.0)
     for i, part in enumerate((in_ref[...].astype(f32), rows, final)):
@@ -698,11 +764,11 @@
     sums_ref[...] += sums
 
 
-def run_output(blocks, slot_column, rows, rows_in, live):
+def run_output(blocks, slot_row, rows, rows_in, live):
     count, width = rows.shape
     whole = lambda *_: (0, 0)
     part = pl.BlockSpec((ROWS, width), lambda i: (i, 0))
-    column = pl.BlockSpec((ROWS, 1), lambda i: (i, 0))
+    column = pl.BlockSpec((1, ROWS), lambda i: (0, i))
     return pl.pallas_call(
         output_kernel,
         grid=(count // ROWS,),
@@ -712,72 +778,59 @@
         compiler_params=pltpu.CompilerParams(vmem_limit_bytes=VMEM_BYTES),
         cost_estimate=cost(4),
         name="run_output",
-    )(blocks, slot_column, rows, rows_in, live)
-
-
-def out_grad_kernel(mixed_ref, d_attn_ref, router_ref, gain_ref, grad_ref):
-    width = mixed_ref.shape[1]
+    )(blocks, slot_row, rows, rows_in, live)
+
+
+def dense_grads_kernel(mixed_ref, d_attn_ref, router_ref, gain_ref, normed_ref, parts_ref, grad_ref):
+    width = d_attn_ref.shape[1]
     grad_ref[:, :width] = dot(mixed_ref[...], d_attn_ref[...], TN)
-    column = jnp.broadcast_to(gain_ref[...], (LANES, width)).T
-    lane = lax.broadcasted_iota(jnp.int32, column.shape, 1)
-    grad_ref[:, width:] = jnp.where(lane == 1, column, router_ref[...])
-
-
-def run_out_grad(mixed, d_attn, grad_router, grad_gain):
-    width = mixed.shape[1]
-    return pl.pallas_call(
-        out_grad_kernel,
-        out_shape=jax.ShapeDtypeStruct((width, width + LANES), f32),
+    lane = lax.broadcasted_iota(jnp.int32, router_ref.shape, 1)
+    grad_ref[:, width : width + LANES] = jnp.where(lane == 1, across(gain_ref[...]), router_ref[...])
+    grad_ref[:, width + LANES :] = dot(normed_ref[...], parts_ref[...], TN)
+
+
+def run_dense_grads(mixed, d_attn, grad_router, grad_gain, normed, parts):
+    count, width = mixed.shape
+    columns = parts.shape[1]
+    block = ROWS if width % ROWS == 0 else width
+    whole = lambda i: (0, 0)
+    part = pl.BlockSpec((count, block), lambda i: (0, i))
+    return pl.pallas_call(
+        dense_grads_kernel,
+        grid=(width // block,),
+        in_specs=[
+            part,
+            pl.BlockSpec((count, width), whole),
+            pl.BlockSpec((block, LANES), lambda i: (i, 0)),
+            pl.BlockSpec((1, block), lambda i: (0, i)),
+            part,
+            pl.BlockSpec((count, columns), whole),
+        ],
+        out_specs=pl.BlockSpec((block, width + LANES + columns), lambda i: (i, 0)),
+        out_shape=jax.ShapeDtypeStruct((width, width + LANES + columns), f32),
         compiler_params=pltpu.CompilerParams(vmem_limit_bytes=VMEM_BYTES),
-        cost_estimate=cost(3),
-        name="run_out_grad",
-    )(mixed, d_attn, grad_router, grad_gain)
-
-
-def widen_kernel(*refs):
-    half = len(refs) // 2
-    for in_ref, out_ref in zip(refs[:half], refs[half:]):
-        out_ref[...] = in_ref[...].astype(f32)
-
-
-def widen(*arrays):
-    rows, columns = arrays[0].shape
-    part = pl.BlockSpec((rows // 3, columns), lambda i: (i, 0))
+        cost_estimate=cost(7),
+        name="run_dense_grads",
+    )(mixed, d_attn, grad_router, grad_gain, normed, parts)
+
+
+def widen_kernel(sums_ref, in_ref, out_ref):
+    in_ref[...] = sums_ref[0, 0].astype(f32).T
+    out_ref[...] = sums_ref[0, 1].astype(f32)
+
+
+def widen(sums):
+    block, width = sums.shape[2:]
+    step = ROWS if block % ROWS == 0 else LANES
     return pl.pallas_call(
         widen_kernel,
-        grid=(3,),
-        in_specs=[part] * len(arrays),
-        out_specs=[part] * len(arrays),
-        out_shape=[jax.ShapeDtypeStruct(array.shape, f32) for array in arrays],
+        grid=(block // step,),
+        in_specs=[pl.BlockSpec((1, 2, step, width), lambda i: (0, 0, i, 0))],
+        out_specs=[pl.BlockSpec((width, step), lambda i: (0, i)), pl.BlockSpec((step, width), lambda i: (i, 0))],
+        out_shape=[jax.ShapeDtypeStruct((width, block), f32), jax.ShapeDtypeStruct((block, width), f32)],
         cost_estimate=cost(2),
         name="widen",
-    )(*arrays)
-
-
-def project_kernel(in_ref, gain_ref, weight_ref, packed_ref, normed_ref):
-    rows = in_ref[...].astype(f32)
-    normed = (rows * row_factor(rows) * gain_ref[...]).astype(bf16)
-    normed_ref[...] = normed
-    packed_ref[...] = dot(normed, weight_ref[...], NN).astype(bf16)
-
-
-def run_project(rows_in, gain, weights, columns):
-    count, width = rows_in.shape
-    whole = lambda i: (0, 0)
-    return pl.pallas_call(
-        project_kernel,
-        grid=(count // ROWS,),
-        in_specs=[
-            pl.BlockSpec((ROWS, width), lambda i: (i, 0)),
-            pl.BlockSpec((1, width), whole),
-            pl.BlockSpec((width, columns), whole),
-        ],
-        out_specs=[pl.BlockSpec((ROWS, columns), lambda i: (i, 0)), pl.BlockSpec((ROWS, width), lambda i: (i, 0))],
-        out_shape=[jax.ShapeDtypeStruct((count, columns), bf16), jax.ShapeDtypeStruct((count, width), bf16)],
-        compiler_params=pltpu.CompilerParams(vmem_limit_bytes=VMEM_BYTES),
-        cost_estimate=cost(4),
-        name="run_project",
-    )(rows_in, gain, weights)
+    )(sums)
 
 
 HIGHEST = lax.Precision.HIGHEST
@@ -907,8 +960,7 @@
     slot_index = jnp.where(
         dropped.reshape(tokens) == 1, slots, routes.reshape(tokens) * capacity + positions.reshape(tokens)
     )
-    slot_row, slot_column = slot_index.reshape(1, tokens), slot_index.reshape(tokens, 1)
-    live = valid_mask.reshape(tokens, 1).astype(f32)
+    slot_row, live = slot_index.reshape(1, tokens), valid_mask.reshape(1, tokens)
     rows_in = inputs.reshape(tokens, model_width)
     top = cotangent.reshape(tokens, model_width)
 
@@ -919,95 +971,110 @@
         qkv_weight, out_weight, attn_gain, ffn_gain, router_weight, width, steps - 1, lax.axis_size("expert")
     )
     near = swap_blocks(near)
-    near, rest, tiles, all_masks = lax.optimization_barrier((near, rest, tiles, all_masks))
+    bounds = [tile_bounds(segment_ids[seq]) for seq in range(seq_count)]
+    near, rest, tiles = lax.optimization_barrier((near, rest, tiles))
     rest = swap_blocks(rest)
     filled_cotangent = fill_slots(slot_row, top, slots)
     terms = start_gather(near)
-    terms, filled_cotangent, rest = lax.optimization_barrier((terms, filled_cotangent, rest))
+    terms, filled_cotangent, rest, all_masks, bounds = lax.optimization_barrier(
+        (terms, filled_cotangent, rest, all_masks, bounds)
+    )
     weights = [finish_gather(terms)]
-    small = weights[0][:, small_at * LANES : small_at * LANES + SMALL_GAINS].astype(f32)
-    gain_one, gain_two = small[:, 0][None], small[:, 1][None]
-
-    bounds = [tile_bounds(segment_ids[seq]) for seq in range(seq_count)]
-    packs, lses = [], []
+
+    packs, lses, normeds = [], [], None
     mixes = [None] * seq_count
     for g, (first, many) in enumerate(groups):
         if g == 0:
-            packed, normed = run_project(rows_in, gain_one, weights[0], 3 * many * width)
-        else:
-            packed = jnp.dot(normed, weights[g][:, : 3 * many * width], preferred_element_type=f32).astype(bf16)
-        packs.append([packed[seq * seq_length : (seq + 1) * seq_length] for seq in range(seq_count)])
+            terms = start_gather(rest)
+            weights[0], filled_cotangent = lax.optimization_barrier((weights[0], filled_cotangent))
+            d_final_rows = send_slots(filled_cotangent)
+        done = [
+            attend_forward(
+                rows_in[seq * seq_length : (seq + 1) * seq_length],
+                weights[0],
+                small_at,
+                weights[g],
+                *all_masks[seq],
+                bounds[seq],
+                tiles,
+                mixes[seq],
+                first,
+                many,
+                head_dim,
+            )
+            for seq in range(seq_count)
+        ]
+        packs.append([packed for packed, unused, unused, unused in done])
+        mixes = [mixed for unused, mixed, unused, unused in done]
+        lses.append([lse for unused, unused, lse, unused in done])
         if g == 0:
-            terms = start_gather(rest)
-            packs[0], filled_cotangent = lax.optimization_barrier((packs[0], filled_cotangent))
-            d_final_rows = send_slots(filled_cotangent)
-        lses.append([])
-        for seq in range(seq_count):
-            mixes[seq], lse = attend_forward(
-                packs[g][seq], *all_masks[seq], bounds[seq], tiles, mixes[seq], first, head_dim
-            )
-            lses[g].append(lse)
-        if g == 0:
-            terms, mixes, lses = lax.optimization_barrier((terms, mixes, lses))
+            normeds = [normed for unused, unused, unused, normed in done]
+            terms, mixes, lses, packs, normeds = lax.optimization_barrier((terms, mixes, lses, packs, normeds))
             weights.append(finish_gather(terms))
     mixed = join(mixes)
     mixed, d_final_rows = lax.optimization_barrier((mixed, d_final_rows))
-    mid_rows, filled = run_middle(mixed, weights[1], out_at, rows_in, gain_two, slot_row, slots)
+    mid_rows, filled = run_middle(mixed, weights[1], out_at, rows_in, weights[0], small_at, slot_row, slots)
     slot_rows = send_slots(filled)
 
     w_in, w_back = expert_in[0], expert_out[0]
     d_hidden = dot(after(d_final_rows, filled), w_back, NT).astype(bf16)
-    slot_rows, d_hidden = lax.optimization_barrier((slot_rows, d_hidden))
-    hidden, d_pre, d_rows, d_logits, gate = run_expert(me, slot_rows, w_in, weights[0], small_at, d_hidden, experts)
+    held_packs = lax.optimization_barrier((packs, filled))[0]
+    probs = [
+        [
+            attend_probs(
+                held_packs[g][seq], lses[g][seq], *all_masks[seq], bounds[seq], tiles, first, head_dim
+            )
+            for seq in range(seq_count)
+        ]
+        for g, (first, many) in enumerate(groups)
+    ]
+    slot_rows, d_hidden, probs = lax.optimization_barrier((slot_rows, d_hidden, probs))
+    d_rows, d_logits, gate = run_expert(me, slot_rows, w_in, weights[0], small_at, d_hidden, experts)
     d_returned = send_slots(d_rows)
 
-    part_in, part_out, moe_rows, grad_router = expert_grads(
-        gate, slot_rows, hidden, d_pre, d_final_rows, w_back, d_logits
-    )
-    d_returned, moe_rows, part_in, part_out, grad_router = lax.optimization_barrier(
-        (d_returned, moe_rows, part_in, part_out, grad_router)
-    )
-    grad_expert_in = lax.psum_scatter(part_in, "dp", scatter_dimension=1, tiled=True)
-    grad_expert_out = lax.psum_scatter(part_out, "dp", scatter_dimension=0, tiled=True)
-    d_mid, d_attn, d_mixed, grad_gain_two = run_middle_back(
-        d_returned, slot_column, mid_rows, gain_two, top, weights[1], out_at
+    expert_parts, moe_rows, grad_router = expert_grads(
+        gate, slot_rows, w_in, d_hidden, d_final_rows, w_back, d_logits, lax.axis_size("dp")
+    )
+    d_returned, moe_rows, expert_parts, grad_router = lax.optimization_barrier(
+        (d_returned, moe_rows, expert_parts, grad_router)
+    )
+    expert_sums = lax.psum_scatter(expert_parts, "dp", scatter_dimension=0, tiled=True)
+    d_mid, d_mixed, grad_gain_two = run_middle_back(
+        d_returned, slot_row, mid_rows, weights[0], small_at, top, weights[1], out_at
     )
     moe_returned = send_slots(moe_rows)
 
-    grad_out = run_out_grad(mixed, d_attn, grad_router, grad_gain_two)
-    diagonals, all_parts, near_terms = [], [], []
-    terms, waits = scatter_dp(grad_out), [moe_returned]
+    diagonals, all_parts = [], []
+    terms = None
     for g, (first, many) in enumerate(groups):
         parts, diagonal = [], None
         for seq in range(seq_count):
             at = slice(seq * seq_length, (seq + 1) * seq_length)
             part, here = attend_backward(
-                packs[g][seq], d_mixed[at], mixed[at], lses[g][seq], *all_masks[seq], bounds[seq], tiles, first, head_dim
+                packs[g][seq], d_mixed[at], mixed[at], probs[g][seq], bounds[seq], 2 * REACH + 1, first, head_dim
             )
             parts.append(part)
             diagonal = here if diagonal is None else diagonal + here
-        parts, diagonal, terms, waits = lax.optimization_barrier((parts, diagonal, terms, waits))
+        parts = join(parts)
         if g == 0:
-            moe_returned = waits[0]
+            grads = run_dense_grads(mixed, d_mid, grad_router, grad_gain_two, join(normeds), parts)
+            grads, parts, diagonal, moe_returned = lax.optimization_barrier((grads, parts, diagonal, moe_returned))
+            terms = scatter_dp(grads)
+            output, sums = run_output(moe_returned, slot_row, mid_rows, rows_in, live)
+            d_mixed, output, sums = lax.optimization_barrier((d_mixed, output, sums))
         else:
-            near_terms.append(waits[0])
+            parts, diagonal, terms = lax.optimization_barrier((parts, diagonal, terms))
+            half, parts = lax.optimization_barrier((finish_dp(terms), parts))
+            waits = [near_parts(half)]
+            terms = scatter_dp(dot(join(normeds), parts, TN))
         diagonals.append(diagonal)
-        all_parts.append(join(parts))
-        half = finish_dp(terms)
-        grad_group = None
-        for seq in range(seq_count):
-            here = dot(normed[seq * seq_length : (seq + 1) * seq_length], parts[seq], TN)
-            grad_group = here if grad_group is None else grad_group + here
-        waits = [near_parts(half)]
-        terms = scatter_dp(grad_group)
-        if g < len(groups) - 1:
-            output, sums = run_output(moe_returned, slot_column, mid_rows, rows_in, live)
-            d_mixed = after(d_mixed, half, output)
-    all_parts = lax.optimization_barrier((all_parts, terms[0]))[0]
-    input_grad = run_first_back(rows_in, gain_one, d_mid, all_parts, weights)
+        all_parts.append(parts)
+    held, all_parts = lax.optimization_barrier((terms[0], all_parts))
+    terms = (held, terms[1])
+    input_grad = run_first_back(rows_in, small_at, d_mid, all_parts, weights)
     input_grad, terms, waits = lax.optimization_barrier((input_grad, terms, waits))
-    near_terms.append(waits[0])
-    grad_expert_in, grad_expert_out = widen(grad_expert_in, grad_expert_out)
+    near_terms = list(waits)
+    grad_expert_in, grad_expert_out = widen(expert_sums)
     grad_rel = jnp.einsum("hgp,gpb->bh", jnp.concatenate(diagonals, axis=0), one_hot_windows, precision=HIGHEST)
 
     tail = jnp.concatenate([grad_rel.reshape(-1), sums[0, :4]])
@@ -1033,7 +1100,8 @@
     totals = tail[bucket_count * head_count : tail_size]
     stats = jnp.sqrt(totals[:3] / (totals[3] * model_width))
 
-    dense_out, *dense_qkv = [jnp.sum(block.astype(f32), axis=0) for block in near_terms]
+    dense_out, last_qkv = [jnp.sum(block.astype(f32), axis=0) for block in near_terms]
+    dense_qkv = [dense_out[:, model_width + LANES :], last_qkv]
     grad_parts = [total.reshape(-1, many, 3, width) for total, (first, many) in zip(dense_qkv, groups)]
     grad_qkv = jnp.concatenate(grad_parts, axis=1).transpose(0, 2, 1, 3).reshape(-1, 3 * model_width)
     grad_gain_one = jnp.sum(grad_qkv * qkv_weight.astype(f32), axis=1) / attn_gain.astype(f32)

time: 438 us -> 422 us (0.963)
  waiting for transfers between devices: 78.4 us -> 49.1 us
  Pallas kernels: 221 us -> 247 us
  matrix products: 22.8 us -> 13.1 us
    all_to_all x9 -> x8, waiting for transfers between devices: 66.6 us -> 31.2 us  [swap_blocks(): lax.all_to_all(blocks, 'expert', split_axis=0, concat_axis=0, tiled=True)]
    pallas_call x7 -> x8, Pallas kernels: 116 us -> 137 us  [the longest x2 49.9 us: attend_backward(): pl.pallas_call(functools.partial(backward_kernel, head_dim, groups // 2),...]
    pallas_call x2, Pallas kernels: 36.8 us -> 44.5 us  [attend_forward(): pl.pallas_call(functools.partial(forward_kernel, head_dim, reach), grid_s...]
    dot_general x3 -> x2, matrix products: 19.7 us -> 12.5 us  [dot(): return lax.dot_general(left, right, dims, preferred_element_type=f32)]
    ppermute x12 -> x10, waiting for transfers between devices: 11.3 us -> 17.9 us  [exchange(): lax.ppermute(rows, axis, [(i, i ^ distance) for i in range(lax.axis_size(...]
    all_to_all x9 -> x8, starting transfers between devices: 44.1 us -> 40.9 us  [swap_blocks(): lax.all_to_all(blocks, 'expert', split_axis=0, concat_axis=0, tiled=True)]
    ppermute x12 -> x10, starting transfers between devices: 6.76 us -> 9.96 us  [exchange(): lax.ppermute(rows, axis, [(i, i ^ distance) for i in range(lax.axis_size(...]
    unnamed x60 -> x59, local copies, waits for them, and re-layouts: 11.1 us -> 10.3 us
  transfers between devices with their start and end apart: 23 -> 19, of which waited for: 8 -> 10; matrix products, arithmetic and copies ran while one was open for 12% -> 10% of each run, Pallas kernels for 43% -> 51%
where the time goes in v4:
time: 422 us; the launch traced here: 415 us
  Pallas kernels  247 us (59%)
  starting transfers between devices  51.3 us (12%)
  waiting for transfers between devices  49.1 us (12%)
  local copies, waits for them, and re-layouts  23 us (5%)
  other arithmetic  16.8 us (4%)
  between operations  15.5 us (4%)
  matrix products  13.1 us (3%)
    pallas_call x2, Pallas kernels, attend_backward(): pl.pallas_call(functools.partial(backward_kernel, head_dim, groups // 2),...  49.9 us
    pallas_call x2, Pallas kernels, attend_forward(): pl.pallas_call(functools.partial(forward_kernel, head_dim, reach), grid_s...  44.5 us
    all_to_all x8, starting transfers between devices, swap_blocks(): lax.all_to_all(blocks, 'expert', split_axis=0, concat_axis=0, tiled=True)  40.9 us
    pallas_call x1, Pallas kernels, expert_grads(): pl.pallas_call(expert_grads_kernel, grid=(owners,), in_specs=[pl.BlockSpe...  37 us
    all_to_all x8, waiting for transfers between devices, swap_blocks(): lax.all_to_all(blocks, 'expert', split_axis=0, concat_axis=0, tiled=True)  31.2 us
    pallas_call x2, Pallas kernels, attend_probs(): pl.pallas_call(functools.partial(probs_kernel, head_dim, reach), grid_spe...  26 us
    pallas_call x1, Pallas kernels, run_expert(): pl.pallas_call(functools.partial(expert_kernel, experts), grid_spec=grid_...  23.4 us
    ppermute x10, waiting for transfers between devices, exchange(): lax.ppermute(rows, axis, [(i, i ^ distance) for i in range(lax.axis_size(...  17.9 us
  transfers between devices with their start and end apart: 19, of which 10 were waited for; matrix products, arithmetic and copies ran while one was open for 10% of the time, Pallas kernels for 51%

profile of v4, /device:TPU:0, one launch (start us, length us, event | category | flops | bytes accessed | tf_op | source)
XLA Modules:
  0.0 415.4 jit_solution(8459957493743829169)
XLA Ops:
  9.3 7.4 %all-to-all-start = ((bf16[8,24,1664]{2,1,0:T(8,128)(2,1)}), bf16[8,24,1664]{2,1,0:T(8,128)(2,1)S(1)}, u32[]{:S(2)}, u32[]{:S(2)}) async-start(bf16[8,24,1664]{2,1,0:T(8,128)(2,1)} %get-tuple-element.94), calls=%async_computation | async-start | bytes 1277952 | tf_op jit(solution)/shard_map/all_to_all | solution.py:858
  21.9 9.5 %toeplitz_tiles.1.bias_ref = f32[12,1408,128]{2,1,0:T(8,128)} custom-call(f32[12,11,256]{2,1,0:T(8,128)} %bitcast.133), custom_call_target="tpu_custom_call" | custom-call | flops 9900000256 | tf_op jit(solution)/shard_map/toeplitz_tiles/pallas_call | solution.py:50
  46.4 7.9 %collective-permute-done = bf16[1,8,24,1664]{3,2,1,0:T(8,128)(2,1)S(1)} collective-permute-done((bf16[1,8,24,1664]{3,2,1,0:T(8,128)(2,1)S(1)}, bf16[1,8,24,1664]{3,2,1,0:T(8,128)(2,1)S(1)}, u32[]{:S(2)}, u32[]{:S(2)}) %collective-permute-start) | collective-permute-done | bytes 639008 | tf_op jit(solution)/shard_map/ppermute | solution.py:850
  62.5 6.0 %all-to-all-start.2 = ((bf16[8,160,768]{2,1,0:T(8,128)(2,1)}), bf16[8,160,768]{2,1,0:T(8,128)(2,1)}, u32[]{:S(2)}, u32[]{:S(2)}) async-start(bf16[8,160,768]{2,1,0:T(8,128)(2,1)} %bitcast.36), calls=%async_computation.2 | async-start | bytes 3932160 | tf_op jit(solution)/shard_map/all_to_all | solution.py:858
  68.5 27.9 %attend_forward.2 = (bf16[1024,1536]{1,0:T(8,128)(2,1)}, bf16[1024,768]{1,0:T(8,128)(2,1)}, f32[2,4,1024]{2,1,0:T(4,128)}, bf16[1024,768]{1,0:T(8,128)(2,1)}) custom-call(s32[4]{0:T(128)} %get-tuple-element.98.low_ref, s32[4]{0:T(128)} %get-tuple-element.99.high_ref, bf16[1024,768]{1,0:T(8,128)(2,1)} %bitcast.112, bf16[768,1664]{1,0:T(8,128)(2,1)} %bitcast.101, ...), custom_call_target="tpu_custom_call" | custom-call | flops 1100000000 | tf_op jit(solution)/shard_map/attend_forward/pallas_call | solution.py:324
  102.7 16.5 %attend_forward.3 = (bf16[1024,768]{1,0:T(8,128)(2,1)}, bf16[1024,768]{1,0:T(8,128)(2,1)}, f32[1,4,1024]{2,1,0:T(4,128)}, bf16[1024,768]{1,0:T(8,128)(2,1)}) custom-call(s32[4]{0:T(128)} %get-tuple-element.98.low_ref, s32[4]{0:T(128)} %get-tuple-element.99.high_ref, bf16[1024,768]{1,0:T(8,128)(2,1)} %bitcast.113, ...), custom_call_target="tpu_custom_call", output_to_operand_aliasing={{1}: (8, {})} | custom-call | flops 1100000000 | tf_op jit(solution)/shard_map/attend_forward/pallas_call | solution.py:324
  119.2 7.8 %run_middle.1 = (f32[1024,768]{1,0:T(8,128)}, bf16[1280,768]{1,0:T(8,128)(2,1)}) custom-call(bf16[1024,768]{1,0:T(8,128)(2,1)} %get-tuple-element.117.mixed_ref.mix_ref, bf16[768,1536]{1,0:T(8,128)(2,1)} %bitcast.109, bf16[1024,768]{1,0:T(8,128)(2,1)} %bitcast.114, bf16[768,1664]{1,0:T(8,128)(2,1)} %bitcast.104, s32[1,1024]{1,0:T(1,128)} %compare_select_fusion.slot_ref), custom_call_target="tpu_custom_call" | custom-call | flops 5500000256 | tf_op jit(solution)/shard_map/run_middle/pallas_call | solution.py:653
  127.1 5.4 %all-to-all-start.3 = ((bf16[8,160,768]{2,1,0:T(8,128)(2,1)}), bf16[8,160,768]{2,1,0:T(8,128)(2,1)S(1)}, u32[]{:S(2)}, u32[]{:S(2)}) async-start(bf16[8,160,768]{2,1,0:T(8,128)(2,1)} %bitcast.128), calls=%async_computation.3 | async-start | bytes 3932160 | tf_op jit(solution)/shard_map/all_to_all | solution.py:858
  132.5 10.7 %attend_probs.3.probs_ref = bf16[4,4,1024,256]{3,2,1,0:T(8,128)(2,1)} custom-call(s32[4]{0:T(128)} %get-tuple-element.98.low_ref, s32[4]{0:T(128)} %get-tuple-element.99.high_ref, bf16[1024,768]{1,0:T(8,128)(2,1)} %get-tuple-element.125.q_ref.k_ref.v_ref, bf16[1024,768]{1,0:T(8,128)(2,1)} %get-tuple-element.125.q_ref.k_ref.v_ref, ...), custom_call_target="tpu_custom_call" | custom-call | flops 9900000256 | tf_op jit(solution)/shard_map/attend_probs/pallas_call | solution.py:360
  143.2 11.1 %convolution_convert_fusion.d_hidden_ref = bf16[1280,3072]{1,0:T(8,128)(2,1)} fusion(bf16[1280,768]{1,0:T(8,128)(2,1)} %bitcast.37.d_slots_ref, bf16[1,3072,768]{2,1,0:T(8,128)(2,1)} %param.25), kind=kOutput, calls=%fused_computation | convolution fusion | flops 6043729920 | bytes 14548992 | tf_op jit(solution)/shard_map/dot_general | solution.py:28
  154.3 15.3 %attend_probs.2.probs_ref = bf16[8,4,1024,256]{3,2,1,0:T(8,128)(2,1)} custom-call(s32[4]{0:T(128)} %get-tuple-element.98.low_ref, s32[4]{0:T(128)} %get-tuple-element.99.high_ref, bf16[1024,1536]{1,0:T(8,128)(2,1)} %get-tuple-element.123.q_ref.k_ref.v_ref, bf16[1024,1536]{1,0:T(8,128)(2,1)} %get-tuple-element.123.q_ref.k_ref.v_ref, ...), custom_call_target="tpu_custom_call" | custom-call | flops 19800000512 | tf_op jit(solution)/shard_map/attend_probs/pallas_call | solution.py:360
  169.6 8.9 %all-to-all-done.3 = bf16[8,160,768]{2,1,0:T(8,128)(2,1)S(1)} async-done(((bf16[8,160,768]{2,1,0:T(8,128)(2,1)}), bf16[8,160,768]{2,1,0:T(8,128)(2,1)S(1)}, u32[]{:S(2)}, u32[]{:S(2)}) %all-to-all-start.3) | async-done | bytes 1966112 | tf_op jit(solution)/shard_map/all_to_all | solution.py:858
  179.7 23.4 %run_expert.1 = (bf16[1280,768]{1,0:T(8,128)(2,1)}, bf16[1280,128]{1,0:T(8,128)(2,1)}, f32[1280,1]{1,0:T(8,128)}) custom-call(s32[1]{0:T(128)} %bitcast.me_ref, bf16[1280,768]{1,0:T(8,128)(2,1)} %bitcast.125, bf16[768,3072]{1,0:T(8,128)(2,1)} %bitcast.150, bf16[768,1664]{1,0:T(8,128)(2,1)} %bitcast.105, bf16[1280,3072]{1,0:T(8,128)(2,1)} %convolution_convert_fusion.d_hidden_ref), custom_call_target="tpu_custom_call" | custom-call | flops 19800000512 | tf_op jit(solution)/shard_map/run_expert/pallas_call | solution.py:512
  207.2 37.0 %expert_grads.1 = (bf16[4,2,768,768]{3,2,1,0:T(8,128)(2,1)}, bf16[1280,768]{1,0:T(8,128)(2,1)}, f32[768,128]{1,0:T(8,128)}) custom-call(f32[1280,1]{1,0:T(8,128)} %get-tuple-element.130.gate_ref, bf16[1280,768]{1,0:T(8,128)(2,1)} %bitcast.126, bf16[768,3072]{1,0:T(8,128)(2,1)} %bitcast.151, bf16[1280,3072]{1,0:T(8,128)(2,1)} %convolution_convert_fusion.d_hidden_ref, ...), custom_call_target="tpu_custom_call" | custom-call | flops 38499999744 | tf_op jit(solution)/shard_map/expert_grads/pallas_call | solution.py:560
  244.2 8.2 %all-to-all-done.4 = bf16[8,160,768]{2,1,0:T(8,128)(2,1)S(1)} async-done(((bf16[8,160,768]{2,1,0:T(8,128)(2,1)}), bf16[8,160,768]{2,1,0:T(8,128)(2,1)S(1)}, u32[]{:S(2)}, u32[]{:S(2)}) %all-to-all-start.4) | async-done | bytes 1966112 | tf_op jit(solution)/shard_map/all_to_all | solution.py:858
  258.2 10.8 %run_middle_back.1 = (bf16[1024,768]{1,0:T(8,128)(2,1)}, bf16[1024,768]{1,0:T(8,128)(2,1)}, f32[1,768]{1,0:T(1,128)}) custom-call(bf16[1280,768]{1,0:T(8,128)(2,1)} %bitcast.123, s32[1,1024]{1,0:T(1,128)} %compare_select_fusion.slot_ref, f32[1024,768]{1,0:T(8,128)} %get-tuple-element.136.rows_ref, bf16[768,1664]{1,0:T(8,128)(2,1)} %bitcast.106, ...), custom_call_target="tpu_custom_call" | custom-call | flops 7699999744 | tf_op jit(solution)/shard_map/run_middle_back/pallas_call | solution.py:696
  272.4 31.8 %attend_backward.2 = (bf16[1024,1536]{1,0:T(8,128)(2,1)S(1)}, f32[8,11,256]{2,1,0:T(8,128)S(1)}) custom-call(s32[4]{0:T(128)S(1)} %copy-done.5, s32[4]{0:T(128)S(1)} %copy-done.4, bf16[1024,1536]{1,0:T(8,128)(2,1)S(1)} %copy-done.6, bf16[1024,1536]{1,0:T(8,128)(2,1)S(1)} %copy-done.6, bf16[1024,1536]{1,0:T(8,128)(2,1)S(1)} %copy-done.6, ...), custom_call_target="tpu_custom_call" | custom-call | flops 32999999488 | tf_op jit(solution)/shard_map/attend_backward/pallas_call | solution.py:397
  305.9 9.4 %run_dense_grads.1 = f32[768,2432]{1,0:T(8,128)} custom-call(bf16[1024,768]{1,0:T(8,128)(2,1)} %get-tuple-element.117.mixed_ref.mix_ref, bf16[1024,768]{1,0:T(8,128)(2,1)} %get-tuple-element.138.d_attn_ref.d_mid_ref, f32[768,128]{1,0:T(8,128)} %get-tuple-element.139.router_ref, f32[1,768]{1,0:T(1,128)} %get-tuple-element.140.gain_ref, ...), custom_call_target="tpu_custom_call" | custom-call | flops 7699999744 | tf_op jit(solution)/shard_map/run_dense_grads/pallas_call | solution.py:798
  318.7 7.2 %run_output.1 = (bf16[1024,768]{1,0:T(8,128)(2,1)}, f32[1,128]{1,0:T(1,128)}) custom-call(bf16[1280,768]{1,0:T(8,128)(2,1)} %bitcast.45.blocks_ref, s32[1,1024]{1,0:T(1,128)} %compare_select_fusion.slot_ref, f32[1024,768]{1,0:T(8,128)} %get-tuple-element.136.rows_ref, bf16[1024,768]{1,0:T(8,128)(2,1)} %bitcast.115, s32[1,1024]{1,0:T(1,128)} %live_ref.1), custom_call_target="tpu_custom_call" | custom-call | flops 4400000000 | tf_op jit(solution)/shard_map/run_output/pallas_call | solution.py:772
  331.6 18.1 %attend_backward.3 = (bf16[1024,768]{1,0:T(8,128)(2,1)S(1)}, f32[4,11,256]{2,1,0:T(8,128)S(1)}) custom-call(s32[4]{0:T(128)S(1)} %copy-done.5, s32[4]{0:T(128)S(1)} %copy-done.4, bf16[1024,768]{1,0:T(8,128)(2,1)S(1)} %copy-done.7, bf16[1024,768]{1,0:T(8,128)(2,1)S(1)} %copy-done.7, bf16[1024,768]{1,0:T(8,128)(2,1)S(1)} %copy-done.7, ...), custom_call_target="tpu_custom_call" | custom-call | flops 16499999744 | tf_op jit(solution)/shard_map/attend_backward/pallas_call | solution.py:397
  358.2 6.5 %all-to-all-start.6 = ((bf16[8,24,2432]{2,1,0:T(8,128)(2,1)}), bf16[8,24,2432]{2,1,0:T(8,128)(2,1)S(1)}, u32[]{:S(2)}, u32[]{:S(2)}) async-start(bf16[8,24,2432]{2,1,0:T(8,128)(2,1)} %bitcast.54), calls=%async_computation.6 | async-start | bytes 1867776 | tf_op jit(solution)/shard_map/all_to_all | solution.py:858
  371.5 10.0 %run_first_back.1 = f32[1024,768]{1,0:T(8,128)} custom-call(bf16[1024,768]{1,0:T(8,128)(2,1)} %bitcast.116, bf16[1024,768]{1,0:T(8,128)(2,1)} %get-tuple-element.138.d_attn_ref.d_mid_ref, bf16[1024,1536]{1,0:T(8,128)(2,1)} %copy-done.9, bf16[1024,768]{1,0:T(8,128)(2,1)} %copy-done.8, bf16[768,1664]{1,0:T(8,128)(2,1)} %bitcast.107, bf16[768,1536]{1,0:T(8,128)(2,1)} %bitcast.111), custom_call_target="tpu_custom_call" | custom-call | flops 8800000000 | tf_op jit(solution)/shard_map/run_first_back/pallas_call | solution.py:735
  381.5 6.7 %all-to-all-done.6 = bf16[8,24,2432]{2,1,0:T(8,128)(2,1)S(1)} async-done(((bf16[8,24,2432]{2,1,0:T(8,128)(2,1)}), bf16[8,24,2432]{2,1,0:T(8,128)(2,1)S(1)}, u32[]{:S(2)}, u32[]{:S(2)}) %all-to-all-start.6) | async-done | bytes 933920 | tf_op jit(solution)/shard_map/all_to_all | solution.py:858
  399.5 5.1 %all-to-all-done.7 = bf16[8,27,768]{2,1,0:T(8,128)(2,1)S(1)} async-done(((bf16[8,27,768]{2,1,0:T(8,128)(2,1)}), bf16[8,27,768]{2,1,0:T(8,128)(2,1)S(1)}, u32[]{:S(2)}, u32[]{:S(2)}) %all-to-all-start.7) | async-done | bytes 331808 | tf_op jit(solution)/shard_map/all_to_all | solution.py:858
  (177 shorter events, 91.4 us)
Async XLA Ops:
  9.3 11.3 %copy-start.21 = (s32[1,1024]{1,0:T(1,128)S(1)}, s32[1,1024]{1,0:T(1,128)}, u32[]{:S(2)}) copy-start(s32[1,1024]{1,0:T(1,128)} %param.28) | copy-start | bytes 12292
  9.3 11.3 %copy-start.22 = (s32[1,1024]{1,0:T(1,128)S(1)}, s32[1,1024]{1,0:T(1,128)}, u32[]{:S(2)}) copy-start(s32[1,1024]{1,0:T(1,128)} %param.27) | copy-start | bytes 12292
  9.3 24.4 %all-to-all-start = ((bf16[8,24,1664]{2,1,0:T(8,128)(2,1)}), bf16[8,24,1664]{2,1,0:T(8,128)(2,1)S(1)}, u32[]{:S(2)}, u32[]{:S(2)}) async-start(bf16[8,24,1664]{2,1,0:T(8,128)(2,1)} %get-tuple-element.94), calls=%async_computation | async-start | bytes 1277952 | tf_op jit(solution)/shard_map/all_to_all | solution.py:858
  18.0 13.4 %copy-start.15 = (s32[11,256]{1,0:T(8,128)}, s32[11,256]{1,0:T(8,128)S(1)}, u32[]{:S(2)}) copy-start(s32[11,256]{1,0:T(8,128)S(1)} %stack.83) | copy-start | bytes 33796
  33.7 20.7 %all-to-all-start.1 = ((bf16[8,24,1536]{2,1,0:T(8,128)(2,1)}), bf16[8,24,1536]{2,1,0:T(8,128)(2,1)S(1)}, u32[]{:S(2)}, u32[]{:S(2)}) async-start(bf16[8,24,1536]{2,1,0:T(8,128)(2,1)} %get-tuple-element.97), calls=%async_computation.1 | async-start | bytes 1179648 | tf_op jit(solution)/shard_map/all_to_all | solution.py:858
  38.5 15.9 %collective-permute-start = (bf16[1,8,24,1664]{3,2,1,0:T(8,128)(2,1)S(1)}, bf16[1,8,24,1664]{3,2,1,0:T(8,128)(2,1)S(1)}, u32[]{:S(2)}, u32[]{:S(2)}) collective-permute-start(bf16[1,8,24,1664]{3,2,1,0:T(8,128)(2,1)S(1)} %bitcast.119), channel_id=1, source_target_pairs={{0,16},{8,24},{16,0},{24,8},{1,17},{9,25},{17,1},{25,9},{2,18},{10... | collective-permute-start | bytes 1916936 | tf_op jit(solution)/shard_map/ppermute | solution.py:850
  55.7 3.3 collective-permute-start.1
  55.7 40.8 %collective-permute-start.2 = (bf16[1,8,24,1536]{3,2,1,0:T(8,128)(2,1)S(1)}, bf16[1,8,24,1536]{3,2,1,0:T(8,128)(2,1)S(1)}, u32[]{:S(2)}, u32[]{:S(2)}) collective-permute-start(bf16[1,8,24,1536]{3,2,1,0:T(8,128)(2,1)S(1)} %bitcast.121), channel_id=1, source_target_pairs={{0,16},{8,24},{16,0},{24,8},{1,17},{9,25},{17,1},{25,9},{2,18},{10... | collective-permute-start | bytes 1769480 | tf_op jit(solution)/shard_map/ppermute | solution.py:850
  62.5 56.7 %all-to-all-start.2 = ((bf16[8,160,768]{2,1,0:T(8,128)(2,1)}), bf16[8,160,768]{2,1,0:T(8,128)(2,1)}, u32[]{:S(2)}, u32[]{:S(2)}) async-start(bf16[8,160,768]{2,1,0:T(8,128)(2,1)} %bitcast.36), calls=%async_computation.2 | async-start | bytes 3932160 | tf_op jit(solution)/shard_map/all_to_all | solution.py:858
  97.7 3.1 collective-permute-start.3
  127.1 51.4 %all-to-all-start.3 = ((bf16[8,160,768]{2,1,0:T(8,128)(2,1)}), bf16[8,160,768]{2,1,0:T(8,128)(2,1)S(1)}, u32[]{:S(2)}, u32[]{:S(2)}) async-start(bf16[8,160,768]{2,1,0:T(8,128)(2,1)} %bitcast.128), calls=%async_computation.3 | async-start | bytes 3932160 | tf_op jit(solution)/shard_map/all_to_all | solution.py:858
  203.1 49.3 %all-to-all-start.4 = ((bf16[8,160,768]{2,1,0:T(8,128)(2,1)}), bf16[8,160,768]{2,1,0:T(8,128)(2,1)S(1)}, u32[]{:S(2)}, u32[]{:S(2)}) async-start(bf16[8,160,768]{2,1,0:T(8,128)(2,1)} %bitcast.127), calls=%async_computation.4 | async-start | bytes 3932160 | tf_op jit(solution)/shard_map/all_to_all | solution.py:858
  206.7 188.4 %reduce-scatter.2.cloned.1.call-start = ((), (), s32[]{:S(2)}) async-start(), calls=%async_computation.9 | async-start | bytes 11796480 | tf_op jit(solution)/shard_map/reduce_scatter | solution.py:1041
  253.6 61.6 %all-to-all-start.5 = ((bf16[8,160,768]{2,1,0:T(8,128)(2,1)}), bf16[8,160,768]{2,1,0:T(8,128)(2,1)}, u32[]{:S(2)}, u32[]{:S(2)}) async-start(bf16[8,160,768]{2,1,0:T(8,128)(2,1)} %bitcast.124), calls=%async_computation.5 | async-start | bytes 3932160 | tf_op jit(solution)/shard_map/all_to_all | solution.py:858
  318.7 7.2 %collective-permute-start.4 = (bf16[2,192,2432]{2,1,0:T(8,128)(2,1)}, bf16[2,192,2432]{2,1,0:T(8,128)(2,1)S(1)}, u32[]{:S(2)}, u32[]{:S(2)}) collective-permute-start(bf16[2,192,2432]{2,1,0:T(8,128)(2,1)} %fusion), channel_id=1, source_target_pairs={{0,8},{8,0},{16,24},{24,16},{1,9},{9,1},{17,25},{25,17},{2,10},{10... | collective-permute-start | bytes 5603336 | tf_op jit(solution)/shard_map/ppermute | solution.py:850
  328.8 20.9 %copy-start.26 = (f32[1,128]{1,0:T(1,128)S(1)}, f32[1,128]{1,0:T(1,128)}, u32[]{:S(2)}) copy-start(f32[1,128]{1,0:T(1,128)} %get-tuple-element.170) | copy-start | bytes 1540
  328.8 24.2 %collective-permute-start.5 = (bf16[1,192,2432]{2,1,0:T(8,128)(2,1)S(1)}, bf16[1,192,2432]{2,1,0:T(8,128)(2,1)S(1)}, u32[]{:S(2)}, u32[]{:S(2)}) collective-permute-start(bf16[1,192,2432]{2,1,0:T(8,128)(2,1)S(1)} %dynamic-slice_convert_fusion.1), channel_id=1, source_target_pairs={{0,16},{8,24},{16,0},{24,8},{1,17},{9,25},{17,1},{25,9},{2,18},{10... | collective-permute-start | bytes 2801672 | tf_op jit(solution)/shard_map/ppermute | solution.py:850
  357.1 11.3 %collective-permute-start.6 = (bf16[2,192,768]{2,1,0:T(8,128)(2,1)}, bf16[2,192,768]{2,1,0:T(8,128)(2,1)}, u32[]{:S(2)}, u32[]{:S(2)}) collective-permute-start(bf16[2,192,768]{2,1,0:T(8,128)(2,1)} %fusion.2), channel_id=1, source_target_pairs={{0,8},{8,0},{16,24},{24,16},{1,9},{9,1},{17,25},{25,17},{2,10},{10... | collective-permute-start | bytes 1769480 | tf_op jit(solution)/shard_map/ppermute | solution.py:850
  357.6 7.1 %collective-permute-start.8 = (f32[1,768]{1,0:T(1,128)S(1)}, f32[1,768]{1,0:T(1,128)S(1)}, u32[]{:S(2)}, u32[]{:S(2)}) collective-permute-start(f32[1,768]{1,0:T(1,128)S(1)} %reshape.254), channel_id=1, source_target_pairs={{0,8},{8,0},{16,24},{24,16},{1,9},{9,1},{17,25},{25,17},{2,10},{10... | collective-permute-start | bytes 9224 | tf_op jit(solution)/shard_map/ppermute | solution.py:850
  358.2 30.0 %all-to-all-start.6 = ((bf16[8,24,2432]{2,1,0:T(8,128)(2,1)}), bf16[8,24,2432]{2,1,0:T(8,128)(2,1)S(1)}, u32[]{:S(2)}, u32[]{:S(2)}) async-start(bf16[8,24,2432]{2,1,0:T(8,128)(2,1)} %bitcast.54), calls=%async_computation.6 | async-start | bytes 1867776 | tf_op jit(solution)/shard_map/all_to_all | solution.py:858
  364.7 3.7 collective-permute-start.9
  369.7 11.8 %collective-permute-start.7 = (bf16[1,192,768]{2,1,0:T(8,128)(2,1)S(1)}, bf16[1,192,768]{2,1,0:T(8,128)(2,1)S(1)}, u32[]{:S(2)}, u32[]{:S(2)}) collective-permute-start(bf16[1,192,768]{2,1,0:T(8,128)(2,1)S(1)} %dynamic-slice_convert_fusion.3), channel_id=1, source_target_pairs={{0,16},{8,24},{16,0},{24,8},{1,17},{9,25},{17,1},{25,9},{2,18},{10... | collective-permute-start | bytes 884744 | tf_op jit(solution)/shard_map/ppermute | solution.py:850
  389.1 15.5 %all-to-all-start.7 = ((bf16[8,27,768]{2,1,0:T(8,128)(2,1)}), bf16[8,27,768]{2,1,0:T(8,128)(2,1)S(1)}, u32[]{:S(2)}, u32[]{:S(2)}) async-start(bf16[8,27,768]{2,1,0:T(8,128)(2,1)} %pad_maximum_fusion.2), calls=%async_computation.7 | async-start | bytes 786432 | tf_op jit(solution)/shard_map/all_to_all | solution.py:858
  395.1 13.2 %copy-start.1 = (f32[32,12]{0,1:T(8,128)S(1)}, f32[32,12]{0,1:T(8,128)}, u32[]{:S(2)}) copy-start(f32[32,12]{0,1:T(8,128)} %param.23) | copy-start | bytes 4612
  (22 other events, 129.8 us)
Sparse Core Ops, SparseCore 0:
  252.5 78.0 reduce-scatter.1
